TPU v7x, 32 devices: a whole 2x2x4 slice. The times are simulated.
32 devices in a mesh: groups: 2 (over y), boxes: 4 (over z), sub: 2 (over x), pair: 2 (over core).
Axes of the slice: x: 2, y: 2, z: 4, core: 2. Of those that a mesh axis runs over, the one named last changes fastest.
Arguments:
- phase: float32 [256, 128, 256], P(('groups', 'boxes'), 'sub', 'pair'), parts along dimension 0, may hold values from 0 to 1
- target_mask: int32 [256, 128, 256], P(('groups', 'boxes'), 'sub', 'pair'), parts along dimension 0, may hold values 0 or 1
- deviation: float32 [256, 128, 256], P(('groups', 'boxes'), 'sub', 'pair'), parts along dimension 0, may hold values from -12 to 12
Outputs:
- adjoint_field: float32 [256, 128, 256], P(('groups', 'boxes'), 'sub', 'pair'), parts along dimension 0
- residual: float32 [256, 128, 256], P(('groups', 'boxes'), 'sub', 'pair'), parts along dimension 0
There are 2 independent parts, one for each index of `groups`. A program takes and returns all parts, laid end to end along the dimension named above; each array names one. Nothing has to cross between parts.
All inputs are finite; a program needn't handle non-finite values. No bound on the sum of `target_mask` on one device may be relied on, other than what follows from the above.
Results may differ from a plain program's by a relative error of at most 0.00011.
Values sent between devices are 32-bit elements; how exact they have to be, the bound alone decides.
No kernel may reach another device: no remote copies, remote signals or barrier semaphores. Data moves between devices by JAX's collectives and lax.ppermute only.
A program may use at most 320 MiB of HBM per device.

v0:
```python
import jax
import jax.numpy as jnp
from jax import lax
from jax.sharding import PartitionSpec as P

SWEEPS = 2
BOTTOM_SWEEPS = 8


floor_conduct = 0.1
relax_weight = 0.8


def extended(block, sides, width):
    for axis, dim in sides:
        count = lax.axis_size(axis)
        forward = [(i, i + 1) for i in range(count - 1)]
        backward = [(target, source) for source, target in forward]
        low = lax.ppermute(
            lax.slice_in_dim(block, block.shape[dim] - width, None, axis=dim), axis, forward
        )
        high = lax.ppermute(lax.slice_in_dim(block, 0, width, axis=dim), axis, backward)
        block = jnp.concatenate([low, block, high], axis=dim)
    return block


def conduct(phase):
    return floor_conduct + (1.0 - floor_conduct) * (phase * phase * phase)


def coarsen(field):
    size_a, size_b, size_c = field.shape
    blocks = field.reshape(size_a // 2, 2, size_b // 2, 2, size_c // 2, 2)
    return jnp.mean(blocks, axis=(1, 3, 5))


def refine(field):
    return jnp.repeat(jnp.repeat(jnp.repeat(field, 2, axis=0), 2, axis=1), 2, axis=2)


def neighbours(padded):
    return [
        padded[2:, 1:-1, 1:-1],
        padded[:-2, 1:-1, 1:-1],
        padded[1:-1, 2:, 1:-1],
        padded[1:-1, :-2, 1:-1],
        padded[1:-1, 1:-1, 2:],
        padded[1:-1, 1:-1, :-2],
    ]


def face_terms(loop):
    center = loop[1:-1, 1:-1, 1:-1]
    return [0.5 * (center + other) for other in neighbours(loop)]


def diagonal_of(faces, scale):
    total = faces[0]
    for other in faces[1:]:
        total = total + other
    return total * scale


def operate(padded, faces, scale):
    center = padded[1:-1, 1:-1, 1:-1]
    others = neighbours(padded)
    total = faces[0] * (center - others[0])
    for index in range(1, 6):
        total = total + faces[index] * (center - others[index])
    return total * scale


def fine_pad(field):
    return extended(field, (("boxes", 0), ("sub", 1), ("pair", 2)), 1)


def coarse_pad(field):
    return extended(field, (("boxes", 0), ("sub", 1), ("pair", 2)), 1)


def relax_sweep(field, padded, source, faces, diagonal, scale):
    return field + relax_weight * (source - operate(padded, faces, scale)) / diagonal


def per_device(phase, target_mask, deviation):
    cond0 = conduct(phase)
    padded_fine = extended(cond0, (("boxes", 0), ("sub", 1), ("pair", 2)), 4)
    padded_middle = coarsen(padded_fine)
    padded_lowest = coarsen(padded_middle)
    faces0 = face_terms(padded_fine[3:-3, 3:-3, 3:-3])
    faces1 = face_terms(padded_middle[1:-1, 1:-1, 1:-1])
    faces2 = face_terms(padded_lowest)
    diag0 = diagonal_of(faces0, 1.0)
    diag1 = diagonal_of(faces1, 0.25)
    diag2 = diagonal_of(faces2, 0.0625)
    source = target_mask.astype(jnp.float32) * deviation
    field0 = relax_weight * source / diag0
    field0 = relax_sweep(field0, fine_pad(field0), source, faces0, diag0, 1.0)
    rest0 = source - operate(fine_pad(field0), faces0, 1.0)
    source1 = coarsen(rest0)
    field1 = relax_weight * source1 / diag1
    field1 = relax_sweep(field1, coarse_pad(field1), source1, faces1, diag1, 0.25)
    rest1 = source1 - operate(coarse_pad(field1), faces1, 0.25)
    source2 = coarsen(rest1)
    field2 = relax_weight * source2 / diag2
    for repeat in range(BOTTOM_SWEEPS - 1):
        field2 = relax_sweep(field2, coarse_pad(field2), source2, faces2, diag2, 0.0625)
    field1 = field1 + refine(field2)
    for repeat in range(SWEEPS):
        field1 = relax_sweep(field1, coarse_pad(field1), source1, faces1, diag1, 0.25)
    field0 = field0 + refine(field1)
    for repeat in range(SWEEPS):
        field0 = relax_sweep(field0, fine_pad(field0), source, faces0, diag0, 1.0)
    residual = source - operate(fine_pad(field0), faces0, 1.0)
    return (field0, residual)


def solution(mesh):
    return jax.shard_map(
        per_device,
        mesh=mesh,
        in_specs=(
            P(("groups", "boxes"), "sub", "pair"),
            P(("groups", "boxes"), "sub", "pair"),
            P(("groups", "boxes"), "sub", "pair"),
        ),
        out_specs=(P(("groups", "boxes"), "sub", "pair"), P(("groups", "boxes"), "sub", "pair")),
        check_vma=False,
    )
```

profile of v0, /device:TPU:0, one launch (start us, length us, event | category | flops | bytes accessed | tf_op | source)
XLA Modules:
  0.0 806.7 jit_solution(7072477304071291901)
XLA Ops:
  6.7 4.9 collective-permute-start.1
  12.9 4.2 collective-permute-done.1
  53.9 17.5 %fusion.93 = (f32[32,64,128]{1,0,2:T(8,128)S(1)}, f32[32,64,128]{1,0,2:T(8,128)}, f32[32,64,128]{1,0,2:T(8,128)}, f32[32,64,128]{1,0,2:T(8,128)}, f32[32,64,128]{1,0,2:T(8,128)}, /*index=5*/f32[32,64,128]{1,0,2:T(8,128)}) fusion(f32[32,64,128]{1,0,2:T(8,128)S(1)} %fusion.1, f32[4,64,128]{1,0,2:T(4,128)S(1)} %collective-permute-done, ...), kind=kLoop, calls=%fused_computation.136 | loop fusion | flops 10223616 | bytes 9955328 | tf_op jit(solution)/shard_map/div | solution.py:97
  87.4 4.2 collective-permute-done.8
  113.7 11.8 %fusion.70 = f32[32,64,128]{1,0,2:T(8,128)S(1)} fusion(f32[32,64,128]{1,0,2:T(8,128)} %copy-done.3, f32[32,64,128]{1,0,2:T(8,128)} %get-tuple-element.25, f32[32,64,128]{1,0,2:T(8,128)} %get-tuple-element.29, f32[34,66,128]{1,0,2:T(8,128)} %copy.148, f32[34,66,1]{1,0,2:T(8,128)S(1)} %collective-permute-done.11, f32[32,64,128]{1,0,2:T(8,128)} %get-tuple-element.28, ...), kind=kLoop, calls=%fused_computation.90 | loop fusion | flops 9437184 | bytes 11980320 | tf_op jit(solution)/shard_map/add | solution.py:82
  135.1 4.8 copy.161
  139.9 51.3 %reshape.36 = f32[20,2,36,2,68,2]{5,4,3,2,1,0:T(8,128)} reshape(f32[40,72,136]{2,1,0:T(8,128)} %copy.161) | data formatting | bytes 3133440 | tf_op jit(solution)/shard_map/reshape | solution.py:33
  191.2 32.5 %reduce_sum.37 = f32[20,36,68]{2,1,0:T(8,128)S(1)} reduce(f32[20,2,36,2,68,2]{5,4,3,2,1,0:T(8,128)} %reshape.36, f32[]{:T(128)} %constant.12.clone.1), dimensions={1,3,5}, to_apply=%region_1.0 | reduce | flops 342720 | bytes 1762564 | tf_op jit(solution)/shard_map/reduce_sum | solution.py:34
  231.6 4.2 collective-permute-done.14
  257.0 12.9 %fusion.53 = f32[32,64,128]{1,0,2:T(8,128)} fusion(f32[32,64,128]{1,0,2:T(8,128)} %get-tuple-element.25, f32[32,64,128]{1,0,2:T(8,128)} %get-tuple-element.29, f32[32,64,128]{1,0,2:T(8,128)} %copy-done.2, f32[34,66,128]{1,0,2:T(8,128)} %copy.157, f32[34,66,1]{1,0,2:T(8,128)S(1)} %collective-permute-done.17, f32[32,64,128]{1,0,2:T(8,128)} %get-tuple-element.28, ...), kind=kLoop, calls=%fused_computation.69 | loop fusion | flops 7340032 | bytes 11980320 | tf_op jit(solution)/shard_map/sub | solution.py:99
  273.6 69.2 %reshape.35 = f32[16,2,32,2,64,2]{5,4,3,2,1,0:T(8,128)} reshape(f32[32,64,128]{2,1,0:T(8,128)} %copy.160) | data formatting | bytes 2097152 | tf_op jit(solution)/shard_map/reshape | solution.py:33
  342.8 20.8 %reduce_sum.36 = f32[16,32,64]{2,1,0:T(8,128)S(1)} reduce(f32[16,2,32,2,64,2]{5,4,3,2,1,0:T(8,128)} %reshape.35, f32[]{:T(128)} %constant.12.clone.1), dimensions={1,3,5}, to_apply=%region_0.0 | reduce | flops 229376 | bytes 1179652 | tf_op jit(solution)/shard_map/reduce_sum | solution.py:34
  364.2 4.5 collective-permute-start.19
  370.2 4.2 collective-permute-done.18
  401.4 7.0 div.82
  408.4 6.4 reduce_sum.39
  423.6 10.8 %reshape.37 = f32[8,2,16,2,32,2]{5,4,3,2,1,0:T(8,128)} reshape(f32[16,32,64]{2,1,0:T(8,128)} %fusion.142) | data formatting | bytes 262144 | tf_op jit(solution)/shard_map/reshape | solution.py:33
  447.6 5.1 collective-permute-start.33
  596.3 4.2 collective-permute-done.72
  656.1 4.2 collective-permute-done.86
  682.3 12.2 %fusion.39 = f32[32,64,128]{1,0,2:T(8,128)S(1)} fusion(f32[32,64,128]{1,0,2:T(8,128)} %copy-done.4, f32[32,64,128]{1,0,2:T(8,128)} %get-tuple-element.25, f32[32,64,128]{1,0,2:T(8,128)} %get-tuple-element.29, f32[34,66,128]{1,0,2:T(8,128)} %copy.173, f32[34,66,1]{1,0,2:T(8,128)S(1)} %collective-permute-done.89, f32[32,64,128]{1,0,2:T(8,128)} %get-tuple-element.28, ...), kind=kLoop, calls=%fused_computation.51 | loop fusion | flops 9437184 | bytes 11980320 | tf_op jit(solution)/shard_map/add | solution.py:82
  735.9 12.2 %fusion.22 = f32[32,64,128]{1,0,2:T(8,128)S(1)} fusion(f32[32,64,128]{1,0,2:T(8,128)} %copy-done.6, f32[32,64,128]{1,0,2:T(8,128)} %get-tuple-element.25, f32[32,64,128]{1,0,2:T(8,128)} %get-tuple-element.29, f32[34,66,128]{1,0,2:T(8,128)} %copy.182, f32[34,66,1]{1,0,2:T(8,128)S(1)} %collective-permute-done.95, f32[32,64,128]{1,0,2:T(8,128)} %get-tuple-element.28, ...), kind=kLoop, calls=%fused_computation.30 | loop fusion | flops 9437184 | bytes 11980320 | tf_op jit(solution)/shard_map/add | solution.py:82
  763.3 4.2 collective-permute-done.98
  789.7 13.1 %fusion.5 = f32[32,64,128]{1,0,2:T(8,128)} fusion(f32[32,64,128]{1,0,2:T(8,128)} %get-tuple-element.25, f32[32,64,128]{1,0,2:T(8,128)} %get-tuple-element.29, f32[32,64,128]{1,0,2:T(8,128)} %copy-done.5, f32[34,66,128]{1,0,2:T(8,128)} %copy.191, f32[34,66,1]{1,0,2:T(8,128)S(1)} %collective-permute-done.101, f32[32,64,128]{1,0,2:T(8,128)} %get-tuple-element.28, ...), kind=kLoop, calls=%fused_computation.9 | loop fusion | flops 7340032 | bytes 11980320 | tf_op jit(solution)/shard_map/sub | solution.py:114
  (402 shorter events, 477.7 us)
Async XLA Ops:
  6.7 10.5 %collective-permute-start.1 = (f32[4,64,128]{1,0,2:T(4,128)S(1)}, f32[4,64,128]{1,0,2:T(4,128)S(1)}, u32[]{:S(2)}, u32[]{:S(2)}) collective-permute-start(f32[4,64,128]{1,0,2:T(4,128)S(1)} %get-tuple-element.54), channel_id=1, source_target_pairs={{0,4},{4,8},{8,12},{1,5},{5,9},{9,13},{2,6},{6,10},{10,14},{3,7},{... | collective-permute-start | bytes 393224 | tf_op jit(solution)/shard_map/ppermute | solution.py:19
  11.6 9.7 %collective-permute-start = (f32[4,64,128]{1,0,2:T(4,128)S(1)}, f32[4,64,128]{1,0,2:T(4,128)S(1)}, u32[]{:S(2)}, u32[]{:S(2)}) collective-permute-start(f32[4,64,128]{1,0,2:T(4,128)S(1)} %get-tuple-element.55), channel_id=1, source_target_pairs={{4,0},{8,4},{12,8},{5,1},{9,5},{13,9},{6,2},{10,6},{14,10},{7,3},{... | collective-permute-start | bytes 393224 | tf_op jit(solution)/shard_map/ppermute | solution.py:22
  27.4 7.2 collective-permute-start.3
  43.2 10.7 %collective-permute-start.5 = (f32[40,72,4]{1,0,2:T(8,128)S(1)}, f32[40,72,4]{1,0,2:T(8,128)S(1)}, u32[]{:S(2)}, u32[]{:S(2)}) collective-permute-start(f32[40,72,4]{1,0,2:T(8,128)S(1)} %get-tuple-element.30), channel_id=1, source_target_pairs={{0,1},{2,3},{4,5},{6,7},{8,9},{10,11},{12,13},{14,15},{16,17},{18,... | collective-permute-start | bytes 138248 | tf_op jit(solution)/shard_map/ppermute | solution.py:19
  44.5 9.4 %collective-permute-start.4 = (f32[40,72,4]{1,0,2:T(8,128)S(1)}, f32[40,72,4]{1,0,2:T(8,128)S(1)}, u32[]{:S(2)}, u32[]{:S(2)}) collective-permute-start(f32[40,72,4]{1,0,2:T(8,128)S(1)} %get-tuple-element.31), channel_id=1, source_target_pairs={{1,0},{3,2},{5,4},{7,6},{9,8},{11,10},{13,12},{15,14},{17,16},{19,... | collective-permute-start | bytes 138248 | tf_op jit(solution)/shard_map/ppermute | solution.py:22
  72.9 8.9 %collective-permute-start.7 = (f32[1,64,128]{1,0,2:T(1,128)S(1)}, f32[1,64,128]{1,0,2:T(1,128)S(1)}, u32[]{:S(2)}, u32[]{:S(2)}) collective-permute-start(f32[1,64,128]{1,0,2:T(1,128)S(1)} %get-tuple-element.52), channel_id=1, source_target_pairs={{0,4},{4,8},{8,12},{1,5},{5,9},{9,13},{2,6},{6,10},{10,14},{3,7},{... | collective-permute-start | bytes 98312 | tf_op jit(solution)/shard_map/ppermute | solution.py:19
  76.3 6.7 collective-permute-start.6
  98.0 15.7 %collective-permute-start.10 = (f32[34,66,1]{1,0,2:T(8,128)S(1)}, f32[34,66,1]{1,0,2:T(8,128)S(1)}, u32[]{:S(2)}, u32[]{:S(2)}) collective-permute-start(f32[34,66,1]{1,0,2:T(8,128)S(1)} %get-tuple-element.40), channel_id=1, source_target_pairs={{1,0},{3,2},{5,4},{7,6},{9,8},{11,10},{13,12},{15,14},{17,16},{19,... | collective-permute-start | bytes 26936 | tf_op jit(solution)/shard_map/ppermute | solution.py:22
  99.3 14.4 %collective-permute-start.11 = (f32[34,66,1]{1,0,2:T(8,128)S(1)}, f32[34,66,1]{1,0,2:T(8,128)S(1)}, u32[]{:S(2)}, u32[]{:S(2)}) collective-permute-start(f32[34,66,1]{1,0,2:T(8,128)S(1)} %get-tuple-element.41), channel_id=1, source_target_pairs={{0,1},{2,3},{4,5},{6,7},{8,9},{10,11},{12,13},{14,15},{16,17},{18,... | collective-permute-start | bytes 26936 | tf_op jit(solution)/shard_map/ppermute | solution.py:19
  126.9 100.4 %collective-permute-start.13 = (f32[1,64,128]{1,0,2:T(1,128)S(1)}, f32[1,64,128]{1,0,2:T(1,128)S(1)}, u32[]{:S(2)}, u32[]{:S(2)}) collective-permute-start(f32[1,64,128]{1,0,2:T(1,128)S(1)} %get-tuple-element.50), channel_id=1, source_target_pairs={{0,4},{4,8},{8,12},{1,5},{5,9},{9,13},{2,6},{6,10},{10,14},{3,7},{... | collective-permute-start | bytes 98312 | tf_op jit(solution)/shard_map/ppermute | solution.py:19
  130.4 96.9 %collective-permute-start.12 = (f32[1,64,128]{1,0,2:T(1,128)S(1)}, f32[1,64,128]{1,0,2:T(1,128)S(1)}, u32[]{:S(2)}, u32[]{:S(2)}) collective-permute-start(f32[1,64,128]{1,0,2:T(1,128)S(1)} %get-tuple-element.51), channel_id=1, source_target_pairs={{4,0},{8,4},{12,8},{5,1},{9,5},{13,9},{6,2},{10,6},{14,10},{7,3},{... | collective-permute-start | bytes 98312 | tf_op jit(solution)/shard_map/ppermute | solution.py:22
  241.0 16.0 %collective-permute-start.16 = (f32[34,66,1]{1,0,2:T(8,128)S(1)}, f32[34,66,1]{1,0,2:T(8,128)S(1)}, u32[]{:S(2)}, u32[]{:S(2)}) collective-permute-start(f32[34,66,1]{1,0,2:T(8,128)S(1)} %get-tuple-element.38), channel_id=1, source_target_pairs={{1,0},{3,2},{5,4},{7,6},{9,8},{11,10},{13,12},{15,14},{17,16},{19,... | collective-permute-start | bytes 26936 | tf_op jit(solution)/shard_map/ppermute | solution.py:22
  242.3 14.7 %collective-permute-start.17 = (f32[34,66,1]{1,0,2:T(8,128)S(1)}, f32[34,66,1]{1,0,2:T(8,128)S(1)}, u32[]{:S(2)}, u32[]{:S(2)}) collective-permute-start(f32[34,66,1]{1,0,2:T(8,128)S(1)} %get-tuple-element.39), channel_id=1, source_target_pairs={{0,1},{2,3},{4,5},{6,7},{8,9},{10,11},{12,13},{14,15},{16,17},{18,... | collective-permute-start | bytes 26936 | tf_op jit(solution)/shard_map/ppermute | solution.py:19
  397.6 17.2 %collective-permute-start.27 = (f32[18,1,64]{2,1,0:T(1,128)}, f32[18,1,64]{2,1,0:T(1,128)}, u32[]{:S(2)}, u32[]{:S(2)}) collective-permute-start(f32[18,1,64]{2,1,0:T(1,128)} %get-tuple-element.88), channel_id=1, source_target_pairs={{0,2},{1,3},{4,6},{5,7},{8,10},{9,11},{12,14},{13,15},{16,18},{17,... | collective-permute-start | bytes 13832 | tf_op jit(solution)/shard_map/ppermute | solution.py:19
  399.9 15.0 %collective-permute-start.26 = (f32[18,1,64]{2,1,0:T(1,128)}, f32[18,1,64]{2,1,0:T(1,128)}, u32[]{:S(2)}, u32[]{:S(2)}) collective-permute-start(f32[18,1,64]{2,1,0:T(1,128)} %get-tuple-element.89), channel_id=1, source_target_pairs={{2,0},{3,1},{6,4},{7,5},{10,8},{11,9},{14,12},{15,13},{18,16},{19,... | collective-permute-start | bytes 13832 | tf_op jit(solution)/shard_map/ppermute | solution.py:22
  643.8 6.9 collective-permute-start.85
  666.6 15.7 %collective-permute-start.88 = (f32[34,66,1]{1,0,2:T(8,128)S(1)}, f32[34,66,1]{1,0,2:T(8,128)S(1)}, u32[]{:S(2)}, u32[]{:S(2)}) collective-permute-start(f32[34,66,1]{1,0,2:T(8,128)S(1)} %get-tuple-element.36), channel_id=1, source_target_pairs={{1,0},{3,2},{5,4},{7,6},{9,8},{11,10},{13,12},{15,14},{17,16},{19,... | collective-permute-start | bytes 26936 | tf_op jit(solution)/shard_map/ppermute | solution.py:22
  667.9 14.4 %collective-permute-start.89 = (f32[34,66,1]{1,0,2:T(8,128)S(1)}, f32[34,66,1]{1,0,2:T(8,128)S(1)}, u32[]{:S(2)}, u32[]{:S(2)}) collective-permute-start(f32[34,66,1]{1,0,2:T(8,128)S(1)} %get-tuple-element.37), channel_id=1, source_target_pairs={{0,1},{2,3},{4,5},{6,7},{8,9},{10,11},{12,13},{14,15},{16,17},{18,... | collective-permute-start | bytes 26936 | tf_op jit(solution)/shard_map/ppermute | solution.py:19
  695.9 8.4 %collective-permute-start.91 = (f32[1,64,128]{1,0,2:T(1,128)S(1)}, f32[1,64,128]{1,0,2:T(1,128)S(1)}, u32[]{:S(2)}, u32[]{:S(2)}) collective-permute-start(f32[1,64,128]{1,0,2:T(1,128)S(1)} %get-tuple-element.46), channel_id=1, source_target_pairs={{0,4},{4,8},{8,12},{1,5},{5,9},{9,13},{2,6},{6,10},{10,14},{3,7},{... | collective-permute-start | bytes 98312 | tf_op jit(solution)/shard_map/ppermute | solution.py:19
  720.2 15.7 %collective-permute-start.94 = (f32[34,66,1]{1,0,2:T(8,128)S(1)}, f32[34,66,1]{1,0,2:T(8,128)S(1)}, u32[]{:S(2)}, u32[]{:S(2)}) collective-permute-start(f32[34,66,1]{1,0,2:T(8,128)S(1)} %get-tuple-element.34), channel_id=1, source_target_pairs={{1,0},{3,2},{5,4},{7,6},{9,8},{11,10},{13,12},{15,14},{17,16},{19,... | collective-permute-start | bytes 26936 | tf_op jit(solution)/shard_map/ppermute | solution.py:22
  721.5 14.4 %collective-permute-start.95 = (f32[34,66,1]{1,0,2:T(8,128)S(1)}, f32[34,66,1]{1,0,2:T(8,128)S(1)}, u32[]{:S(2)}, u32[]{:S(2)}) collective-permute-start(f32[34,66,1]{1,0,2:T(8,128)S(1)} %get-tuple-element.35), channel_id=1, source_target_pairs={{0,1},{2,3},{4,5},{6,7},{8,9},{10,11},{12,13},{14,15},{16,17},{18,... | collective-permute-start | bytes 26936 | tf_op jit(solution)/shard_map/ppermute | solution.py:19
  749.6 8.4 %collective-permute-start.97 = (f32[1,64,128]{1,0,2:T(1,128)S(1)}, f32[1,64,128]{1,0,2:T(1,128)S(1)}, u32[]{:S(2)}, u32[]{:S(2)}) collective-permute-start(f32[1,64,128]{1,0,2:T(1,128)S(1)} %get-tuple-element.44), channel_id=1, source_target_pairs={{0,4},{4,8},{8,12},{1,5},{5,9},{9,13},{2,6},{6,10},{10,14},{3,7},{... | collective-permute-start | bytes 98312 | tf_op jit(solution)/shard_map/ppermute | solution.py:19
  773.8 15.9 %collective-permute-start.100 = (f32[34,66,1]{1,0,2:T(8,128)S(1)}, f32[34,66,1]{1,0,2:T(8,128)S(1)}, u32[]{:S(2)}, u32[]{:S(2)}) collective-permute-start(f32[34,66,1]{1,0,2:T(8,128)S(1)} %get-tuple-element.32), channel_id=1, source_target_pairs={{1,0},{3,2},{5,4},{7,6},{9,8},{11,10},{13,12},{15,14},{17,16},{19,... | collective-permute-start | bytes 26936 | tf_op jit(solution)/shard_map/ppermute | solution.py:22
  775.1 14.6 %collective-permute-start.101 = (f32[34,66,1]{1,0,2:T(8,128)S(1)}, f32[34,66,1]{1,0,2:T(8,128)S(1)}, u32[]{:S(2)}, u32[]{:S(2)}) collective-permute-start(f32[34,66,1]{1,0,2:T(8,128)S(1)} %get-tuple-element.33), channel_id=1, source_target_pairs={{0,1},{2,3},{4,5},{6,7},{8,9},{10,11},{12,13},{14,15},{16,17},{18,... | collective-permute-start | bytes 26936 | tf_op jit(solution)/shard_map/ppermute | solution.py:19
  (111 other events, 730.3 us)
where the time goes:
time: 821 us; the launch traced here: 807 us
  local copies, waits for them, and re-layouts  275 us (33%)
  starting transfers between devices  197 us (24%)
  other arithmetic  195 us (24%)
  waiting for transfers between devices  137 us (17%)
    reshape x3, local copies, waits for them, and re-layouts, coarsen(): blocks = field.reshape(size_a // 2, 2, size_b // 2, 2, size_c // 2, 2)  131 us
    ppermute x51, starting transfers between devices, extended(): lax.ppermute(lax.slice_in_dim(block, block.shape[dim] - width, None, axis...  131 us
    ppermute x51, waiting for transfers between devices, extended(): lax.ppermute(lax.slice_in_dim(block, 0, width, axis=dim), axis, backward)  121 us
    unnamed x81, local copies, waits for them, and re-layouts  67 us
    ppermute x51, starting transfers between devices, extended(): lax.ppermute(lax.slice_in_dim(block, 0, width, axis=dim), axis, backward)  66.7 us
    reduce_sum x4, other arithmetic, coarsen(): return jnp.mean(blocks, axis=(1, 3, 5))  63.7 us
    concatenate x40, other arithmetic, extended(): block = jnp.concatenate([low, block, high], axis=dim)  39.1 us
    add x13, other arithmetic, relax_sweep(): field + relax_weight * (source - operate(padded, faces, scale)) / diagonal  38.7 us
  transfers between devices with their start and end apart: 102, of which 55 were waited for; matrix products, arithmetic and copies ran while one was open for 24% of the time, Pallas kernels for 0%

commit v1 on v0

v1 whole, which is shorter than its diff:
```python
import jax
import jax.numpy as jnp
from jax import lax
from jax.experimental import pallas as pl
from jax.experimental.pallas import tpu as pltpu
from jax.sharding import PartitionSpec as P

SWEEPS = 2
BOTTOM_SWEEPS = 8

floor_conduct = 0.1
relax_weight = 0.8

XH = 8
YH = 16
GX = 6
DC, DG = 6, 5
ZW = 16
L2X = 10
HI = lax.Precision.HIGHEST
F32 = jnp.float32
MIB = 1 << 20


def exchanges(count, step=1):
    swaps = []
    for e in range(2):
        pairs = []
        for i in range(count):
            if (i // step + e) % 2 == 0 and i + step < count:
                pairs += [(i, i + step), (i + step, i)]
        if pairs:
            swaps.append(pairs)
    return swaps


def upward(index, e, step=1):
    return ((index // step) + e) % 2 == 0


def spec(shape):
    return jax.ShapeDtypeStruct(shape, F32)


def in_vmem(shape):
    return pltpu.VMEM(shape, F32)


def held(x):
    return pltpu.with_memory_space_constraint(x, pltpu.VMEM)


def params(mib):
    return pltpu.CompilerParams(vmem_limit_bytes=mib * MIB)


def roll_up(v, axis):
    return pltpu.roll(v, v.shape[axis] - 1, axis)


def roll_down(v, axis):
    return pltpu.roll(v, 1, axis)


def loop(low, high, body, init=None):
    if init is None:

        def plain(i, carry):
            body(i)
            return carry

        lax.fori_loop(low, high, plain, 0)
        return None
    return lax.fori_loop(low, high, body, init)


def coefficients(c, kx, ky, kz, rd, low, high, scale):
    half = 0.5 * scale

    def faces(x):
        cx = c[x]
        fx = half * (cx + c[x + 1])
        fy = half * (cx + roll_up(cx, 0))
        fz = half * (cx + roll_up(cx, 1))
        kx[x] = fx
        ky[x] = fy
        kz[x] = fz
        return cx, fx, fy, fz

    _, first, _, _ = faces(low - 1)

    def body(x, before):
        cx, fx, fy, fz = faces(x)
        diagonal = fx + before + fy + roll_down(fy, 0) + fz + roll_down(fz, 1)
        inside = cx > 0.0
        rd[x] = jnp.where(inside, relax_weight / jnp.where(inside, diagonal, 1.0), 0.0)
        return fx

    loop(low, high, body, first)


def operate(v, kx, ky, kz, low, high, use):
    def body(x, before):
        vx = v[x]
        fx = kx[x] * (vx - v[x + 1])
        fy = ky[x] * (vx - roll_up(vx, 0))
        fz = kz[x] * (vx - roll_up(vx, 1))
        use(x, vx, (fx - before) + (fy - roll_down(fy, 0)) + (fz - roll_down(fz, 1)))
        return fx

    loop(low, high, body, kx[low - 1] * (v[low - 1] - v[low]))


def sweep(v, out, g, kx, ky, kz, rd, low, high):
    def use(x, vx, av):
        out[x] = vx + rd[x] * (g[x] - av)

    operate(v, kx, ky, kz, low, high, use)


def iota2(shape, dim):
    return lax.broadcasted_iota(jnp.int32, shape, dim)


def send_kernel(nx, ny, phase, mask, dev, c_out, g_out, *outs):
    ox, oy, _ = phase.shape

    def body(x):
        p = phase[x]
        c_out[x] = floor_conduct + (1.0 - floor_conduct) * (p * p * p)
        g_out[x] = mask[x].astype(F32) * dev[x]

    loop(0, ox, body)
    bx = lax.axis_index("boxes")
    sy = lax.axis_index("sub")
    place = 0
    rows = [pl.ds(pl.multiple_of(jnp.where(upward(sy, f), oy - YH, 0), 8), YH) for f in range(ny)]
    for e in range(nx):
        up = upward(bx, e)
        face = outs[place]
        place += 1
        face[0:XH] = c_out[pl.ds(jnp.where(up, ox - XH, 0), XH)]
        face[XH:XH + GX] = g_out[pl.ds(jnp.where(up, ox - GX, 0), GX)]
    for f in range(ny):
        face = outs[place]
        place += 1
        face[0] = c_out[:, rows[f], :]
        face[1] = g_out[:, rows[f], :]
    for e in range(nx):
        up = upward(bx, e)
        for f in range(ny):
            face = outs[place]
            place += 1
            face[0:DC] = c_out[pl.ds(jnp.where(up, ox - DC, 0), DC), rows[f], :]
            face[DC:DC + DG] = g_out[pl.ds(jnp.where(up, ox - DG, 0), DG), rows[f], :]


def halo_rows(ny, f, oy, up):
    if ny == 1:
        return oy
    return jnp.where(up, oy, oy + YH)


def extend_kernel(nx, ny, c, g, *refs):
    count = nx + ny + nx * ny
    got, (c_out, g_out, strip) = refs[:count], refs[count:]
    ox, oy, oz = c.shape
    bx = lax.axis_index("boxes")
    sy = lax.axis_index("sub")
    pz = lax.axis_index("pair")
    c_out[...] = jnp.zeros_like(c_out)
    g_out[...] = jnp.zeros_like(g_out)
    c_out[XH:XH + ox, 0:oy, :] = c[...]
    g_out[XH:XH + ox, 0:oy, :] = g[...]
    place = 0
    row = iota2((YH, oz), 0)

    def trim(values, up):
        if ny > 1:
            return values
        return jnp.where(lax.div(row, 2) == jnp.where(up, YH // 2 - 1, 0), 0.0, values)

    def below(up, planes):
        return jnp.where(up, XH + ox, XH - planes)

    for e in range(nx):
        up = upward(bx, e)
        face = got[place]
        place += 1
        c_out[pl.ds(below(up, XH), XH), 0:oy, :] = face[0:XH]
        g_out[pl.ds(below(up, GX), GX), 0:oy, :] = face[XH:XH + GX]
    for f in range(ny):
        up = upward(sy, f)
        face = got[place]
        place += 1
        rows = pl.ds(pl.multiple_of(halo_rows(ny, f, oy, up), 8), YH)

        def copy(x, face=face, rows=rows, up=up):
            c_out[XH + x, rows, :] = trim(face[0, x], up)
            g_out[XH + x, rows, :] = trim(face[1, x], up)

        loop(0, ox, copy)
    for e in range(nx):
        ux = upward(bx, e)
        for f in range(ny):
            up = upward(sy, f)
            face = got[place]
            place += 1
            rows = pl.ds(pl.multiple_of(halo_rows(ny, f, oy, up), 8), YH)
            for x in range(DC):
                c_out[below(ux, DC) + x, rows, :] = trim(face[x], up)
            for x in range(DG):
                g_out[below(ux, DG) + x, rows, :] = trim(face[DC + x], up)
    group = oz // ZW
    nrows = c_out.shape[1]
    lane = iota2((nrows, oz), 1)
    start = jnp.where(pz == 0, oz - ZW, 0)
    packed = c_out.shape[0] // group

    def pack(a):
        for which, source in enumerate((c_out, g_out)):
            total = None
            for b in range(group):
                moved = pltpu.roll(source[group * a + b], lax.rem(ZW * b + oz - start, oz), 1)
                total = moved if total is None else jnp.where(lane >= ZW * b, moved, total)
            strip[which * packed + a] = total

    loop(0, packed, pack)


def pool(source, low, high, out, matrix, work, rows, first):
    half = rows // 2

    def body(j):
        work[...] = jnp.dot(source(2 * j) + source(2 * j + 1), matrix, precision=HI, preferred_element_type=F32)
        out[j - first] = work[pl.ds(0, half, stride=2), :] + work[pl.ds(1, half, stride=2), :]

    loop(low, high, body)


def pool_matrix(size_in, size_out, limit, shift, weight):
    i, j = iota2((size_in, size_out), 0), iota2((size_in, size_out), 1)
    return jnp.where((i < limit) & (j == shift + lax.div(i, 2)), weight, 0.0).astype(F32)


def down_kernel(nx, cpad, gpad, strip, *refs):
    kx, ky, kz, rd, g, u0, kx1, ky1, kz1, rd1, c1, f1, u1, f2 = refs[:14]
    faces = refs[14:14 + nx]
    c, first, v1, work, work1 = refs[14 + nx:]
    planes, rows, oz = cpad.shape
    pz = lax.axis_index("pair")
    bx = lax.axis_index("boxes")
    group = oz // ZW
    packed = planes // group
    lane = iota2((rows, oz), 1)
    start = jnp.where(pz == 0, 0, oz - ZW)
    near = (lane >= start) & (lane < start + ZW)

    def unpack(a):
        cs, gs = strip[a], strip[packed + a]
        for b in range(group):
            x = group * a + b
            turn = lax.rem(start + oz - ZW * b, oz)
            c[x, :, 0:oz] = cpad[x]
            g[x, :, 0:oz] = gpad[x]
            c[x, :, oz:] = jnp.where(near, pltpu.roll(cs, turn, 1), 0.0)
            g[x, :, oz:] = jnp.where(near, pltpu.roll(gs, turn, 1), 0.0)

    loop(0, packed, unpack)
    edge = XH - GX
    coefficients(c, kx, ky, kz, rd, edge, planes - edge, 1.0)

    def start_sweep(x):
        first[x] = g[x] * rd[x]

    loop(edge, planes - edge, start_sweep)
    sweep(first, u0, g, kx, ky, kz, rd, edge + 1, planes - edge - 1)
    rest = first

    def use(x, vx, av):
        rest[x] = g[x] - av

    operate(u0, kx, ky, kz, edge + 2, planes - edge - 2, use)
    matrix = pool_matrix(2 * oz, oz, 2 * oz, 0, 0.125)
    planes1 = planes // 2
    pool(lambda x: c[x], 0, planes1, c1, matrix, work, rows, 0)
    f1[...] = jnp.zeros_like(f1)
    low1 = (edge + 2) // 2
    high1 = planes1 - low1
    pool(lambda x: rest[x], low1, high1, f1, matrix, work, rows, 0)
    coefficients(c1, kx1, ky1, kz1, rd1, 1, planes1 - 1, 0.25)

    def start_sweep1(x):
        v1[x] = f1[x] * rd1[x]

    loop(low1, high1, start_sweep1)
    u1[...] = jnp.zeros_like(u1)
    sweep(v1, u1, f1, kx1, ky1, kz1, rd1, low1 + 1, high1 - 1)
    h1 = XH // 2
    o1 = planes1 - XH

    def use1(x, vx, av):
        v1[x] = f1[x] - av

    operate(u1, kx1, ky1, kz1, h1, planes1 - h1, use1)
    half = oz // 2
    matrix1 = pool_matrix(oz, oz, half, jnp.where(pz == 0, 0, half // 2), 0.125)
    own1 = 2 * f2.shape[1]
    pool(lambda x: v1[x, 0:own1, :], h1 // 2, (planes1 - h1) // 2, f2, matrix1, work1, own1, h1 // 2)
    for e in range(nx):
        up = upward(bx, e)
        faces[e][0:h1] = u1[pl.ds(jnp.where(up, o1, h1), h1)]
        faces[e][h1:2 * h1 - 1] = f1[pl.ds(jnp.where(up, o1 + 1, h1), h1 - 1)]


def c2_kernel(c, c2, work):
    ox, oy, oz = c.shape
    pz = lax.axis_index("pair")
    quarter = oz // 4
    i, j = iota2((oz, oz), 0), iota2((oz, oz), 1)
    matrix = jnp.where(j == pz * quarter + lax.div(i, 4), 1.0 / 64.0, 0.0).astype(F32)

    def body(x):
        total = (c[4 * x] + c[4 * x + 1]) + (c[4 * x + 2] + c[4 * x + 3])
        work[...] = jnp.dot(total, matrix, precision=HI, preferred_element_type=F32)
        part = [work[pl.ds(k, oy // 4, stride=4), :] for k in range(4)]
        c2[x] = (part[0] + part[1]) + (part[2] + part[3])

    loop(0, ox // 4, body)


def up_kernel(nx, ny, nfar, *refs):
    kx, ky, kz, rd, g, u0, kx1, ky1, kz1, rd1, c1, f1, u1 = refs[:13]
    at = 13
    faces = refs[at:at + nx]
    at += nx
    pieces = 1 + nx + nfar
    got_f = refs[at:at + pieces]
    at += pieces
    got_c = refs[at:at + pieces]
    at += pieces
    field, residual = refs[at:at + 2]
    at += 2
    ua, ub, v1, w1, g1, c2, f2, kx2, ky2, kz2, rd2, v2, w2, work, wide = refs[at:]
    planes, rows, lanes = u0.shape
    planes1, rows1, oz = u1.shape
    planes2, rows2, _ = c2.shape
    ox, oy, _ = field.shape
    bx = lax.axis_index("boxes")
    sy = lax.axis_index("sub")
    pz = lax.axis_index("pair")
    o2x, o2y = ox // 4, oy // 4

    c2[...] = jnp.zeros_like(c2)
    f2[...] = jnp.zeros_like(f2)
    for out, got in ((c2, got_c), (f2, got_f)):
        places = [(L2X, o2x)]
        for e in range(nx):
            places.append((jnp.where(upward(bx, e), L2X + o2x, L2X - o2x), o2x))
        for e in range(nfar):
            places.append((jnp.where(upward(bx, e, 2), L2X + 2 * o2x, 0), L2X - o2x))
        for (x0, count), piece in zip(places, got):
            for f in range(ny + 1):
                if f == 0:
                    y0 = 0
                elif ny == 1:
                    y0 = pl.multiple_of(jnp.where(upward(sy, 0), o2y, rows2 - o2y), 8)
                else:
                    y0 = pl.multiple_of(jnp.where(upward(sy, f - 1), o2y, rows2 - o2y), 8)
                for x in range(count):
                    out[x0 + x, pl.ds(y0, o2y), :] = piece[f, x]
    coefficients(c2, kx2, ky2, kz2, rd2, 1, planes2 - 1, 0.0625)

    def start_sweep2(x):
        v2[x] = f2[x] * rd2[x]

    loop(1, planes2 - 1, start_sweep2)
    old, new = v2, w2
    for k in range(2, BOTTOM_SWEEPS + 1):
        sweep(old, new, f2, kx2, ky2, kz2, rd2, k, planes2 - k)
        old, new = new, old

    h1 = XH // 2
    o1 = planes1 - XH
    for x in range(planes1):
        g1[x] = f1[x]
        v1[x] = u1[x]
    for e in range(nx):
        up = upward(bx, e)
        v1[pl.ds(jnp.where(up, planes1 - h1, 0), h1)] = faces[e][0:h1]
        g1[pl.ds(jnp.where(up, planes1 - h1, 1), h1 - 1)] = faces[e][h1:2 * h1 - 1]
    i, j = iota2((oz, oz), 0), iota2((oz, oz), 1)
    spread_z = jnp.where(i == lax.div(lax.rem(pz * (oz // 2) + j, oz), 2), 1.0, 0.0).astype(F32)
    i, j = iota2((rows1, rows2), 0), iota2((rows1, rows2), 1)
    own1 = oy // 2
    if ny == 1:
        low_rows = (i >= own1) & jnp.logical_not(upward(sy, 0))
    else:
        low_rows = i >= own1 + YH // 2
    spread_y = jnp.where(j == lax.div(i, 2) + jnp.where(low_rows, rows2 - rows1 // 2, 0), 1.0, 0.0).astype(F32)
    base = L2X - h1 // 2

    def spread(x):
        moved = jnp.dot(old[base + x], spread_z, precision=HI, preferred_element_type=F32)
        moved = jnp.dot(spread_y, moved, precision=HI, preferred_element_type=F32)
        for k in range(2):
            y = 2 * x + k
            v1[y] = jnp.where(c1[y] > 0.0, v1[y] + moved, 0.0)

    loop(0, planes1 // 2, spread)
    sweep(v1, w1, g1, kx1, ky1, kz1, rd1, 1, planes1 - 1)
    sweep(w1, v1, g1, kx1, ky1, kz1, rd1, 2, planes1 - 2)

    i, j = iota2((oz, lanes), 0), iota2((oz, lanes), 1)
    spread_z0 = jnp.where(i == lax.div(j, 2), 1.0, 0.0).astype(F32)

    def spread0(x):
        work[...] = jnp.dot(v1[x], spread_z0, precision=HI, preferred_element_type=F32)
        for h in range(lanes // 128):
            values = work[:, 128 * h:128 * h + 128]
            wide[h, pl.ds(0, rows1, stride=2), :] = values
            wide[h, pl.ds(1, rows1, stride=2), :] = values
        for k in range(2):
            y = 2 * x + k
            for h in range(lanes // 128):
                cols = slice(128 * h, 128 * h + 128)
                ua[y, :, cols] = jnp.where(rd[y, :, cols] > 0.0, u0[y, :, cols] + wide[h], 0.0)

    loop(2, planes1 - 2, spread0)
    sweep(ua, ub, g, kx, ky, kz, rd, XH - 2, planes - XH + 2)
    sweep(ub, ua, g, kx, ky, kz, rd, XH - 1, planes - XH + 1)

    def use(x, vx, av):
        field[x - XH] = vx[0:oy, 0:oz]
        residual[x - XH] = g[x, 0:oy, 0:oz] - av[0:oy, 0:oz]

    operate(ua, kx, ky, kz, XH, planes - XH, use)


def call(kernel, outs, scratch=(), mib=60):
    return pl.pallas_call(
        kernel,
        out_shape=tuple(outs),
        scratch_shapes=tuple(pltpu.VMEM(s, F32) for s in scratch),
        compiler_params=params(mib),
    )


def per_device(phase, target_mask, deviation):
    ox, oy, oz = phase.shape
    nbox, nsub = lax.axis_size("boxes"), lax.axis_size("sub")
    swap_x, swap_y, far_x = exchanges(nbox), exchanges(nsub), exchanges(nbox, 2)
    nx, ny, nfar = len(swap_x), len(swap_y), len(far_x)
    pair_swap = [(0, 1), (1, 0)]

    def both(px, py):
        return [(a * nsub + c, b * nsub + d) for a, b in px for c, d in py]

    def traded(faces):
        out = []
        for e in range(nx):
            out.append(lax.ppermute(faces[e], "boxes", swap_x[e]))
        for f in range(ny):
            out.append(lax.ppermute(faces[nx + f], "sub", swap_y[f]))
        for e in range(nx):
            for f in range(ny):
                out.append(lax.ppermute(faces[nx + ny + e * ny + f], ("boxes", "sub"), both(swap_x[e], swap_y[f])))
        return out

    def gathered(own):
        line = own + lax.ppermute(own, "pair", pair_swap)
        sheet = jnp.stack([line] + [lax.ppermute(line, "sub", p) for p in swap_y])
        out = [sheet]
        for p in swap_x:
            out.append(lax.ppermute(sheet, "boxes", p))
        for e, p in enumerate(far_x):
            count = L2X - ox // 4
            at = jnp.where(upward(lax.axis_index("boxes"), e, 2), ox // 4 - count, 0)
            out.append(lax.ppermute(lax.dynamic_slice_in_dim(sheet, at, count, axis=1), "boxes", p))
        return out

    planes, rows = ox + 2 * XH, oy + YH * ny
    planes1, rows1 = planes // 2, rows // 2
    o2x, o2y = ox // 4, oy // 4
    planes2 = o2x + 2 * L2X
    rows2 = o2y * (ny + 1) + (8 if ny == 1 else 0)

    box = spec((ox, oy, oz))
    faces = [spec((XH + GX, oy, oz))] * nx + [spec((2, ox, YH, oz))] * ny + [spec((DC + DG, YH, oz))] * (nx * ny)
    c, g, *faces = call(lambda *r: send_kernel(nx, ny, *r), [box, box] + faces)(phase, target_mask, deviation)
    got = traded(faces)
    (c2,) = call(c2_kernel, [spec((o2x, o2y, oz))], [(oy, oz)])(c)
    got_c = gathered(c2)
    packed = 2 * planes // (oz // ZW)
    cpad, gpad, strip = call(
        lambda *r: extend_kernel(nx, ny, *r),
        [spec((planes, rows, oz)), spec((planes, rows, oz)), spec((packed, rows, oz))],
    )(c, g, *got)
    strip = lax.ppermute(strip, "pair", pair_swap)
    fine = (planes, rows, 2 * oz)
    middle = (planes1, rows1, oz)
    down = call(
        lambda *r: down_kernel(nx, *r),
        [in_vmem(fine)] * 6 + [in_vmem(middle)] * 7 + [spec((o2x, o2y, oz))] + [spec((XH - 1, rows1, oz))] * nx,
        [fine, fine, middle, (rows, oz), (oy // 2, oz)],
        mib=24,
    )(cpad, gpad, strip)
    kept, f2, sides = down[:13], down[13], down[14:]
    sides = [lax.ppermute(s, "boxes", p) for s, p in zip(sides, swap_x)]
    got_f = gathered(f2)
    lowest = (planes2, rows2, oz)
    return tuple(call(
        lambda *r: up_kernel(nx, ny, nfar, *r),
        [box, box],
        [fine, fine, middle, middle, middle] + [lowest] * 8 + [(rows1, 2 * oz), (2, rows, oz)],
        mib=24,
    )(*[held(x) for x in kept], *sides, *got_f, *got_c))


def solution(mesh):
    where = P(("groups", "boxes"), "sub", "pair")
    return jax.shard_map(
        per_device,
        mesh=mesh,
        in_specs=(where, where, where),
        out_specs=(where, where),
        check_vma=False,
    )
```

time: 821 us -> 167 us (0.20); the launches traced: 807 us -> 166 us
  local copies, waits for them, and re-layouts: 275 us -> 2.65 us
  other arithmetic: 195 us -> 0.89 us
  starting transfers between devices: 197 us -> 28.6 us
  waiting for transfers between devices: 137 us -> 15.2 us
  Pallas kernels: 0 us -> 118 us
    ppermute x102 -> x18, starting transfers between devices: 197 us -> 28.6 us  [the longest x4 13 us: gathered(): out.append(lax.ppermute(sheet, 'boxes', p))]
    reshape x6 -> x0, local copies, waits for them, and re-layouts: 138 us -> none  [the longest x3 131 us: coarsen(): blocks = field.reshape(size_a // 2, 2, size_b // 2, 2, size_c // 2, 2)]
    ppermute x102 -> x18, waiting for transfers between devices: 137 us -> 15.2 us  [the longest x2 6.7 us: traded(): lax.ppermute(faces[nx + ny + e * ny + f], ('boxes', 'sub'), both(swap_x[e...]
    pallas_call x0 -> x5, Pallas kernels: none -> 118 us  [the longest x1 57.4 us: per_device(): call(lambda *r: up_kernel(nx, ny, nfar, *r), [box, box], [fine, fine, mid...]
    unnamed x81 -> x12, local copies, waits for them, and re-layouts: 67 us -> 2.65 us
    reduce_sum x4 -> x0, other arithmetic: 63.7 us -> none  [coarsen(): return jnp.mean(blocks, axis=(1, 3, 5))]
    add x16 -> x2, other arithmetic: 43.9 us -> 0.86 us  [gathered(): line = own + lax.ppermute(own, 'pair', pair_swap)]
    concatenate x40 -> x0, other arithmetic: 39.1 us -> none  [extended(): block = jnp.concatenate([low, block, high], axis=dim)]
  transfers between devices with their start and end apart: 102 -> 18, of which waited for: 55 -> 5; matrix products, arithmetic and copies ran while one was open for 24% -> 1% of each run, Pallas kernels for 0% -> 30%
where the time goes in v1:
time: 167 us; the launch traced here: 166 us
  Pallas kernels  118 us (71%)
  starting transfers between devices  28.6 us (17%)
  waiting for transfers between devices  15.2 us (9%)
  local copies, waits for them, and re-layouts  2.65 us (2%)
    pallas_call x1, Pallas kernels, per_device(): call(lambda *r: up_kernel(nx, ny, nfar, *r), [box, box], [fine, fine, mid...  57.4 us
    pallas_call x1, Pallas kernels, per_device(): call(lambda *r: down_kernel(nx, *r), [in_vmem(fine)] * 6 + [in_vmem(middl...  47.2 us
    ppermute x4, starting transfers between devices, gathered(): out.append(lax.ppermute(sheet, 'boxes', p))  13 us
    ppermute x2, waiting for transfers between devices, traded(): lax.ppermute(faces[nx + ny + e * ny + f], ('boxes', 'sub'), both(swap_x[e...  6.7 us
    pallas_call x1, Pallas kernels, per_device(): call(lambda *r: extend_kernel(nx, ny, *r), [spec((planes, rows, oz)), spe...  5.89 us
    ppermute x2, waiting for transfers between devices, gathered(): lax.ppermute(lax.dynamic_slice_in_dim(sheet, at, count, axis=1), 'boxes', p)  5.41 us
    ppermute x2, starting transfers between devices, traded(): lax.ppermute(faces[nx + ny + e * ny + f], ('boxes', 'sub'), both(swap_x[e...  5.06 us
    pallas_call x1, Pallas kernels, per_device(): call(lambda *r: send_kernel(nx, ny, *r), [box, box] + faces)  4.18 us
  transfers between devices with their start and end apart: 18, of which 5 were waited for; matrix products, arithmetic and copies ran while one was open for 1% of the time, Pallas kernels for 30%

profile of v1, /device:TPU:0, one launch (start us, length us, event | category | flops | bytes accessed | tf_op | source)
XLA Modules:
  0.0 166.3 jit_solution(13774268555507823890)
XLA Ops:
  0.6 4.2 %shard_map.50 = (f32[32,64,128]{2,1,0:T(8,128)}, f32[32,64,128]{2,1,0:T(8,128)}, f32[14,64,128]{2,1,0:T(8,128)}, f32[14,64,128]{2,1,0:T(8,128)}, f32[2,32,16,128...) custom-call(f32[32,64,128]{2,1,0:T(8,128)} %r_0_.1, s32[32,64,128]{2,1,0:T(8,128)} %r_1_.1, ...), custom_call_target="tpu_custom_call" | custom-call | tf_op jit(solution)/shard_map/pallas_call | solution.py:490
  4.8 2.9 %collective-permute-start.2 = (f32[2,32,16,128]{3,2,1,0:T(8,128)}, f32[2,32,16,128]{3,2,1,0:T(8,128)S(1)}, u32[]{:S(2)}, u32[]{:S(2)}) collective-permute-start(f32[2,32,16,128]{3,2,1,0:T(8,128)} %get-tuple-element.32), channel_id=1, source_target_pairs={{0,2},{2,0},{1,3},{3,1},{4,6},{6,4},{5,7},{7,5},{8,10},{10,8},{9,1... | collective-permute-start | bytes 1572872 | tf_op jit(solution)/shard_map/ppermute | solution.py:464
  7.7 1.6 collective-permute-start
  9.3 0.7 collective-permute-start.1
  10.0 4.4 %collective-permute-start.3 = (f32[11,16,128]{2,1,0:T(8,128)}, f32[11,16,128]{2,1,0:T(8,128)S(1)}, u32[]{:S(2)}, u32[]{:S(2)}) collective-permute-start(f32[11,16,128]{2,1,0:T(8,128)} %get-tuple-element.33), channel_id=1, source_target_pairs={{0,6},{2,4},{4,2},{6,0},{8,14},{10,12},{12,10},{14,8},{1,7},{3,5},... | collective-permute-start | bytes 270344 | tf_op jit(solution)/shard_map/ppermute | solution.py:467
  14.4 0.7 collective-permute-start.4
  15.1 6.7 %collective-permute-done.3.r_5_ = f32[11,16,128]{2,1,0:T(8,128)S(1)} collective-permute-done((f32[11,16,128]{2,1,0:T(8,128)}, f32[11,16,128]{2,1,0:T(8,128)S(1)}, u32[]{:S(2)}, u32[]{:S(2)}) %collective-permute-start.3) | collective-permute-done | bytes 90144 | tf_op jit(solution)/shard_map/ppermute | solution.py:467
  22.9 5.9 %shard_map.51 = (f32[48,80,128]{2,1,0:T(8,128)}, f32[48,80,128]{2,1,0:T(8,128)}, f32[12,80,128]{2,1,0:T(8,128)}) custom-call(f32[32,64,128]{2,1,0:T(8,128)} %get-tuple-element.28.r_0_.c, f32[32,64,128]{2,1,0:T(8,128)} %get-tuple-element.29.r_1_, f32[14,64,128]{2,1,0:T(8,128)} %copy-done.2, f32[14,64,128]{2,1,0:T(8,128)} %copy-done.3, ...), custom_call_target="tpu_custom_call" | custom-call | tf_op jit(solution)/shard_map/pallas_call | solution.py:495
  28.8 3.4 %shard_map.53 = f32[8,16,128]{2,1,0:T(8,128)} custom-call(f32[32,64,128]{2,1,0:T(8,128)} %get-tuple-element.28.r_0_.c), custom_call_target="tpu_custom_call" | custom-call | tf_op jit(solution)/shard_map/pallas_call | solution.py:492
  32.8 1.1 collective-permute-done.13
  33.9 0.8 add.16
  34.7 1.7 %collective-permute-start.14 = (f32[8,16,128]{2,1,0:T(8,128)S(1)}, f32[8,16,128]{2,1,0:T(8,128)S(1)}, u32[]{:S(2)}, u32[]{:S(2)}) collective-permute-start(f32[8,16,128]{2,1,0:T(8,128)S(1)} %add.16), channel_id=1, source_target_pairs={{0,2},{2,0},{1,3},{3,1},{4,6},{6,4},{5,7},{7,5},{8,10},{10,8},{9,1... | collective-permute-start | bytes 196616 | tf_op jit(solution)/shard_map/ppermute | solution.py:472
  36.5 1.5 copy-done
  38.0 47.2 %shard_map.52 = (f32[48,80,256]{2,1,0:T(8,128)S(1)}, f32[48,80,256]{2,1,0:T(8,128)S(1)}, f32[48,80,256]{2,1,0:T(8,128)S(1)}, f32[48,80,256]{2,1,0:T(8,128)S(1)},...) custom-call(f32[48,80,128]{2,1,0:T(8,128)S(1)} %copy-done, ...), custom_call_target="tpu_custom_call" | custom-call | tf_op jit(solution)/shard_map/pallas_call | solution.py:502
  85.4 0.7 collective-permute-start.16
  86.1 7.5 %collective-permute-start.15 = (f32[2,8,16,128]{3,2,1,0:T(8,128)S(1)}, f32[2,8,16,128]{3,2,1,0:T(8,128)S(1)}, u32[]{:S(2)}, u32[]{:S(2)}) collective-permute-start(f32[2,8,16,128]{3,2,1,0:T(8,128)S(1)} %pad_maximum_fusion.1.r_19_), channel_id=1, source_target_pairs={{0,4},{4,0},{8,12},{12,8},{1,5},{5,1},{9,13},{13,9},{2,6},{6,2},{1... | collective-permute-start | bytes 393224 | tf_op jit(solution)/shard_map/ppermute | solution.py:475
  94.2 1.8 %collective-permute-start.6 = (f32[7,40,128]{2,1,0:T(8,128)S(1)}, f32[7,40,128]{2,1,0:T(8,128)S(1)}, u32[]{:S(2)}, u32[]{:S(2)}) collective-permute-start(f32[7,40,128]{2,1,0:T(8,128)S(1)} %get-tuple-element.51), channel_id=1, source_target_pairs={{0,4},{4,0},{8,12},{12,8},{1,5},{5,1},{9,13},{13,9},{2,6},{6,2},{1... | collective-permute-start | bytes 430088 | tf_op jit(solution)/shard_map/ppermute | solution.py:509
  95.9 2.0 %collective-permute-done.9 = f32[8,16,128]{2,1,0:T(8,128)S(1)} collective-permute-done((f32[8,16,128]{2,1,0:T(8,128)S(1)}, f32[8,16,128]{2,1,0:T(8,128)S(1)}, u32[]{:S(2)}, u32[]{:S(2)}) %collective-permute-start.9) | collective-permute-done | bytes 65568 | tf_op jit(solution)/shard_map/ppermute | solution.py:472
  97.9 0.7 collective-permute-start.7
  98.6 0.6 collective-permute-done.17.r_22_
  99.2 0.7 collective-permute-start.11
  99.9 4.2 %collective-permute-start.10 = (f32[2,8,16,128]{3,2,1,0:T(8,128)S(1)}, f32[2,8,16,128]{3,2,1,0:T(8,128)S(1)}, u32[]{:S(2)}, u32[]{:S(2)}) collective-permute-start(f32[2,8,16,128]{3,2,1,0:T(8,128)S(1)} %pad_maximum_fusion.r_15_), channel_id=1, source_target_pairs={{0,4},{4,0},{8,12},{12,8},{1,5},{5,1},{9,13},{13,9},{2,6},{6,2},{1... | collective-permute-start | bytes 393224 | tf_op jit(solution)/shard_map/ppermute | solution.py:475
  104.1 4.8 %collective-permute-done.12.r_18_ = f32[2,2,16,128]{3,2,1,0:T(8,128)S(1)} collective-permute-done((f32[2,2,16,128]{3,2,1,0:T(8,128)S(1)}, f32[2,2,16,128]{3,2,1,0:T(8,128)S(1)}, u32[]{:S(2)}, u32[]{:S(2)}) %collective-permute-start.12) | collective-permute-done | bytes 32800 | tf_op jit(solution)/shard_map/ppermute | solution.py:479
  108.9 57.4 %shard_map.54 = (f32[32,64,128]{2,1,0:T(8,128)}, f32[32,64,128]{2,1,0:T(8,128)}) custom-call(f32[48,80,256]{2,1,0:T(8,128)S(1)} %get-tuple-element.38.r_0_, f32[48,80,256]{2,1,0:T(8,128)S(1)} %get-tuple-element.39.r_1_, f32[48,80,256]{2,1,0:T(8,128)S(1)} %get-tuple-element.40.r_2_, f32[48,80,256]{2,1,0:T(8,128)S(1)} %get-tuple-element.41.r_3_, ...), custom_call_target="tpu_custom_call" | custom-call | tf_op jit(solution)/shard_map/pallas_call | solution.py:512
  (35 shorter events, 2.4 us)
Async XLA Ops:
  4.8 17.0 %collective-permute-start.2 = (f32[2,32,16,128]{3,2,1,0:T(8,128)}, f32[2,32,16,128]{3,2,1,0:T(8,128)S(1)}, u32[]{:S(2)}, u32[]{:S(2)}) collective-permute-start(f32[2,32,16,128]{3,2,1,0:T(8,128)} %get-tuple-element.32), channel_id=1, source_target_pairs={{0,2},{2,0},{1,3},{3,1},{4,6},{6,4},{5,7},{7,5},{8,10},{10,8},{9,1... | collective-permute-start | bytes 1572872 | tf_op jit(solution)/shard_map/ppermute | solution.py:464
  7.7 14.0 %collective-permute-start = (f32[14,64,128]{2,1,0:T(8,128)}, f32[14,64,128]{2,1,0:T(8,128)S(1)}, u32[]{:S(2)}, u32[]{:S(2)}) collective-permute-start(f32[14,64,128]{2,1,0:T(8,128)} %get-tuple-element.30), channel_id=1, source_target_pairs={{0,4},{4,0},{8,12},{12,8},{1,5},{5,1},{9,13},{13,9},{2,6},{6,2},{1... | collective-permute-start | bytes 1376264 | tf_op jit(solution)/shard_map/ppermute | solution.py:462
  9.3 12.5 %collective-permute-start.1 = (f32[14,64,128]{2,1,0:T(8,128)}, f32[14,64,128]{2,1,0:T(8,128)S(1)}, u32[]{:S(2)}, u32[]{:S(2)}) collective-permute-start(f32[14,64,128]{2,1,0:T(8,128)} %get-tuple-element.31), channel_id=1, source_target_pairs={{4,8},{8,4},{5,9},{9,5},{6,10},{10,6},{7,11},{11,7},{20,24},{24,20... | collective-permute-start | bytes 1376264 | tf_op jit(solution)/shard_map/ppermute | solution.py:462
  10.0 11.8 %collective-permute-start.3 = (f32[11,16,128]{2,1,0:T(8,128)}, f32[11,16,128]{2,1,0:T(8,128)S(1)}, u32[]{:S(2)}, u32[]{:S(2)}) collective-permute-start(f32[11,16,128]{2,1,0:T(8,128)} %get-tuple-element.33), channel_id=1, source_target_pairs={{0,6},{2,4},{4,2},{6,0},{8,14},{10,12},{12,10},{14,8},{1,7},{3,5},... | collective-permute-start | bytes 270344 | tf_op jit(solution)/shard_map/ppermute | solution.py:467
  14.4 7.4 %collective-permute-start.4 = (f32[11,16,128]{2,1,0:T(8,128)}, f32[11,16,128]{2,1,0:T(8,128)S(1)}, u32[]{:S(2)}, u32[]{:S(2)}) collective-permute-start(f32[11,16,128]{2,1,0:T(8,128)} %get-tuple-element.34), channel_id=1, source_target_pairs={{4,10},{6,8},{8,6},{10,4},{5,11},{7,9},{9,7},{11,5},{20,26},{22,24... | collective-permute-start | bytes 270344 | tf_op jit(solution)/shard_map/ppermute | solution.py:467
  21.8 0.6 copy-start.4
  21.8 0.7 copy-start.5
  21.8 0.8 copy-start.2
  21.8 1.0 copy-start.3
  21.8 1.1 copy-start.1
  28.8 7.6 %collective-permute-start.5 = (f32[12,80,128]{2,1,0:T(8,128)}, f32[12,80,128]{2,1,0:T(8,128)S(1)}, u32[]{:S(2)}, u32[]{:S(2)}) collective-permute-start(f32[12,80,128]{2,1,0:T(8,128)} %get-tuple-element.37), channel_id=1, source_target_pairs={{0,1},{1,0},{2,3},{3,2},{4,5},{5,4},{6,7},{7,6},{8,9},{9,8},{10,11... | collective-permute-start | bytes 1474568 | tf_op jit(solution)/shard_map/ppermute | solution.py:499
  32.3 1.6 collective-permute-start.13
  34.7 50.6 %collective-permute-start.14 = (f32[8,16,128]{2,1,0:T(8,128)S(1)}, f32[8,16,128]{2,1,0:T(8,128)S(1)}, u32[]{:S(2)}, u32[]{:S(2)}) collective-permute-start(f32[8,16,128]{2,1,0:T(8,128)S(1)} %add.16), channel_id=1, source_target_pairs={{0,2},{2,0},{1,3},{3,1},{4,6},{6,4},{5,7},{7,5},{8,10},{10,8},{9,1... | collective-permute-start | bytes 196616 | tf_op jit(solution)/shard_map/ppermute | solution.py:472
  36.5 1.5 copy-start
  85.2 8.3 %collective-permute-start.8 = (f32[8,16,128]{2,1,0:T(8,128)S(1)}, f32[8,16,128]{2,1,0:T(8,128)S(1)}, u32[]{:S(2)}, u32[]{:S(2)}) collective-permute-start(f32[8,16,128]{2,1,0:T(8,128)S(1)} %get-tuple-element.53), channel_id=1, source_target_pairs={{0,1},{1,0},{2,3},{3,2},{4,5},{5,4},{6,7},{7,6},{8,9},{9,8},{10,11... | collective-permute-start | bytes 196616 | tf_op jit(solution)/shard_map/ppermute | solution.py:471
  85.4 14.5 %collective-permute-start.16 = (f32[2,8,16,128]{3,2,1,0:T(8,128)S(1)}, f32[2,8,16,128]{3,2,1,0:T(8,128)S(1)}, u32[]{:S(2)}, u32[]{:S(2)}) collective-permute-start(f32[2,8,16,128]{3,2,1,0:T(8,128)S(1)} %pad_maximum_fusion.1.r_19_), channel_id=1, source_target_pairs={{4,8},{8,4},{5,9},{9,5},{6,10},{10,6},{7,11},{11,7},{20,24},{24,20... | collective-permute-start | bytes 393224 | tf_op jit(solution)/shard_map/ppermute | solution.py:475
  86.1 18.0 %collective-permute-start.15 = (f32[2,8,16,128]{3,2,1,0:T(8,128)S(1)}, f32[2,8,16,128]{3,2,1,0:T(8,128)S(1)}, u32[]{:S(2)}, u32[]{:S(2)}) collective-permute-start(f32[2,8,16,128]{3,2,1,0:T(8,128)S(1)} %pad_maximum_fusion.1.r_19_), channel_id=1, source_target_pairs={{0,4},{4,0},{8,12},{12,8},{1,5},{5,1},{9,13},{13,9},{2,6},{6,2},{1... | collective-permute-start | bytes 393224 | tf_op jit(solution)/shard_map/ppermute | solution.py:475
  93.6 4.3 %collective-permute-start.9 = (f32[8,16,128]{2,1,0:T(8,128)S(1)}, f32[8,16,128]{2,1,0:T(8,128)S(1)}, u32[]{:S(2)}, u32[]{:S(2)}) collective-permute-start(f32[8,16,128]{2,1,0:T(8,128)S(1)} %add.14), channel_id=1, source_target_pairs={{0,2},{2,0},{1,3},{3,1},{4,6},{6,4},{5,7},{7,5},{8,10},{10,8},{9,1... | collective-permute-start | bytes 196616 | tf_op jit(solution)/shard_map/ppermute | solution.py:472
  94.2 5.0 %collective-permute-start.17 = (f32[2,2,16,128]{3,2,1,0:T(8,128)S(1)}, f32[2,2,16,128]{3,2,1,0:T(8,128)S(1)}, u32[]{:S(2)}, u32[]{:S(2)}) collective-permute-start(f32[2,2,16,128]{3,2,1,0:T(8,128)S(1)} %fusion), channel_id=1, source_target_pairs={{0,8},{8,0},{4,12},{12,4},{1,9},{9,1},{5,13},{13,5},{2,10},{10,2},... | collective-permute-start | bytes 98312 | tf_op jit(solution)/shard_map/ppermute | solution.py:479
  94.2 9.9 %collective-permute-start.6 = (f32[7,40,128]{2,1,0:T(8,128)S(1)}, f32[7,40,128]{2,1,0:T(8,128)S(1)}, u32[]{:S(2)}, u32[]{:S(2)}) collective-permute-start(f32[7,40,128]{2,1,0:T(8,128)S(1)} %get-tuple-element.51), channel_id=1, source_target_pairs={{0,4},{4,0},{8,12},{12,8},{1,5},{5,1},{9,13},{13,9},{2,6},{6,2},{1... | collective-permute-start | bytes 430088 | tf_op jit(solution)/shard_map/ppermute | solution.py:509
  97.9 6.2 %collective-permute-start.7 = (f32[7,40,128]{2,1,0:T(8,128)S(1)}, f32[7,40,128]{2,1,0:T(8,128)S(1)}, u32[]{:S(2)}, u32[]{:S(2)}) collective-permute-start(f32[7,40,128]{2,1,0:T(8,128)S(1)} %get-tuple-element.52), channel_id=1, source_target_pairs={{4,8},{8,4},{5,9},{9,5},{6,10},{10,6},{7,11},{11,7},{20,24},{24,20... | collective-permute-start | bytes 430088 | tf_op jit(solution)/shard_map/ppermute | solution.py:509
  99.2 9.7 %collective-permute-start.11 = (f32[2,8,16,128]{3,2,1,0:T(8,128)S(1)}, f32[2,8,16,128]{3,2,1,0:T(8,128)S(1)}, u32[]{:S(2)}, u32[]{:S(2)}) collective-permute-start(f32[2,8,16,128]{3,2,1,0:T(8,128)S(1)} %pad_maximum_fusion.r_15_), channel_id=1, source_target_pairs={{4,8},{8,4},{5,9},{9,5},{6,10},{10,6},{7,11},{11,7},{20,24},{24,20... | collective-permute-start | bytes 393224 | tf_op jit(solution)/shard_map/ppermute | solution.py:475
  99.9 9.0 %collective-permute-start.10 = (f32[2,8,16,128]{3,2,1,0:T(8,128)S(1)}, f32[2,8,16,128]{3,2,1,0:T(8,128)S(1)}, u32[]{:S(2)}, u32[]{:S(2)}) collective-permute-start(f32[2,8,16,128]{3,2,1,0:T(8,128)S(1)} %pad_maximum_fusion.r_15_), channel_id=1, source_target_pairs={{0,4},{4,0},{8,12},{12,8},{1,5},{5,1},{9,13},{13,9},{2,6},{6,2},{1... | collective-permute-start | bytes 393224 | tf_op jit(solution)/shard_map/ppermute | solution.py:475
  104.1 4.8 %collective-permute-start.12 = (f32[2,2,16,128]{3,2,1,0:T(8,128)S(1)}, f32[2,2,16,128]{3,2,1,0:T(8,128)S(1)}, u32[]{:S(2)}, u32[]{:S(2)}) collective-permute-start(f32[2,2,16,128]{3,2,1,0:T(8,128)S(1)} %fusion.1), channel_id=1, source_target_pairs={{0,8},{8,0},{4,12},{12,4},{1,9},{9,1},{5,13},{13,5},{2,10},{10,2},... | collective-permute-start | bytes 98312 | tf_op jit(solution)/shard_map/ppermute | solution.py:479

commit v2 on v1

--- a/solution.py
+++ b/solution.py
@@ -62,16 +62,34 @@
     return pltpu.roll(v, 1, axis)
 
 
-def loop(low, high, body, init=None):
-    if init is None:
-
-        def plain(i, carry):
+def loop(low, high, body, init=None, unroll=1):
+    def step(i, carry):
+        if init is None:
             body(i)
             return carry
-
-        lax.fori_loop(low, high, plain, 0)
-        return None
-    return lax.fori_loop(low, high, body, init)
+        return body(i, carry)
+
+    carry = 0 if init is None else init
+    whole = (high - low) // unroll
+    if whole > 1:
+
+        def several(k, carry):
+            for j in range(unroll):
+                carry = step(low + k * unroll + j, carry)
+            return carry
+
+        carry = lax.fori_loop(0, whole, several, carry)
+        low += whole * unroll
+    for i in range(low, high):
+        carry = step(i, carry)
+    return carry
+
+
+def unrolling(ref):
+    return UNROLL.get(ref.shape[1] * ref.shape[2] // 1024, 4)
+
+
+UNROLL = {20: 4, 5: 8}
 
 
 def coefficients(c, kx, ky, kz, rd, low, high, scale):
@@ -96,7 +114,7 @@
         rd[x] = jnp.where(inside, relax_weight / jnp.where(inside, diagonal, 1.0), 0.0)
         return fx
 
-    loop(low, high, body, first)
+    loop(low, high, body, first, unrolling(rd))
 
 
 def operate(v, kx, ky, kz, low, high, use):
@@ -108,7 +126,7 @@
         use(x, vx, (fx - before) + (fy - roll_down(fy, 0)) + (fz - roll_down(fz, 1)))
         return fx
 
-    loop(low, high, body, kx[low - 1] * (v[low - 1] - v[low]))
+    loop(low, high, body, kx[low - 1] * (v[low - 1] - v[low]), unrolling(v))
 
 
 def sweep(v, out, g, kx, ky, kz, rd, low, high):
@@ -235,7 +253,7 @@
         work[...] = jnp.dot(source(2 * j) + source(2 * j + 1), matrix, precision=HI, preferred_element_type=F32)
         out[j - first] = work[pl.ds(0, half, stride=2), :] + work[pl.ds(1, half, stride=2), :]
 
-    loop(low, high, body)
+    loop(low, high, body, unroll=4)
 
 
 def pool_matrix(size_in, size_out, limit, shift, weight):

time: 167 us -> 108 us (0.65)
  Pallas kernels: 118 us -> 59.4 us
    pallas_call x1, Pallas kernels: 57.4 us -> 23.8 us  [per_device(): call(lambda *r: up_kernel(nx, ny, nfar, *r), [box, box], [fine, fine, mid...]
    pallas_call x1, Pallas kernels: 47.2 us -> 22.1 us  [per_device(): call(lambda *r: down_kernel(nx, *r), [in_vmem(fine)] * 6 + [in_vmem(middl...]
  transfers between devices with their start and end apart: 18 -> 18, of which waited for: 5 -> 5; matrix products, arithmetic and copies ran while one was open for 1% -> 1% of each run, Pallas kernels for 30% -> 24%
where the time goes in v2:
time: 108 us
  Pallas kernels  59.4 us (55%)
  starting transfers between devices  28.6 us (26%)
  waiting for transfers between devices  15.2 us (14%)
  local copies, waits for them, and re-layouts  2.65 us (2%)
    pallas_call x1, Pallas kernels, per_device(): call(lambda *r: up_kernel(nx, ny, nfar, *r), [box, box], [fine, fine, mid...  23.8 us
    pallas_call x1, Pallas kernels, per_device(): call(lambda *r: down_kernel(nx, *r), [in_vmem(fine)] * 6 + [in_vmem(middl...  22.1 us
    ppermute x4, starting transfers between devices, gathered(): out.append(lax.ppermute(sheet, 'boxes', p))  13 us
    ppermute x2, waiting for transfers between devices, traded(): lax.ppermute(faces[nx + ny + e * ny + f], ('boxes', 'sub'), both(swap_x[e...  6.7 us
    pallas_call x1, Pallas kernels, per_device(): call(lambda *r: extend_kernel(nx, ny, *r), [spec((planes, rows, oz)), spe...  5.89 us
    ppermute x2, waiting for transfers between devices, gathered(): lax.ppermute(lax.dynamic_slice_in_dim(sheet, at, count, axis=1), 'boxes', p)  5.42 us
    ppermute x2, starting transfers between devices, traded(): lax.ppermute(faces[nx + ny + e * ny + f], ('boxes', 'sub'), both(swap_x[e...  5.06 us
    pallas_call x1, Pallas kernels, per_device(): call(lambda *r: send_kernel(nx, ny, *r), [box, box] + faces)  4.18 us
  transfers between devices with their start and end apart: 18, of which 5 were waited for; matrix products, arithmetic and copies ran while one was open for 1% of the time, Pallas kernels for 24%

profile of v2, /device:TPU:0, one launch (start us, length us, event | category | flops | bytes accessed | tf_op | source)
XLA Modules:
  0.0 107.5 jit_solution(10737319618681656267)
XLA Ops:
  0.6 4.2 %shard_map.50 = (f32[32,64,128]{2,1,0:T(8,128)}, f32[32,64,128]{2,1,0:T(8,128)}, f32[14,64,128]{2,1,0:T(8,128)}, f32[14,64,128]{2,1,0:T(8,128)}, f32[2,32,16,128...) custom-call(f32[32,64,128]{2,1,0:T(8,128)} %r_0_.1, s32[32,64,128]{2,1,0:T(8,128)} %r_1_.1, ...), custom_call_target="tpu_custom_call" | custom-call | tf_op jit(solution)/shard_map/pallas_call | solution.py:508
  4.8 2.9 %collective-permute-start.2 = (f32[2,32,16,128]{3,2,1,0:T(8,128)}, f32[2,32,16,128]{3,2,1,0:T(8,128)S(1)}, u32[]{:S(2)}, u32[]{:S(2)}) collective-permute-start(f32[2,32,16,128]{3,2,1,0:T(8,128)} %get-tuple-element.32), channel_id=1, source_target_pairs={{0,2},{2,0},{1,3},{3,1},{4,6},{6,4},{5,7},{7,5},{8,10},{10,8},{9,1... | collective-permute-start | bytes 1572872 | tf_op jit(solution)/shard_map/ppermute | solution.py:482
  7.7 1.6 %collective-permute-start = (f32[14,64,128]{2,1,0:T(8,128)}, f32[14,64,128]{2,1,0:T(8,128)S(1)}, u32[]{:S(2)}, u32[]{:S(2)}) collective-permute-start(f32[14,64,128]{2,1,0:T(8,128)} %get-tuple-element.30), channel_id=1, source_target_pairs={{0,4},{4,0},{8,12},{12,8},{1,5},{5,1},{9,13},{13,9},{2,6},{6,2},{1... | collective-permute-start | bytes 1376264 | tf_op jit(solution)/shard_map/ppermute | solution.py:480
  9.3 0.7 collective-permute-start.1
  10.0 4.4 %collective-permute-start.3 = (f32[11,16,128]{2,1,0:T(8,128)}, f32[11,16,128]{2,1,0:T(8,128)S(1)}, u32[]{:S(2)}, u32[]{:S(2)}) collective-permute-start(f32[11,16,128]{2,1,0:T(8,128)} %get-tuple-element.33), channel_id=1, source_target_pairs={{0,6},{2,4},{4,2},{6,0},{8,14},{10,12},{12,10},{14,8},{1,7},{3,5},... | collective-permute-start | bytes 270344 | tf_op jit(solution)/shard_map/ppermute | solution.py:485
  14.4 0.7 collective-permute-start.4
  15.1 6.7 %collective-permute-done.3.r_5_ = f32[11,16,128]{2,1,0:T(8,128)S(1)} collective-permute-done((f32[11,16,128]{2,1,0:T(8,128)}, f32[11,16,128]{2,1,0:T(8,128)S(1)}, u32[]{:S(2)}, u32[]{:S(2)}) %collective-permute-start.3) | collective-permute-done | bytes 90144 | tf_op jit(solution)/shard_map/ppermute | solution.py:485
  22.9 5.9 %shard_map.51 = (f32[48,80,128]{2,1,0:T(8,128)}, f32[48,80,128]{2,1,0:T(8,128)}, f32[12,80,128]{2,1,0:T(8,128)}) custom-call(f32[32,64,128]{2,1,0:T(8,128)} %get-tuple-element.28.r_0_.c, f32[32,64,128]{2,1,0:T(8,128)} %get-tuple-element.29.r_1_, f32[14,64,128]{2,1,0:T(8,128)} %copy-done.2, f32[14,64,128]{2,1,0:T(8,128)} %copy-done.3, ...), custom_call_target="tpu_custom_call" | custom-call | tf_op jit(solution)/shard_map/pallas_call | solution.py:513
  28.8 3.4 %shard_map.53 = f32[8,16,128]{2,1,0:T(8,128)} custom-call(f32[32,64,128]{2,1,0:T(8,128)} %get-tuple-element.28.r_0_.c), custom_call_target="tpu_custom_call" | custom-call | tf_op jit(solution)/shard_map/pallas_call | solution.py:510
  32.8 1.1 %collective-permute-done.13 = f32[8,16,128]{2,1,0:T(8,128)S(1)} collective-permute-done((f32[8,16,128]{2,1,0:T(8,128)}, f32[8,16,128]{2,1,0:T(8,128)S(1)}, u32[]{:S(2)}, u32[]{:S(2)}) %collective-permute-start.13) | collective-permute-done | bytes 65568 | tf_op jit(solution)/shard_map/ppermute | solution.py:489
  33.9 0.8 add.16
  34.7 1.7 %collective-permute-start.14 = (f32[8,16,128]{2,1,0:T(8,128)S(1)}, f32[8,16,128]{2,1,0:T(8,128)S(1)}, u32[]{:S(2)}, u32[]{:S(2)}) collective-permute-start(f32[8,16,128]{2,1,0:T(8,128)S(1)} %add.16), channel_id=1, source_target_pairs={{0,2},{2,0},{1,3},{3,1},{4,6},{6,4},{5,7},{7,5},{8,10},{10,8},{9,1... | collective-permute-start | bytes 196616 | tf_op jit(solution)/shard_map/ppermute | solution.py:490
  36.5 1.5 %copy-done = f32[48,80,128]{2,1,0:T(8,128)S(1)} copy-done((f32[48,80,128]{2,1,0:T(8,128)S(1)}, f32[48,80,128]{2,1,0:T(8,128)}, u32[]{:S(2)}) %copy-start) | copy-done | bytes 1966104
  38.0 22.1 %shard_map.52 = (f32[48,80,256]{2,1,0:T(8,128)S(1)}, f32[48,80,256]{2,1,0:T(8,128)S(1)}, f32[48,80,256]{2,1,0:T(8,128)S(1)}, f32[48,80,256]{2,1,0:T(8,128)S(1)},...) custom-call(f32[48,80,128]{2,1,0:T(8,128)S(1)} %copy-done, ...), custom_call_target="tpu_custom_call" | custom-call | tf_op jit(solution)/shard_map/pallas_call | solution.py:520
  60.2 0.7 collective-permute-start.16
  60.9 7.5 %collective-permute-start.15 = (f32[2,8,16,128]{3,2,1,0:T(8,128)S(1)}, f32[2,8,16,128]{3,2,1,0:T(8,128)S(1)}, u32[]{:S(2)}, u32[]{:S(2)}) collective-permute-start(f32[2,8,16,128]{3,2,1,0:T(8,128)S(1)} %pad_maximum_fusion.1.r_19_), channel_id=1, source_target_pairs={{0,4},{4,0},{8,12},{12,8},{1,5},{5,1},{9,13},{13,9},{2,6},{6,2},{1... | collective-permute-start | bytes 393224 | tf_op jit(solution)/shard_map/ppermute | solution.py:493
  69.0 1.8 %collective-permute-start.6 = (f32[7,40,128]{2,1,0:T(8,128)S(1)}, f32[7,40,128]{2,1,0:T(8,128)S(1)}, u32[]{:S(2)}, u32[]{:S(2)}) collective-permute-start(f32[7,40,128]{2,1,0:T(8,128)S(1)} %get-tuple-element.51), channel_id=1, source_target_pairs={{0,4},{4,0},{8,12},{12,8},{1,5},{5,1},{9,13},{13,9},{2,6},{6,2},{1... | collective-permute-start | bytes 430088 | tf_op jit(solution)/shard_map/ppermute | solution.py:527
  70.8 2.0 %collective-permute-done.9 = f32[8,16,128]{2,1,0:T(8,128)S(1)} collective-permute-done((f32[8,16,128]{2,1,0:T(8,128)S(1)}, f32[8,16,128]{2,1,0:T(8,128)S(1)}, u32[]{:S(2)}, u32[]{:S(2)}) %collective-permute-start.9) | collective-permute-done | bytes 65568 | tf_op jit(solution)/shard_map/ppermute | solution.py:490
  72.8 0.7 collective-permute-start.7
  73.4 0.6 collective-permute-done.17.r_22_
  74.1 0.7 collective-permute-start.11
  74.8 4.1 %collective-permute-start.10 = (f32[2,8,16,128]{3,2,1,0:T(8,128)S(1)}, f32[2,8,16,128]{3,2,1,0:T(8,128)S(1)}, u32[]{:S(2)}, u32[]{:S(2)}) collective-permute-start(f32[2,8,16,128]{3,2,1,0:T(8,128)S(1)} %pad_maximum_fusion.r_15_), channel_id=1, source_target_pairs={{0,4},{4,0},{8,12},{12,8},{1,5},{5,1},{9,13},{13,9},{2,6},{6,2},{1... | collective-permute-start | bytes 393224 | tf_op jit(solution)/shard_map/ppermute | solution.py:493
  78.9 4.8 %collective-permute-done.12.r_18_ = f32[2,2,16,128]{3,2,1,0:T(8,128)S(1)} collective-permute-done((f32[2,2,16,128]{3,2,1,0:T(8,128)S(1)}, f32[2,2,16,128]{3,2,1,0:T(8,128)S(1)}, u32[]{:S(2)}, u32[]{:S(2)}) %collective-permute-start.12) | collective-permute-done | bytes 32800 | tf_op jit(solution)/shard_map/ppermute | solution.py:497
  83.7 23.8 %shard_map.54 = (f32[32,64,128]{2,1,0:T(8,128)}, f32[32,64,128]{2,1,0:T(8,128)}) custom-call(f32[48,80,256]{2,1,0:T(8,128)S(1)} %get-tuple-element.38.r_0_, f32[48,80,256]{2,1,0:T(8,128)S(1)} %get-tuple-element.39.r_1_, f32[48,80,256]{2,1,0:T(8,128)S(1)} %get-tuple-element.40.r_2_, f32[48,80,256]{2,1,0:T(8,128)S(1)} %get-tuple-element.41.r_3_, ...), custom_call_target="tpu_custom_call" | custom-call | tf_op jit(solution)/shard_map/pallas_call | solution.py:530
  (35 shorter events, 2.4 us)
Async XLA Ops:
  4.8 17.0 %collective-permute-start.2 = (f32[2,32,16,128]{3,2,1,0:T(8,128)}, f32[2,32,16,128]{3,2,1,0:T(8,128)S(1)}, u32[]{:S(2)}, u32[]{:S(2)}) collective-permute-start(f32[2,32,16,128]{3,2,1,0:T(8,128)} %get-tuple-element.32), channel_id=1, source_target_pairs={{0,2},{2,0},{1,3},{3,1},{4,6},{6,4},{5,7},{7,5},{8,10},{10,8},{9,1... | collective-permute-start | bytes 1572872 | tf_op jit(solution)/shard_map/ppermute | solution.py:482
  7.7 14.0 %collective-permute-start = (f32[14,64,128]{2,1,0:T(8,128)}, f32[14,64,128]{2,1,0:T(8,128)S(1)}, u32[]{:S(2)}, u32[]{:S(2)}) collective-permute-start(f32[14,64,128]{2,1,0:T(8,128)} %get-tuple-element.30), channel_id=1, source_target_pairs={{0,4},{4,0},{8,12},{12,8},{1,5},{5,1},{9,13},{13,9},{2,6},{6,2},{1... | collective-permute-start | bytes 1376264 | tf_op jit(solution)/shard_map/ppermute | solution.py:480
  9.3 12.5 %collective-permute-start.1 = (f32[14,64,128]{2,1,0:T(8,128)}, f32[14,64,128]{2,1,0:T(8,128)S(1)}, u32[]{:S(2)}, u32[]{:S(2)}) collective-permute-start(f32[14,64,128]{2,1,0:T(8,128)} %get-tuple-element.31), channel_id=1, source_target_pairs={{4,8},{8,4},{5,9},{9,5},{6,10},{10,6},{7,11},{11,7},{20,24},{24,20... | collective-permute-start | bytes 1376264 | tf_op jit(solution)/shard_map/ppermute | solution.py:480
  10.0 11.8 %collective-permute-start.3 = (f32[11,16,128]{2,1,0:T(8,128)}, f32[11,16,128]{2,1,0:T(8,128)S(1)}, u32[]{:S(2)}, u32[]{:S(2)}) collective-permute-start(f32[11,16,128]{2,1,0:T(8,128)} %get-tuple-element.33), channel_id=1, source_target_pairs={{0,6},{2,4},{4,2},{6,0},{8,14},{10,12},{12,10},{14,8},{1,7},{3,5},... | collective-permute-start | bytes 270344 | tf_op jit(solution)/shard_map/ppermute | solution.py:485
  14.4 7.4 %collective-permute-start.4 = (f32[11,16,128]{2,1,0:T(8,128)}, f32[11,16,128]{2,1,0:T(8,128)S(1)}, u32[]{:S(2)}, u32[]{:S(2)}) collective-permute-start(f32[11,16,128]{2,1,0:T(8,128)} %get-tuple-element.34), channel_id=1, source_target_pairs={{4,10},{6,8},{8,6},{10,4},{5,11},{7,9},{9,7},{11,5},{20,26},{22,24... | collective-permute-start | bytes 270344 | tf_op jit(solution)/shard_map/ppermute | solution.py:485
  21.8 0.6 copy-start.4
  21.8 0.7 copy-start.5
  21.8 0.8 copy-start.2
  21.8 1.0 copy-start.3
  21.8 1.1 %copy-start.1 = (f32[2,32,16,128]{3,2,1,0:T(8,128)}, f32[2,32,16,128]{3,2,1,0:T(8,128)S(1)}, u32[]{:S(2)}) copy-start(f32[2,32,16,128]{3,2,1,0:T(8,128)S(1)} %collective-permute-done.2.r_4_) | copy-start | bytes 1572868
  28.8 7.6 %collective-permute-start.5 = (f32[12,80,128]{2,1,0:T(8,128)}, f32[12,80,128]{2,1,0:T(8,128)S(1)}, u32[]{:S(2)}, u32[]{:S(2)}) collective-permute-start(f32[12,80,128]{2,1,0:T(8,128)} %get-tuple-element.37), channel_id=1, source_target_pairs={{0,1},{1,0},{2,3},{3,2},{4,5},{5,4},{6,7},{7,6},{8,9},{9,8},{10,11... | collective-permute-start | bytes 1474568 | tf_op jit(solution)/shard_map/ppermute | solution.py:517
  32.3 1.6 %collective-permute-start.13 = (f32[8,16,128]{2,1,0:T(8,128)}, f32[8,16,128]{2,1,0:T(8,128)S(1)}, u32[]{:S(2)}, u32[]{:S(2)}) collective-permute-start(f32[8,16,128]{2,1,0:T(8,128)} %shard_map.53), channel_id=1, source_target_pairs={{0,1},{1,0},{2,3},{3,2},{4,5},{5,4},{6,7},{7,6},{8,9},{9,8},{10,11... | collective-permute-start | bytes 196616 | tf_op jit(solution)/shard_map/ppermute | solution.py:489
  34.7 25.5 %collective-permute-start.14 = (f32[8,16,128]{2,1,0:T(8,128)S(1)}, f32[8,16,128]{2,1,0:T(8,128)S(1)}, u32[]{:S(2)}, u32[]{:S(2)}) collective-permute-start(f32[8,16,128]{2,1,0:T(8,128)S(1)} %add.16), channel_id=1, source_target_pairs={{0,2},{2,0},{1,3},{3,1},{4,6},{6,4},{5,7},{7,5},{8,10},{10,8},{9,1... | collective-permute-start | bytes 196616 | tf_op jit(solution)/shard_map/ppermute | solution.py:490
  36.5 1.5 %copy-start = (f32[48,80,128]{2,1,0:T(8,128)S(1)}, f32[48,80,128]{2,1,0:T(8,128)}, u32[]{:S(2)}) copy-start(f32[48,80,128]{2,1,0:T(8,128)} %get-tuple-element.35.r_0_) | copy-start | bytes 5898244
  60.1 8.3 %collective-permute-start.8 = (f32[8,16,128]{2,1,0:T(8,128)S(1)}, f32[8,16,128]{2,1,0:T(8,128)S(1)}, u32[]{:S(2)}, u32[]{:S(2)}) collective-permute-start(f32[8,16,128]{2,1,0:T(8,128)S(1)} %get-tuple-element.53), channel_id=1, source_target_pairs={{0,1},{1,0},{2,3},{3,2},{4,5},{5,4},{6,7},{7,6},{8,9},{9,8},{10,11... | collective-permute-start | bytes 196616 | tf_op jit(solution)/shard_map/ppermute | solution.py:489
  60.2 14.5 %collective-permute-start.16 = (f32[2,8,16,128]{3,2,1,0:T(8,128)S(1)}, f32[2,8,16,128]{3,2,1,0:T(8,128)S(1)}, u32[]{:S(2)}, u32[]{:S(2)}) collective-permute-start(f32[2,8,16,128]{3,2,1,0:T(8,128)S(1)} %pad_maximum_fusion.1.r_19_), channel_id=1, source_target_pairs={{4,8},{8,4},{5,9},{9,5},{6,10},{10,6},{7,11},{11,7},{20,24},{24,20... | collective-permute-start | bytes 393224 | tf_op jit(solution)/shard_map/ppermute | solution.py:493
  60.9 18.0 %collective-permute-start.15 = (f32[2,8,16,128]{3,2,1,0:T(8,128)S(1)}, f32[2,8,16,128]{3,2,1,0:T(8,128)S(1)}, u32[]{:S(2)}, u32[]{:S(2)}) collective-permute-start(f32[2,8,16,128]{3,2,1,0:T(8,128)S(1)} %pad_maximum_fusion.1.r_19_), channel_id=1, source_target_pairs={{0,4},{4,0},{8,12},{12,8},{1,5},{5,1},{9,13},{13,9},{2,6},{6,2},{1... | collective-permute-start | bytes 393224 | tf_op jit(solution)/shard_map/ppermute | solution.py:493
  68.4 4.3 %collective-permute-start.9 = (f32[8,16,128]{2,1,0:T(8,128)S(1)}, f32[8,16,128]{2,1,0:T(8,128)S(1)}, u32[]{:S(2)}, u32[]{:S(2)}) collective-permute-start(f32[8,16,128]{2,1,0:T(8,128)S(1)} %add.14), channel_id=1, source_target_pairs={{0,2},{2,0},{1,3},{3,1},{4,6},{6,4},{5,7},{7,5},{8,10},{10,8},{9,1... | collective-permute-start | bytes 196616 | tf_op jit(solution)/shard_map/ppermute | solution.py:490
  69.0 5.1 %collective-permute-start.17 = (f32[2,2,16,128]{3,2,1,0:T(8,128)S(1)}, f32[2,2,16,128]{3,2,1,0:T(8,128)S(1)}, u32[]{:S(2)}, u32[]{:S(2)}) collective-permute-start(f32[2,2,16,128]{3,2,1,0:T(8,128)S(1)} %fusion), channel_id=1, source_target_pairs={{0,8},{8,0},{4,12},{12,4},{1,9},{9,1},{5,13},{13,5},{2,10},{10,2},... | collective-permute-start | bytes 98312 | tf_op jit(solution)/shard_map/ppermute | solution.py:497
  69.0 9.9 %collective-permute-start.6 = (f32[7,40,128]{2,1,0:T(8,128)S(1)}, f32[7,40,128]{2,1,0:T(8,128)S(1)}, u32[]{:S(2)}, u32[]{:S(2)}) collective-permute-start(f32[7,40,128]{2,1,0:T(8,128)S(1)} %get-tuple-element.51), channel_id=1, source_target_pairs={{0,4},{4,0},{8,12},{12,8},{1,5},{5,1},{9,13},{13,9},{2,6},{6,2},{1... | collective-permute-start | bytes 430088 | tf_op jit(solution)/shard_map/ppermute | solution.py:527
  72.8 6.2 %collective-permute-start.7 = (f32[7,40,128]{2,1,0:T(8,128)S(1)}, f32[7,40,128]{2,1,0:T(8,128)S(1)}, u32[]{:S(2)}, u32[]{:S(2)}) collective-permute-start(f32[7,40,128]{2,1,0:T(8,128)S(1)} %get-tuple-element.52), channel_id=1, source_target_pairs={{4,8},{8,4},{5,9},{9,5},{6,10},{10,6},{7,11},{11,7},{20,24},{24,20... | collective-permute-start | bytes 430088 | tf_op jit(solution)/shard_map/ppermute | solution.py:527
  74.1 9.6 %collective-permute-start.11 = (f32[2,8,16,128]{3,2,1,0:T(8,128)S(1)}, f32[2,8,16,128]{3,2,1,0:T(8,128)S(1)}, u32[]{:S(2)}, u32[]{:S(2)}) collective-permute-start(f32[2,8,16,128]{3,2,1,0:T(8,128)S(1)} %pad_maximum_fusion.r_15_), channel_id=1, source_target_pairs={{4,8},{8,4},{5,9},{9,5},{6,10},{10,6},{7,11},{11,7},{20,24},{24,20... | collective-permute-start | bytes 393224 | tf_op jit(solution)/shard_map/ppermute | solution.py:493
  74.8 9.0 %collective-permute-start.10 = (f32[2,8,16,128]{3,2,1,0:T(8,128)S(1)}, f32[2,8,16,128]{3,2,1,0:T(8,128)S(1)}, u32[]{:S(2)}, u32[]{:S(2)}) collective-permute-start(f32[2,8,16,128]{3,2,1,0:T(8,128)S(1)} %pad_maximum_fusion.r_15_), channel_id=1, source_target_pairs={{0,4},{4,0},{8,12},{12,8},{1,5},{5,1},{9,13},{13,9},{2,6},{6,2},{1... | collective-permute-start | bytes 393224 | tf_op jit(solution)/shard_map/ppermute | solution.py:493
  78.9 4.8 %collective-permute-start.12 = (f32[2,2,16,128]{3,2,1,0:T(8,128)S(1)}, f32[2,2,16,128]{3,2,1,0:T(8,128)S(1)}, u32[]{:S(2)}, u32[]{:S(2)}) collective-permute-start(f32[2,2,16,128]{3,2,1,0:T(8,128)S(1)} %fusion.1), channel_id=1, source_target_pairs={{0,8},{8,0},{4,12},{12,4},{1,9},{9,1},{5,13},{13,5},{2,10},{10,2},... | collective-permute-start | bytes 98312 | tf_op jit(solution)/shard_map/ppermute | solution.py:497

commit v3 on v2

--- a/solution.py
+++ b/solution.py
@@ -17,8 +17,8 @@
 DC, DG = 6, 5
 ZW = 16
 L2X = 10
-HI = lax.Precision.HIGHEST
 F32 = jnp.float32
+BF16 = jnp.bfloat16
 MIB = 1 << 20
 
 
@@ -140,15 +140,13 @@
     return lax.broadcasted_iota(jnp.int32, shape, dim)
 
 
-def send_kernel(nx, ny, phase, mask, dev, c_out, g_out, *outs):
+def make(phase, mask, dev, x, rows=slice(None)):
+    p = phase[x, rows, :]
+    return floor_conduct + (1.0 - floor_conduct) * (p * p * p), mask[x, rows, :].astype(F32) * dev[x, rows, :]
+
+
+def send_kernel(nx, ny, phase, mask, dev, *outs):
     ox, oy, _ = phase.shape
-
-    def body(x):
-        p = phase[x]
-        c_out[x] = floor_conduct + (1.0 - floor_conduct) * (p * p * p)
-        g_out[x] = mask[x].astype(F32) * dev[x]
-
-    loop(0, ox, body)
     bx = lax.axis_index("boxes")
     sy = lax.axis_index("sub")
     place = 0
@@ -157,20 +155,81 @@
         up = upward(bx, e)
         face = outs[place]
         place += 1
-        face[0:XH] = c_out[pl.ds(jnp.where(up, ox - XH, 0), XH)]
-        face[XH:XH + GX] = g_out[pl.ds(jnp.where(up, ox - GX, 0), GX)]
+        for x in range(XH):
+            p = phase[jnp.where(up, ox - XH, 0) + x]
+            face[x] = floor_conduct + (1.0 - floor_conduct) * (p * p * p)
+        for x in range(GX):
+            at = jnp.where(up, ox - GX, 0) + x
+            face[XH + x] = mask[at].astype(F32) * dev[at]
     for f in range(ny):
         face = outs[place]
         place += 1
-        face[0] = c_out[:, rows[f], :]
-        face[1] = g_out[:, rows[f], :]
+
+        def body(x, face=face, f=f):
+            face[0, x], face[1, x] = make(phase, mask, dev, x, rows[f])
+
+        loop(0, ox, body, unroll=8)
     for e in range(nx):
         up = upward(bx, e)
         for f in range(ny):
             face = outs[place]
             place += 1
-            face[0:DC] = c_out[pl.ds(jnp.where(up, ox - DC, 0), DC), rows[f], :]
-            face[DC:DC + DG] = g_out[pl.ds(jnp.where(up, ox - DG, 0), DG), rows[f], :]
+            for x in range(DC):
+                face[x] = make(phase, mask, dev, jnp.where(up, ox - DC, 0) + x, rows[f])[0]
+            for x in range(DG):
+                face[DC + x] = make(phase, mask, dev, jnp.where(up, ox - DG, 0) + x, rows[f])[1]
+
+
+def pack(planes, turns, lane):
+    total = None
+    for b, (plane, turn) in enumerate(zip(planes, turns)):
+        moved = pltpu.roll(plane, turn, 1)
+        total = moved if total is None else jnp.where(lane >= ZW * b, moved, total)
+    return total
+
+
+def strip_turns(oz, start):
+    return [lax.rem(ZW * b + oz - start, oz) for b in range(oz // ZW)]
+
+
+def split(x):
+    high = x.astype(BF16)
+    rest = x - high.astype(F32)
+    middle = rest.astype(BF16)
+    low = (rest - middle.astype(F32)).astype(BF16)
+    return jnp.concatenate([high, middle, low], axis=-1)
+
+
+def times(x, matrix):
+    return jnp.dot(split(x), matrix, preferred_element_type=F32)
+
+
+def thrice(matrix):
+    return jnp.concatenate([matrix.astype(BF16)] * 3, axis=0)
+
+
+def own_kernel(phase, mask, dev, c, g, strip, c2, sums, work):
+    ox, oy, oz = phase.shape
+    pz = lax.axis_index("pair")
+
+    def body(x):
+        c[x], g[x] = make(phase, mask, dev, x)
+
+    loop(0, ox, body, unroll=4)
+    quarter = oz // 4
+    i, j = iota2((oz, oz), 0), iota2((oz, oz), 1)
+    matrix = thrice(jnp.where(j == pz * quarter + lax.div(i, 4), 1.0 / 64.0, 0.0))
+    for x in range(ox // 4):
+        sums[...] = (c[4 * x] + c[4 * x + 1]) + (c[4 * x + 2] + c[4 * x + 3])
+        part = [sums[pl.ds(k, oy // 4, stride=4), :] for k in range(4)]
+        work[x] = (part[0] + part[1]) + (part[2] + part[3])
+    c2[...] = times(work[...].reshape(-1, oz), matrix).reshape(c2.shape)
+    group = oz // ZW
+    turns = strip_turns(oz, jnp.where(pz == 0, oz - ZW, 0))
+    lane = iota2((oy, oz), 1)
+    for which, source in enumerate((c, g)):
+        for a in range(ox // group):
+            strip[which, a] = pack([source[group * a + b] for b in range(group)], turns, lane)
 
 
 def halo_rows(ny, f, oy, up):
@@ -179,17 +238,18 @@
     return jnp.where(up, oy, oy + YH)
 
 
-def extend_kernel(nx, ny, c, g, *refs):
+def extend_kernel(nx, ny, c, g, own, *refs):
     count = nx + ny + nx * ny
     got, (c_out, g_out, strip) = refs[:count], refs[count:]
     ox, oy, oz = c.shape
+    planes, nrows, _ = c_out.shape
     bx = lax.axis_index("boxes")
     sy = lax.axis_index("sub")
     pz = lax.axis_index("pair")
-    c_out[...] = jnp.zeros_like(c_out)
-    g_out[...] = jnp.zeros_like(g_out)
-    c_out[XH:XH + ox, 0:oy, :] = c[...]
-    g_out[XH:XH + ox, 0:oy, :] = g[...]
+    for out, source in ((c_out, c), (g_out, g)):
+        for low, high in ((0, XH), (XH + ox, planes)):
+            out[low:high] = jnp.zeros((high - low, nrows, oz), F32)
+        out[XH:XH + ox, 0:oy, :] = source[...]
     place = 0
     row = iota2((YH, oz), 0)
 
@@ -217,7 +277,7 @@
             c_out[XH + x, rows, :] = trim(face[0, x], up)
             g_out[XH + x, rows, :] = trim(face[1, x], up)
 
-        loop(0, ox, copy)
+        loop(0, ox, copy, unroll=8)
     for e in range(nx):
         ux = upward(bx, e)
         for f in range(ny):
@@ -230,35 +290,44 @@
             for x in range(DG):
                 g_out[below(ux, DG) + x, rows, :] = trim(face[DC + x], up)
     group = oz // ZW
-    nrows = c_out.shape[1]
-    lane = iota2((nrows, oz), 1)
-    start = jnp.where(pz == 0, oz - ZW, 0)
-    packed = c_out.shape[0] // group
-
-    def pack(a):
-        for which, source in enumerate((c_out, g_out)):
-            total = None
-            for b in range(group):
-                moved = pltpu.roll(source[group * a + b], lax.rem(ZW * b + oz - start, oz), 1)
-                total = moved if total is None else jnp.where(lane >= ZW * b, moved, total)
-            strip[which * packed + a] = total
-
-    loop(0, packed, pack)
-
-
-def pool(source, low, high, out, matrix, work, rows, first):
-    half = rows // 2
-
-    def body(j):
-        work[...] = jnp.dot(source(2 * j) + source(2 * j + 1), matrix, precision=HI, preferred_element_type=F32)
-        out[j - first] = work[pl.ds(0, half, stride=2), :] + work[pl.ds(1, half, stride=2), :]
-
-    loop(low, high, body, unroll=4)
+    turns = strip_turns(oz, jnp.where(pz == 0, oz - ZW, 0))
+    packed = planes // group
+    side = XH // group
+    for which, source in enumerate((c_out, g_out)):
+        for a in range(packed):
+            at = which * packed + a
+            if side <= a < packed - side:
+                strip[at, 0:oy, :] = own[which, a - side]
+                rows = slice(oy, nrows)
+            else:
+                rows = slice(0, nrows)
+            lane = iota2((nrows - (rows.start or 0), oz), 1)
+            strip[at, rows, :] = pack([source[group * a + b, rows, :] for b in range(group)], turns, lane)
+
+
+def pool(source, low, high, out, matrix, work, step):
+    tiles, rows, width = work.shape
+
+    def body(k):
+        sums = []
+        for j in range(step):
+            at = 2 * (low + step * k + j)
+            total = source(at) + source(at + 1)
+            parts = []
+            for h in range(tiles // step):
+                slot = j * (tiles // step) + h
+                work[slot] = total[:, width * h:width * h + width]
+                parts.append(work[slot, pl.ds(0, rows // 2, stride=2), :] + work[slot, pl.ds(1, rows // 2, stride=2), :])
+            sums.append(jnp.concatenate(parts, axis=1))
+        done = times(jnp.concatenate(sums, axis=0), matrix)
+        out[pl.ds(step * k, step)] = done.reshape(step, rows // 2, done.shape[1])
+
+    loop(0, (high - low) // step, body)
 
 
 def pool_matrix(size_in, size_out, limit, shift, weight):
     i, j = iota2((size_in, size_out), 0), iota2((size_in, size_out), 1)
-    return jnp.where((i < limit) & (j == shift + lax.div(i, 2)), weight, 0.0).astype(F32)
+    return thrice(jnp.where((i < limit) & (j == shift + lax.div(i, 2)), weight, 0.0))
 
 
 def down_kernel(nx, cpad, gpad, strip, *refs):
@@ -301,11 +370,11 @@
     operate(u0, kx, ky, kz, edge + 2, planes - edge - 2, use)
     matrix = pool_matrix(2 * oz, oz, 2 * oz, 0, 0.125)
     planes1 = planes // 2
-    pool(lambda x: c[x], 0, planes1, c1, matrix, work, rows, 0)
+    pool(lambda x: c[x], 0, planes1, c1, matrix, work, 4)
     f1[...] = jnp.zeros_like(f1)
     low1 = (edge + 2) // 2
     high1 = planes1 - low1
-    pool(lambda x: rest[x], low1, high1, f1, matrix, work, rows, 0)
+    pool(lambda x: rest[x], low1, high1, f1.at[low1:high1], matrix, work, 4)
     coefficients(c1, kx1, ky1, kz1, rd1, 1, planes1 - 1, 0.25)
 
     def start_sweep1(x):
@@ -324,27 +393,11 @@
     half = oz // 2
     matrix1 = pool_matrix(oz, oz, half, jnp.where(pz == 0, 0, half // 2), 0.125)
     own1 = 2 * f2.shape[1]
-    pool(lambda x: v1[x, 0:own1, :], h1 // 2, (planes1 - h1) // 2, f2, matrix1, work1, own1, h1 // 2)
+    pool(lambda x: v1[x, 0:own1, :], h1 // 2, (planes1 - h1) // 2, f2, matrix1, work1, f2.shape[0])
     for e in range(nx):
         up = upward(bx, e)
         faces[e][0:h1] = u1[pl.ds(jnp.where(up, o1, h1), h1)]
         faces[e][h1:2 * h1 - 1] = f1[pl.ds(jnp.where(up, o1 + 1, h1), h1 - 1)]
-
-
-def c2_kernel(c, c2, work):
-    ox, oy, oz = c.shape
-    pz = lax.axis_index("pair")
-    quarter = oz // 4
-    i, j = iota2((oz, oz), 0), iota2((oz, oz), 1)
-    matrix = jnp.where(j == pz * quarter + lax.div(i, 4), 1.0 / 64.0, 0.0).astype(F32)
-
-    def body(x):
-        total = (c[4 * x] + c[4 * x + 1]) + (c[4 * x + 2] + c[4 * x + 3])
-        work[...] = jnp.dot(total, matrix, precision=HI, preferred_element_type=F32)
-        part = [work[pl.ds(k, oy // 4, stride=4), :] for k in range(4)]
-        c2[x] = (part[0] + part[1]) + (part[2] + part[3])
-
-    loop(0, ox // 4, body)
 
 
 def up_kernel(nx, ny, nfar, *refs):
@@ -359,7 +412,7 @@
     at += pieces
     field, residual = refs[at:at + 2]
     at += 2
-    ua, ub, v1, w1, g1, c2, f2, kx2, ky2, kz2, rd2, v2, w2, work, wide = refs[at:]
+    ua, ub, v1, w1, g1, c2, f2, kx2, ky2, kz2, rd2, v2, w2, tall, wide = refs[at:]
     planes, rows, lanes = u0.shape
     planes1, rows1, oz = u1.shape
     planes2, rows2, _ = c2.shape
@@ -408,43 +461,46 @@
         v1[pl.ds(jnp.where(up, planes1 - h1, 0), h1)] = faces[e][0:h1]
         g1[pl.ds(jnp.where(up, planes1 - h1, 1), h1 - 1)] = faces[e][h1:2 * h1 - 1]
     i, j = iota2((oz, oz), 0), iota2((oz, oz), 1)
-    spread_z = jnp.where(i == lax.div(lax.rem(pz * (oz // 2) + j, oz), 2), 1.0, 0.0).astype(F32)
-    i, j = iota2((rows1, rows2), 0), iota2((rows1, rows2), 1)
-    own1 = oy // 2
-    if ny == 1:
-        low_rows = (i >= own1) & jnp.logical_not(upward(sy, 0))
-    else:
-        low_rows = i >= own1 + YH // 2
-    spread_y = jnp.where(j == lax.div(i, 2) + jnp.where(low_rows, rows2 - rows1 // 2, 0), 1.0, 0.0).astype(F32)
+    spread_z = thrice(jnp.where(i == lax.div(lax.rem(pz * (oz // 2) + j, oz), 2), 1.0, 0.0))
     base = L2X - h1 // 2
-
-    def spread(x):
-        moved = jnp.dot(old[base + x], spread_z, precision=HI, preferred_element_type=F32)
-        moved = jnp.dot(spread_y, moved, precision=HI, preferred_element_type=F32)
+    count = planes1 // 2
+    moved = times(old[base:base + count].reshape(count * rows2, oz), spread_z)
+    row = iota2((8, oz), 0)
+    for x in range(count):
+        t = moved[x * rows2:x * rows2 + rows2]
+        if ny == 1:
+            halo = jnp.where(upward(sy, 0), t[o2y:o2y + 8], pltpu.roll(t[rows2 - 8:], 4, 0))
+        else:
+            halo = jnp.where(row < 4, t[o2y:o2y + 8], t[rows2 - 8:])
+        t = jnp.concatenate([t[0:o2y], halo], axis=0)
+        tall[x, pl.ds(0, o2y + 8, stride=2), :] = t
+        tall[x, pl.ds(1, o2y + 8, stride=2), :] = t
+        both = tall[x, 0:rows1, :]
         for k in range(2):
             y = 2 * x + k
-            v1[y] = jnp.where(c1[y] > 0.0, v1[y] + moved, 0.0)
-
-    loop(0, planes1 // 2, spread)
+            v1[y] = jnp.where(c1[y] > 0.0, v1[y] + both, 0.0)
+
     sweep(v1, w1, g1, kx1, ky1, kz1, rd1, 1, planes1 - 1)
     sweep(w1, v1, g1, kx1, ky1, kz1, rd1, 2, planes1 - 2)
 
     i, j = iota2((oz, lanes), 0), iota2((oz, lanes), 1)
-    spread_z0 = jnp.where(i == lax.div(j, 2), 1.0, 0.0).astype(F32)
-
-    def spread0(x):
-        work[...] = jnp.dot(v1[x], spread_z0, precision=HI, preferred_element_type=F32)
-        for h in range(lanes // 128):
-            values = work[:, 128 * h:128 * h + 128]
-            wide[h, pl.ds(0, rows1, stride=2), :] = values
-            wide[h, pl.ds(1, rows1, stride=2), :] = values
-        for k in range(2):
-            y = 2 * x + k
-            for h in range(lanes // 128):
-                cols = slice(128 * h, 128 * h + 128)
-                ua[y, :, cols] = jnp.where(rd[y, :, cols] > 0.0, u0[y, :, cols] + wide[h], 0.0)
-
-    loop(2, planes1 - 2, spread0)
+    spread_z0 = thrice(jnp.where(i == lax.div(j, 2), 1.0, 0.0))
+    step = 4
+
+    def spread0(n):
+        low = 2 + step * n
+        moved = times(v1[pl.ds(low, step)].reshape(step * rows1, oz), spread_z0)
+        for m in range(step):
+            for h in range(lanes // oz):
+                cols = slice(oz * h, oz * h + oz)
+                values = moved[m * rows1:m * rows1 + rows1, cols]
+                wide[2 * m + h, pl.ds(0, rows1, stride=2), :] = values
+                wide[2 * m + h, pl.ds(1, rows1, stride=2), :] = values
+                for k in range(2):
+                    y = 2 * (low + m) + k
+                    ua[y, :, cols] = jnp.where(rd[y, :, cols] > 0.0, u0[y, :, cols] + wide[2 * m + h], 0.0)
+
+    loop(0, (planes1 - 4) // step, spread0)
     sweep(ua, ub, g, kx, ky, kz, rd, XH - 2, planes - XH + 2)
     sweep(ub, ua, g, kx, ky, kz, rd, XH - 1, planes - XH + 1)
 
@@ -505,24 +561,33 @@
 
     box = spec((ox, oy, oz))
     faces = [spec((XH + GX, oy, oz))] * nx + [spec((2, ox, YH, oz))] * ny + [spec((DC + DG, YH, oz))] * (nx * ny)
-    c, g, *faces = call(lambda *r: send_kernel(nx, ny, *r), [box, box] + faces)(phase, target_mask, deviation)
+    faces = call(lambda *r: send_kernel(nx, ny, *r), faces)(phase, target_mask, deviation)
     got = traded(faces)
-    (c2,) = call(c2_kernel, [spec((o2x, o2y, oz))], [(oy, oz)])(c)
+    phase, target_mask, deviation, _ = lax.optimization_barrier((phase, target_mask, deviation, faces))
+    group = oz // ZW
+    c, g, own, c2 = call(
+        own_kernel,
+        [in_vmem((ox, oy, oz)), in_vmem((ox, oy, oz)), in_vmem((2, ox // group, oy, oz)), spec((o2x, o2y, oz))],
+        [(oy, oz), (o2x, o2y, oz)],
+        mib=24,
+    )(phase, target_mask, deviation)
     got_c = gathered(c2)
-    packed = 2 * planes // (oz // ZW)
+    got, got_c = lax.optimization_barrier((got, got_c))
+    padded = (planes, rows, oz)
     cpad, gpad, strip = call(
         lambda *r: extend_kernel(nx, ny, *r),
-        [spec((planes, rows, oz)), spec((planes, rows, oz)), spec((packed, rows, oz))],
-    )(c, g, *got)
+        [in_vmem(padded), in_vmem(padded), spec((2 * planes // group, rows, oz))],
+        mib=24,
+    )(held(c), held(g), held(own), *got)
     strip = lax.ppermute(strip, "pair", pair_swap)
     fine = (planes, rows, 2 * oz)
     middle = (planes1, rows1, oz)
     down = call(
         lambda *r: down_kernel(nx, *r),
         [in_vmem(fine)] * 6 + [in_vmem(middle)] * 7 + [spec((o2x, o2y, oz))] + [spec((XH - 1, rows1, oz))] * nx,
-        [fine, fine, middle, (rows, oz), (oy // 2, oz)],
+        [fine, fine, middle, (8, rows, oz), (o2x, oy // 2, oz)],
         mib=24,
-    )(cpad, gpad, strip)
+    )(held(cpad), held(gpad), strip)
     kept, f2, sides = down[:13], down[13], down[14:]
     sides = [lax.ppermute(s, "boxes", p) for s, p in zip(sides, swap_x)]
     got_f = gathered(f2)
@@ -530,7 +595,7 @@
     return tuple(call(
         lambda *r: up_kernel(nx, ny, nfar, *r),
         [box, box],
-        [fine, fine, middle, middle, middle] + [lowest] * 8 + [(rows1, 2 * oz), (2, rows, oz)],
+        [fine, fine, middle, middle, middle] + [lowest] * 8 + [(planes1 // 2, 2 * (o2y + 8), oz), (8, rows, oz)],
         mib=24,
     )(*[held(x) for x in kept], *sides, *got_f, *got_c))
 

time: 108 us -> 95 us (0.88)
  Pallas kernels: 59.4 us -> 40.7 us
  local copies, waits for them, and re-layouts: 2.65 us -> 6.08 us
  other arithmetic: 0.89 us -> 2.28 us
    pallas_call x1, Pallas kernels: 23.8 us -> 16 us  [per_device(): call(lambda *r: up_kernel(nx, ny, nfar, *r), [box, box], [fine, fine, mid...]
    pallas_call x3, Pallas kernels: 13.5 us -> 5.86 us  [the longest x1 3.2 us: per_device(): call(lambda *r: send_kernel(nx, ny, *r), faces)]
    ppermute x4, starting transfers between devices: 13 us -> 9.03 us  [gathered(): out.append(lax.ppermute(sheet, 'boxes', p))]
    ppermute x2, starting transfers between devices: 0.01 us -> 3.86 us  [gathered(): lax.ppermute(lax.dynamic_slice_in_dim(sheet, at, count, axis=1), 'boxes', p)]
    unnamed x12, local copies, waits for them, and re-layouts: 2.65 us -> 6.08 us
    pallas_call x1, Pallas kernels: 22.1 us -> 18.8 us  [per_device(): call(lambda *r: down_kernel(nx, *r), [in_vmem(fine)] * 6 + [in_vmem(middl...]
    ppermute x4, waiting for transfers between devices: 0.01 us -> 2.95 us  [gathered(): out.append(lax.ppermute(sheet, 'boxes', p))]
    ppermute x2, waiting for transfers between devices: 1.98 us -> 0.1 us  [gathered(): sheet = jnp.stack([line] + [lax.ppermute(line, 'sub', p) for p in swap_y])]
  transfers between devices with their start and end apart: 18 -> 18, of which waited for: 5 -> 7; matrix products, arithmetic and copies ran while one was open for 1% -> 2% of each run, Pallas kernels for 24% -> 1%
where the time goes in v3:
time: 95 us; the launch traced here: 94.4 us
  Pallas kernels  40.7 us (43%)
  starting transfers between devices  29.1 us (31%)
  waiting for transfers between devices  15.5 us (16%)
  local copies, waits for them, and re-layouts  6.08 us (6%)
  other arithmetic  2.28 us (2%)
    pallas_call x1, Pallas kernels, per_device(): call(lambda *r: down_kernel(nx, *r), [in_vmem(fine)] * 6 + [in_vmem(middl...  18.8 us
    pallas_call x1, Pallas kernels, per_device(): call(lambda *r: up_kernel(nx, ny, nfar, *r), [box, box], [fine, fine, mid...  16 us
    ppermute x4, starting transfers between devices, gathered(): out.append(lax.ppermute(sheet, 'boxes', p))  9.03 us
    unnamed x12, local copies, waits for them, and re-layouts  6.08 us
    ppermute x2, starting transfers between devices, traded(): lax.ppermute(faces[nx + ny + e * ny + f], ('boxes', 'sub'), both(swap_x[e...  5.95 us
    ppermute x2, waiting for transfers between devices, traded(): lax.ppermute(faces[nx + ny + e * ny + f], ('boxes', 'sub'), both(swap_x[e...  4.84 us
    ppermute x2, waiting for transfers between devices, gathered(): lax.ppermute(lax.dynamic_slice_in_dim(sheet, at, count, axis=1), 'boxes', p)  4.65 us
    ppermute x2, starting transfers between devices, gathered(): lax.ppermute(lax.dynamic_slice_in_dim(sheet, at, count, axis=1), 'boxes', p)  3.86 us
  transfers between devices with their start and end apart: 18, of which 7 were waited for; matrix products, arithmetic and copies ran while one was open for 2% of the time, Pallas kernels for 1%

profile of v3, /device:TPU:0, one launch (start us, length us, event | category | flops | bytes accessed | tf_op | source)
XLA Modules:
  0.0 94.4 jit_solution(13346639994419670316)
XLA Ops:
  0.6 3.2 %shard_map.50 = (f32[14,64,128]{2,1,0:T(8,128)}, f32[14,64,128]{2,1,0:T(8,128)}, f32[2,32,16,128]{3,2,1,0:T(8,128)}, f32[11,16,128]{2,1,0:T(8,128)}, f32[11,16,128]{2,1,0:T(8,128)}) custom-call(f32[32,64,128]{2,1,0:T(8,128)} %phase, s32[32,64,128]{2,1,0:T(8,128)} %mask, f32[32,64,128]{2,1,0:T(8,128)} %dev), custom_call_target="tpu_custom_call" | custom-call | tf_op jit(solution)/shard_map/pallas_call | solution.py:564
  3.8 2.9 %collective-permute-start.2 = (f32[2,32,16,128]{3,2,1,0:T(8,128)}, f32[2,32,16,128]{3,2,1,0:T(8,128)S(1)}, u32[]{:S(2)}, u32[]{:S(2)}) collective-permute-start(f32[2,32,16,128]{3,2,1,0:T(8,128)} %get-tuple-element.44), channel_id=1, source_target_pairs={{0,2},{2,0},{1,3},{3,1},{4,6},{6,4},{5,7},{7,5},{8,10},{10,8},{9,1... | collective-permute-start | bytes 1572872 | tf_op jit(solution)/shard_map/ppermute | solution.py:538
  6.8 1.2 %copy-done = f32[32,64,128]{2,1,0:T(8,128)S(1)} copy-done((f32[32,64,128]{2,1,0:T(8,128)S(1)}, f32[32,64,128]{2,1,0:T(8,128)}, u32[]{:S(2)}) %copy-start) | copy-done | bytes 1048600
  8.0 1.2 %copy-done.1 = s32[32,64,128]{2,1,0:T(8,128)S(1)} copy-done((s32[32,64,128]{2,1,0:T(8,128)S(1)}, s32[32,64,128]{2,1,0:T(8,128)}, u32[]{:S(2)}) %copy-start.1) | copy-done | bytes 1048600
  9.2 1.2 %copy-done.2 = f32[32,64,128]{2,1,0:T(8,128)S(1)} copy-done((f32[32,64,128]{2,1,0:T(8,128)S(1)}, f32[32,64,128]{2,1,0:T(8,128)}, u32[]{:S(2)}) %copy-start.2) | copy-done | bytes 1048600
  10.4 0.9 shard_map.51
  12.0 1.6 %collective-permute-start = (f32[14,64,128]{2,1,0:T(8,128)}, f32[14,64,128]{2,1,0:T(8,128)S(1)}, u32[]{:S(2)}, u32[]{:S(2)}) collective-permute-start(f32[14,64,128]{2,1,0:T(8,128)} %get-tuple-element.42), channel_id=1, source_target_pairs={{0,4},{4,0},{8,12},{12,8},{1,5},{5,1},{9,13},{13,9},{2,6},{6,2},{1... | collective-permute-start | bytes 1376264 | tf_op jit(solution)/shard_map/ppermute | solution.py:536
  15.5 5.3 %collective-permute-start.3 = (f32[11,16,128]{2,1,0:T(8,128)}, f32[11,16,128]{2,1,0:T(8,128)}, u32[]{:S(2)}, u32[]{:S(2)}) collective-permute-start(f32[11,16,128]{2,1,0:T(8,128)} %get-tuple-element.45), channel_id=1, source_target_pairs={{0,6},{2,4},{4,2},{6,0},{8,14},{10,12},{12,10},{14,8},{1,7},{3,5},... | collective-permute-start | bytes 270344 | tf_op jit(solution)/shard_map/ppermute | solution.py:541
  22.2 4.8 %collective-permute-done.3.r_6_ = f32[11,16,128]{2,1,0:T(8,128)} collective-permute-done((f32[11,16,128]{2,1,0:T(8,128)}, f32[11,16,128]{2,1,0:T(8,128)}, u32[]{:S(2)}, u32[]{:S(2)}) %collective-permute-start.3) | collective-permute-done | bytes 90144 | tf_op jit(solution)/shard_map/ppermute | solution.py:541
  27.0 2.8 %collective-permute-start.9 = (f32[2,2,16,128]{3,2,1,0:T(8,128)S(1)}, f32[2,2,16,128]{3,2,1,0:T(8,128)S(1)}, u32[]{:S(2)}, u32[]{:S(2)}) collective-permute-start(f32[2,2,16,128]{3,2,1,0:T(8,128)S(1)} %fusion.1), channel_id=1, source_target_pairs={{0,8},{8,0},{4,12},{12,4},{1,9},{9,1},{5,13},{13,5},{2,10},{10,2},... | collective-permute-start | bytes 98312 | tf_op jit(solution)/shard_map/ppermute | solution.py:553
  29.8 0.9 pad_maximum_fusion.r_19_
  32.2 3.2 %collective-permute-start.7 = (f32[2,8,16,128]{3,2,1,0:T(8,128)S(1)}, f32[2,8,16,128]{3,2,1,0:T(8,128)S(1)}, u32[]{:S(2)}, u32[]{:S(2)}) collective-permute-start(f32[2,8,16,128]{3,2,1,0:T(8,128)S(1)} %pad_maximum_fusion.r_19_), channel_id=1, source_target_pairs={{0,4},{4,0},{8,12},{12,8},{1,5},{5,1},{9,13},{13,9},{2,6},{6,2},{1... | collective-permute-start | bytes 393224 | tf_op jit(solution)/shard_map/ppermute | solution.py:549
  35.4 2.9 %collective-permute-done.7.r_20_ = f32[2,8,16,128]{3,2,1,0:T(8,128)S(1)} collective-permute-done((f32[2,8,16,128]{3,2,1,0:T(8,128)S(1)}, f32[2,8,16,128]{3,2,1,0:T(8,128)S(1)}, u32[]{:S(2)}, u32[]{:S(2)}) %collective-permute-start.7) | collective-permute-done | bytes 131104 | tf_op jit(solution)/shard_map/ppermute | solution.py:549
  38.4 0.9 copy-done.4
  39.3 1.8 %shard_map.52 = (f32[48,80,128]{2,1,0:T(8,128)S(1)}, f32[48,80,128]{2,1,0:T(8,128)S(1)}, f32[12,80,128]{2,1,0:T(8,128)S(1)}) custom-call(f32[32,64,128]{2,1,0:T(8,128)S(1)} %get-tuple-element.50.r_0_, f32[32,64,128]{2,1,0:T(8,128)S(1)} %get-tuple-element.51.r_1_, f32[2,4,64,128]{3,2,1,0:T(8,128)S(1)} %copy-done.4, ...), custom_call_target="tpu_custom_call" | custom-call | tf_op jit(solution)/shard_map/pallas_call | solution.py:577
  41.2 1.9 %collective-permute-done.10.r_2_ = f32[12,80,128]{2,1,0:T(8,128)S(1)} collective-permute-done((f32[12,80,128]{2,1,0:T(8,128)S(1)}, f32[12,80,128]{2,1,0:T(8,128)S(1)}, u32[]{:S(2)}, u32[]{:S(2)}) %collective-permute-start.10) | collective-permute-done | bytes 491552 | tf_op jit(solution)/shard_map/ppermute | solution.py:582
  43.8 18.8 %shard_map.53 = (f32[48,80,256]{2,1,0:T(8,128)S(1)}, f32[48,80,256]{2,1,0:T(8,128)S(1)}, f32[48,80,256]{2,1,0:T(8,128)S(1)}, f32[48,80,256]{2,1,0:T(8,128)S(1)},...) custom-call(f32[48,80,128]{2,1,0:T(8,128)S(1)} %get-tuple-element.59, ...), custom_call_target="tpu_custom_call" | custom-call | tf_op jit(solution)/shard_map/pallas_call | solution.py:585
  62.8 1.1 %collective-permute-done.13 = f32[8,16,128]{2,1,0:T(8,128)S(1)} collective-permute-done((f32[8,16,128]{2,1,0:T(8,128)S(1)}, f32[8,16,128]{2,1,0:T(8,128)S(1)}, u32[]{:S(2)}, u32[]{:S(2)}) %collective-permute-start.13) | collective-permute-done | bytes 65568 | tf_op jit(solution)/shard_map/ppermute | solution.py:545
  64.0 1.6 %collective-permute-start.14 = (f32[8,16,128]{2,1,0:T(8,128)S(1)}, f32[8,16,128]{2,1,0:T(8,128)S(1)}, u32[]{:S(2)}, u32[]{:S(2)}) collective-permute-start(f32[8,16,128]{2,1,0:T(8,128)S(1)} %add.16), channel_id=1, source_target_pairs={{0,2},{2,0},{1,3},{3,1},{4,6},{6,4},{5,7},{7,5},{8,10},{10,8},{9,1... | collective-permute-start | bytes 196616 | tf_op jit(solution)/shard_map/ppermute | solution.py:546
  65.5 2.0 %collective-permute-start.11 = (f32[7,40,128]{2,1,0:T(8,128)S(1)}, f32[7,40,128]{2,1,0:T(8,128)S(1)}, u32[]{:S(2)}, u32[]{:S(2)}) collective-permute-start(f32[7,40,128]{2,1,0:T(8,128)S(1)} %get-tuple-element.75), channel_id=1, source_target_pairs={{0,4},{4,0},{8,12},{12,8},{1,5},{5,1},{9,13},{13,9},{2,6},{6,2},{1... | collective-permute-start | bytes 430088 | tf_op jit(solution)/shard_map/ppermute | solution.py:592
  69.0 4.5 %collective-permute-start.15 = (f32[2,8,16,128]{3,2,1,0:T(8,128)S(1)}, f32[2,8,16,128]{3,2,1,0:T(8,128)S(1)}, u32[]{:S(2)}, u32[]{:S(2)}) collective-permute-start(f32[2,8,16,128]{3,2,1,0:T(8,128)S(1)} %pad_maximum_fusion.1.r_15_), channel_id=1, source_target_pairs={{0,4},{4,0},{8,12},{12,8},{1,5},{5,1},{9,13},{13,9},{2,6},{6,2},{1... | collective-permute-start | bytes 393224 | tf_op jit(solution)/shard_map/ppermute | solution.py:549
  73.5 1.1 %collective-permute-start.17 = (f32[2,2,16,128]{3,2,1,0:T(8,128)S(1)}, f32[2,2,16,128]{3,2,1,0:T(8,128)S(1)}, u32[]{:S(2)}, u32[]{:S(2)}) collective-permute-start(f32[2,2,16,128]{3,2,1,0:T(8,128)S(1)} %fusion), channel_id=1, source_target_pairs={{0,8},{8,0},{4,12},{12,4},{1,9},{9,1},{5,13},{13,5},{2,10},{10,2},... | collective-permute-start | bytes 98312 | tf_op jit(solution)/shard_map/ppermute | solution.py:553
  74.6 3.8 %collective-permute-done.17.r_18_ = f32[2,2,16,128]{3,2,1,0:T(8,128)S(1)} collective-permute-done((f32[2,2,16,128]{3,2,1,0:T(8,128)S(1)}, f32[2,2,16,128]{3,2,1,0:T(8,128)S(1)}, u32[]{:S(2)}, u32[]{:S(2)}) %collective-permute-start.17) | collective-permute-done | bytes 32800 | tf_op jit(solution)/shard_map/ppermute | solution.py:553
  78.4 16.0 %shard_map.54 = (f32[32,64,128]{2,1,0:T(8,128)}, f32[32,64,128]{2,1,0:T(8,128)}) custom-call(f32[48,80,256]{2,1,0:T(8,128)S(1)} %get-tuple-element.62.r_0_, f32[48,80,256]{2,1,0:T(8,128)S(1)} %get-tuple-element.63.r_1_, f32[48,80,256]{2,1,0:T(8,128)S(1)} %get-tuple-element.64.r_2_, f32[48,80,256]{2,1,0:T(8,128)S(1)} %get-tuple-element.65.r_3_, ...), custom_call_target="tpu_custom_call" | custom-call | tf_op jit(solution)/shard_map/pallas_call | solution.py:595
  (35 shorter events, 8.0 us)
Async XLA Ops:
  3.8 34.5 %collective-permute-start.2 = (f32[2,32,16,128]{3,2,1,0:T(8,128)}, f32[2,32,16,128]{3,2,1,0:T(8,128)S(1)}, u32[]{:S(2)}, u32[]{:S(2)}) collective-permute-start(f32[2,32,16,128]{3,2,1,0:T(8,128)} %get-tuple-element.44), channel_id=1, source_target_pairs={{0,2},{2,0},{1,3},{3,1},{4,6},{6,4},{5,7},{7,5},{8,10},{10,8},{9,1... | collective-permute-start | bytes 1572872 | tf_op jit(solution)/shard_map/ppermute | solution.py:538
  6.8 1.2 %copy-start = (f32[32,64,128]{2,1,0:T(8,128)S(1)}, f32[32,64,128]{2,1,0:T(8,128)}, u32[]{:S(2)}) copy-start(f32[32,64,128]{2,1,0:T(8,128)} %phase) | copy-start | bytes 3145732
  8.0 1.2 %copy-start.1 = (s32[32,64,128]{2,1,0:T(8,128)S(1)}, s32[32,64,128]{2,1,0:T(8,128)}, u32[]{:S(2)}) copy-start(s32[32,64,128]{2,1,0:T(8,128)} %mask) | copy-start | bytes 3145732
  9.2 1.2 %copy-start.2 = (f32[32,64,128]{2,1,0:T(8,128)S(1)}, f32[32,64,128]{2,1,0:T(8,128)}, u32[]{:S(2)}) copy-start(f32[32,64,128]{2,1,0:T(8,128)} %dev) | copy-start | bytes 3145732
  11.3 0.7 copy-start.3
  12.0 2.3 %collective-permute-start.5 = (f32[8,16,128]{2,1,0:T(8,128)S(1)}, f32[8,16,128]{2,1,0:T(8,128)S(1)}, u32[]{:S(2)}, u32[]{:S(2)}) collective-permute-start(f32[8,16,128]{2,1,0:T(8,128)S(1)} %get-tuple-element.53), channel_id=1, source_target_pairs={{0,1},{1,0},{2,3},{3,2},{4,5},{5,4},{6,7},{7,6},{8,9},{9,8},{10,11... | collective-permute-start | bytes 196616 | tf_op jit(solution)/shard_map/ppermute | solution.py:545
  12.0 26.3 %collective-permute-start = (f32[14,64,128]{2,1,0:T(8,128)}, f32[14,64,128]{2,1,0:T(8,128)S(1)}, u32[]{:S(2)}, u32[]{:S(2)}) collective-permute-start(f32[14,64,128]{2,1,0:T(8,128)} %get-tuple-element.42), channel_id=1, source_target_pairs={{0,4},{4,0},{8,12},{12,8},{1,5},{5,1},{9,13},{13,9},{2,6},{6,2},{1... | collective-permute-start | bytes 1376264 | tf_op jit(solution)/shard_map/ppermute | solution.py:536
  13.6 24.7 %collective-permute-start.1 = (f32[14,64,128]{2,1,0:T(8,128)}, f32[14,64,128]{2,1,0:T(8,128)S(1)}, u32[]{:S(2)}, u32[]{:S(2)}) collective-permute-start(f32[14,64,128]{2,1,0:T(8,128)} %get-tuple-element.43), channel_id=1, source_target_pairs={{4,8},{8,4},{5,9},{9,5},{6,10},{10,6},{7,11},{11,7},{20,24},{24,20... | collective-permute-start | bytes 1376264 | tf_op jit(solution)/shard_map/ppermute | solution.py:536
  14.9 5.8 %collective-permute-start.6 = (f32[8,16,128]{2,1,0:T(8,128)}, f32[8,16,128]{2,1,0:T(8,128)}, u32[]{:S(2)}, u32[]{:S(2)}) collective-permute-start(f32[8,16,128]{2,1,0:T(8,128)} %add.14), channel_id=1, source_target_pairs={{0,2},{2,0},{1,3},{3,1},{4,6},{6,4},{5,7},{7,5},{8,10},{10,8},{9,1... | collective-permute-start | bytes 196616 | tf_op jit(solution)/shard_map/ppermute | solution.py:546
  15.5 11.5 %collective-permute-start.3 = (f32[11,16,128]{2,1,0:T(8,128)}, f32[11,16,128]{2,1,0:T(8,128)}, u32[]{:S(2)}, u32[]{:S(2)}) collective-permute-start(f32[11,16,128]{2,1,0:T(8,128)} %get-tuple-element.45), channel_id=1, source_target_pairs={{0,6},{2,4},{4,2},{6,0},{8,14},{10,12},{12,10},{14,8},{1,7},{3,5},... | collective-permute-start | bytes 270344 | tf_op jit(solution)/shard_map/ppermute | solution.py:541
  20.8 9.9 %collective-permute-start.4 = (f32[11,16,128]{2,1,0:T(8,128)}, f32[11,16,128]{2,1,0:T(8,128)S(1)}, u32[]{:S(2)}, u32[]{:S(2)}) collective-permute-start(f32[11,16,128]{2,1,0:T(8,128)} %get-tuple-element.46), channel_id=1, source_target_pairs={{4,10},{6,8},{8,6},{10,4},{5,11},{7,9},{9,7},{11,5},{20,26},{22,24... | collective-permute-start | bytes 270344 | tf_op jit(solution)/shard_map/ppermute | solution.py:541
  27.0 5.2 %collective-permute-start.9 = (f32[2,2,16,128]{3,2,1,0:T(8,128)S(1)}, f32[2,2,16,128]{3,2,1,0:T(8,128)S(1)}, u32[]{:S(2)}, u32[]{:S(2)}) collective-permute-start(f32[2,2,16,128]{3,2,1,0:T(8,128)S(1)} %fusion.1), channel_id=1, source_target_pairs={{0,8},{8,0},{4,12},{12,4},{1,9},{9,1},{5,13},{13,5},{2,10},{10,2},... | collective-permute-start | bytes 98312 | tf_op jit(solution)/shard_map/ppermute | solution.py:553
  30.7 4.7 %collective-permute-start.8 = (f32[2,8,16,128]{3,2,1,0:T(8,128)S(1)}, f32[2,8,16,128]{3,2,1,0:T(8,128)S(1)}, u32[]{:S(2)}, u32[]{:S(2)}) collective-permute-start(f32[2,8,16,128]{3,2,1,0:T(8,128)S(1)} %pad_maximum_fusion.r_19_), channel_id=1, source_target_pairs={{4,8},{8,4},{5,9},{9,5},{6,10},{10,6},{7,11},{11,7},{20,24},{24,20... | collective-permute-start | bytes 393224 | tf_op jit(solution)/shard_map/ppermute | solution.py:549
  32.2 6.1 %collective-permute-start.7 = (f32[2,8,16,128]{3,2,1,0:T(8,128)S(1)}, f32[2,8,16,128]{3,2,1,0:T(8,128)S(1)}, u32[]{:S(2)}, u32[]{:S(2)}) collective-permute-start(f32[2,8,16,128]{3,2,1,0:T(8,128)S(1)} %pad_maximum_fusion.r_19_), channel_id=1, source_target_pairs={{0,4},{4,0},{8,12},{12,8},{1,5},{5,1},{9,13},{13,9},{2,6},{6,2},{1... | collective-permute-start | bytes 393224 | tf_op jit(solution)/shard_map/ppermute | solution.py:549
  38.3 1.0 %copy-start.4 = (f32[2,4,64,128]{3,2,1,0:T(8,128)S(1)}, f32[2,4,64,128]{3,2,1,0:T(8,128)}, u32[]{:S(2)}) copy-start(f32[2,4,64,128]{3,2,1,0:T(8,128)} %copy-done.3) | copy-start | bytes 786436
  41.1 1.9 %collective-permute-start.10 = (f32[12,80,128]{2,1,0:T(8,128)S(1)}, f32[12,80,128]{2,1,0:T(8,128)S(1)}, u32[]{:S(2)}, u32[]{:S(2)}) collective-permute-start(f32[12,80,128]{2,1,0:T(8,128)S(1)} %get-tuple-element.61), channel_id=1, source_target_pairs={{0,1},{1,0},{2,3},{3,2},{4,5},{5,4},{6,7},{7,6},{8,9},{9,8},{10,11... | collective-permute-start | bytes 1474568 | tf_op jit(solution)/shard_map/ppermute | solution.py:582
  43.0 0.8 copy-start.5
  62.6 1.3 %collective-permute-start.13 = (f32[8,16,128]{2,1,0:T(8,128)S(1)}, f32[8,16,128]{2,1,0:T(8,128)S(1)}, u32[]{:S(2)}, u32[]{:S(2)}) collective-permute-start(f32[8,16,128]{2,1,0:T(8,128)S(1)} %get-tuple-element.77), channel_id=1, source_target_pairs={{0,1},{1,0},{2,3},{3,2},{4,5},{5,4},{6,7},{7,6},{8,9},{9,8},{10,11... | collective-permute-start | bytes 196616 | tf_op jit(solution)/shard_map/ppermute | solution.py:545
  64.0 4.3 %collective-permute-start.14 = (f32[8,16,128]{2,1,0:T(8,128)S(1)}, f32[8,16,128]{2,1,0:T(8,128)S(1)}, u32[]{:S(2)}, u32[]{:S(2)}) collective-permute-start(f32[8,16,128]{2,1,0:T(8,128)S(1)} %add.16), channel_id=1, source_target_pairs={{0,2},{2,0},{1,3},{3,1},{4,6},{6,4},{5,7},{7,5},{8,10},{10,8},{9,1... | collective-permute-start | bytes 196616 | tf_op jit(solution)/shard_map/ppermute | solution.py:546
  65.5 9.1 %collective-permute-start.11 = (f32[7,40,128]{2,1,0:T(8,128)S(1)}, f32[7,40,128]{2,1,0:T(8,128)S(1)}, u32[]{:S(2)}, u32[]{:S(2)}) collective-permute-start(f32[7,40,128]{2,1,0:T(8,128)S(1)} %get-tuple-element.75), channel_id=1, source_target_pairs={{0,4},{4,0},{8,12},{12,8},{1,5},{5,1},{9,13},{13,9},{2,6},{6,2},{1... | collective-permute-start | bytes 430088 | tf_op jit(solution)/shard_map/ppermute | solution.py:592
  67.5 7.1 %collective-permute-start.12 = (f32[7,40,128]{2,1,0:T(8,128)S(1)}, f32[7,40,128]{2,1,0:T(8,128)S(1)}, u32[]{:S(2)}, u32[]{:S(2)}) collective-permute-start(f32[7,40,128]{2,1,0:T(8,128)S(1)} %get-tuple-element.76), channel_id=1, source_target_pairs={{4,8},{8,4},{5,9},{9,5},{6,10},{10,6},{7,11},{11,7},{20,24},{24,20... | collective-permute-start | bytes 430088 | tf_op jit(solution)/shard_map/ppermute | solution.py:592
  68.3 10.1 %collective-permute-start.16 = (f32[2,8,16,128]{3,2,1,0:T(8,128)S(1)}, f32[2,8,16,128]{3,2,1,0:T(8,128)S(1)}, u32[]{:S(2)}, u32[]{:S(2)}) collective-permute-start(f32[2,8,16,128]{3,2,1,0:T(8,128)S(1)} %pad_maximum_fusion.1.r_15_), channel_id=1, source_target_pairs={{4,8},{8,4},{5,9},{9,5},{6,10},{10,6},{7,11},{11,7},{20,24},{24,20... | collective-permute-start | bytes 393224 | tf_op jit(solution)/shard_map/ppermute | solution.py:549
  69.0 9.4 %collective-permute-start.15 = (f32[2,8,16,128]{3,2,1,0:T(8,128)S(1)}, f32[2,8,16,128]{3,2,1,0:T(8,128)S(1)}, u32[]{:S(2)}, u32[]{:S(2)}) collective-permute-start(f32[2,8,16,128]{3,2,1,0:T(8,128)S(1)} %pad_maximum_fusion.1.r_15_), channel_id=1, source_target_pairs={{0,4},{4,0},{8,12},{12,8},{1,5},{5,1},{9,13},{13,9},{2,6},{6,2},{1... | collective-permute-start | bytes 393224 | tf_op jit(solution)/shard_map/ppermute | solution.py:549
  73.5 4.9 %collective-permute-start.17 = (f32[2,2,16,128]{3,2,1,0:T(8,128)S(1)}, f32[2,2,16,128]{3,2,1,0:T(8,128)S(1)}, u32[]{:S(2)}, u32[]{:S(2)}) collective-permute-start(f32[2,2,16,128]{3,2,1,0:T(8,128)S(1)} %fusion), channel_id=1, source_target_pairs={{0,8},{8,0},{4,12},{12,4},{1,9},{9,1},{5,13},{13,5},{2,10},{10,2},... | collective-permute-start | bytes 98312 | tf_op jit(solution)/shard_map/ppermute | solution.py:553

commit v4 on v3

--- a/solution.py
+++ b/solution.py
@@ -218,7 +218,7 @@
     loop(0, ox, body, unroll=4)
     quarter = oz // 4
     i, j = iota2((oz, oz), 0), iota2((oz, oz), 1)
-    matrix = thrice(jnp.where(j == pz * quarter + lax.div(i, 4), 1.0 / 64.0, 0.0))
+    matrix = thrice(jnp.where(j == oz // 2 + pz * quarter + lax.div(i, 4), 1.0 / 64.0, 0.0))
     for x in range(ox // 4):
         sums[...] = (c[4 * x] + c[4 * x + 1]) + (c[4 * x + 2] + c[4 * x + 3])
         part = [sums[pl.ds(k, oy // 4, stride=4), :] for k in range(4)]
@@ -330,7 +330,7 @@
     return thrice(jnp.where((i < limit) & (j == shift + lax.div(i, 2)), weight, 0.0))
 
 
-def down_kernel(nx, cpad, gpad, strip, *refs):
+def down_kernel(nx, cpad, gpad, strip, c2, *refs):
     kx, ky, kz, rd, g, u0, kx1, ky1, kz1, rd1, c1, f1, u1, f2 = refs[:14]
     faces = refs[14:14 + nx]
     c, first, v1, work, work1 = refs[14 + nx:]
@@ -394,6 +394,7 @@
     matrix1 = pool_matrix(oz, oz, half, jnp.where(pz == 0, 0, half // 2), 0.125)
     own1 = 2 * f2.shape[1]
     pool(lambda x: v1[x, 0:own1, :], h1 // 2, (planes1 - h1) // 2, f2, matrix1, work1, f2.shape[0])
+    f2[...] = f2[...] + c2[...]
     for e in range(nx):
         up = upward(bx, e)
         faces[e][0:h1] = u1[pl.ds(jnp.where(up, o1, h1), h1)]
@@ -406,9 +407,7 @@
     faces = refs[at:at + nx]
     at += nx
     pieces = 1 + nx + nfar
-    got_f = refs[at:at + pieces]
-    at += pieces
-    got_c = refs[at:at + pieces]
+    got = refs[at:at + pieces]
     at += pieces
     field, residual = refs[at:at + 2]
     at += 2
@@ -424,22 +423,22 @@
 
     c2[...] = jnp.zeros_like(c2)
     f2[...] = jnp.zeros_like(f2)
-    for out, got in ((c2, got_c), (f2, got_f)):
-        places = [(L2X, o2x)]
-        for e in range(nx):
-            places.append((jnp.where(upward(bx, e), L2X + o2x, L2X - o2x), o2x))
-        for e in range(nfar):
-            places.append((jnp.where(upward(bx, e, 2), L2X + 2 * o2x, 0), L2X - o2x))
-        for (x0, count), piece in zip(places, got):
-            for f in range(ny + 1):
-                if f == 0:
-                    y0 = 0
-                elif ny == 1:
-                    y0 = pl.multiple_of(jnp.where(upward(sy, 0), o2y, rows2 - o2y), 8)
-                else:
-                    y0 = pl.multiple_of(jnp.where(upward(sy, f - 1), o2y, rows2 - o2y), 8)
-                for x in range(count):
-                    out[x0 + x, pl.ds(y0, o2y), :] = piece[f, x]
+    lower = iota2((o2y, oz), 1) < oz // 2
+    places = [(L2X, o2x)]
+    for e in range(nx):
+        places.append((jnp.where(upward(bx, e), L2X + o2x, L2X - o2x), o2x))
+    for e in range(nfar):
+        places.append((jnp.where(upward(bx, e, 2), L2X + 2 * o2x, 0), L2X - o2x))
+    for (x0, count), piece in zip(places, got):
+        for f in range(ny + 1):
+            if f == 0:
+                y0 = 0
+            else:
+                y0 = pl.multiple_of(jnp.where(upward(sy, f - 1), o2y, rows2 - o2y), 8)
+            for x in range(count):
+                values = piece[f, x]
+                f2[x0 + x, pl.ds(y0, o2y), :] = jnp.where(lower, values, 0.0)
+                c2[x0 + x, pl.ds(y0, o2y), :] = jnp.where(lower, pltpu.roll(values, oz // 2, 1), 0.0)
     coefficients(c2, kx2, ky2, kz2, rd2, 1, planes2 - 1, 0.0625)
 
     def start_sweep2(x):
@@ -571,8 +570,6 @@
         [(oy, oz), (o2x, o2y, oz)],
         mib=24,
     )(phase, target_mask, deviation)
-    got_c = gathered(c2)
-    got, got_c = lax.optimization_barrier((got, got_c))
     padded = (planes, rows, oz)
     cpad, gpad, strip = call(
         lambda *r: extend_kernel(nx, ny, *r),
@@ -587,17 +584,17 @@
         [in_vmem(fine)] * 6 + [in_vmem(middle)] * 7 + [spec((o2x, o2y, oz))] + [spec((XH - 1, rows1, oz))] * nx,
         [fine, fine, middle, (8, rows, oz), (o2x, oy // 2, oz)],
         mib=24,
-    )(held(cpad), held(gpad), strip)
+    )(held(cpad), held(gpad), strip, c2)
     kept, f2, sides = down[:13], down[13], down[14:]
     sides = [lax.ppermute(s, "boxes", p) for s, p in zip(sides, swap_x)]
-    got_f = gathered(f2)
+    got = gathered(f2)
     lowest = (planes2, rows2, oz)
     return tuple(call(
         lambda *r: up_kernel(nx, ny, nfar, *r),
         [box, box],
         [fine, fine, middle, middle, middle] + [lowest] * 8 + [(planes1 // 2, 2 * (o2y + 8), oz), (8, rows, oz)],
         mib=24,
-    )(*[held(x) for x in kept], *sides, *got_f, *got_c))
+    )(*[held(x) for x in kept], *sides, *got))
 
 
 def solution(mesh):

time: 95 us -> 105 us (1.11)
  local copies, waits for them, and re-layouts: 6.08 us -> 29.1 us
  waiting for transfers between devices: 15.5 us -> 8.4 us
  starting transfers between devices: 29.1 us -> 23.7 us
    unnamed x12 -> x36, local copies, waits for them, and re-layouts: 6.08 us -> 29.1 us
    ppermute x4 -> x2, starting transfers between devices: 9.03 us -> 3.69 us  [gathered(): out.append(lax.ppermute(sheet, 'boxes', p))]
    ppermute x4 -> x2, waiting for transfers between devices: 2.95 us -> 0.01 us  [gathered(): out.append(lax.ppermute(sheet, 'boxes', p))]
    ppermute x2, waiting for transfers between devices: 4.84 us -> 2.14 us  [traded(): lax.ppermute(faces[nx + ny + e * ny + f], ('boxes', 'sub'), both(swap_x[e...]
    ppermute x2, starting transfers between devices: 2.67 us -> 5.06 us  [per_device(): sides = [lax.ppermute(s, 'boxes', p) for s, p in zip(sides, swap_x)]]
    ppermute x2 -> x1, waiting for transfers between devices: 4.65 us -> 3.27 us  [gathered(): lax.ppermute(lax.dynamic_slice_in_dim(sheet, at, count, axis=1), 'boxes', p)]
    pallas_call x1, Pallas kernels: 16 us -> 17.2 us  [per_device(): call(lambda *r: up_kernel(nx, ny, nfar, *r), [box, box], [fine, fine, mid...]
    ppermute x2 -> x1, starting transfers between devices: 3.86 us -> 2.73 us  [gathered(): lax.ppermute(lax.dynamic_slice_in_dim(sheet, at, count, axis=1), 'boxes', p)]
  transfers between devices with their start and end apart: 18 -> 13, of which waited for: 7 -> 4; matrix products, arithmetic and copies ran while one was open for 2% -> 2% of each run, Pallas kernels for 1% -> 1%
where the time goes in v4:
time: 105 us
  Pallas kernels  41 us (39%)
  local copies, waits for them, and re-layouts  29.1 us (28%)
  starting transfers between devices  23.7 us (23%)
  waiting for transfers between devices  8.4 us (8%)
  other arithmetic  1.59 us (2%)
    unnamed x36, local copies, waits for them, and re-layouts  29.1 us
    pallas_call x1, Pallas kernels, per_device(): call(lambda *r: down_kernel(nx, *r), [in_vmem(fine)] * 6 + [in_vmem(middl...  18.8 us
    pallas_call x1, Pallas kernels, per_device(): call(lambda *r: up_kernel(nx, ny, nfar, *r), [box, box], [fine, fine, mid...  17.2 us
    ppermute x2, starting transfers between devices, traded(): lax.ppermute(faces[nx + ny + e * ny + f], ('boxes', 'sub'), both(swap_x[e...  5.06 us
    ppermute x2, starting transfers between devices, per_device(): sides = [lax.ppermute(s, 'boxes', p) for s, p in zip(sides, swap_x)]  5.06 us
    ppermute x2, starting transfers between devices, gathered(): out.append(lax.ppermute(sheet, 'boxes', p))  3.69 us
    ppermute x1, waiting for transfers between devices, gathered(): lax.ppermute(lax.dynamic_slice_in_dim(sheet, at, count, axis=1), 'boxes', p)  3.27 us
    pallas_call x1, Pallas kernels, per_device(): call(lambda *r: send_kernel(nx, ny, *r), faces)  3.19 us
  transfers between devices with their start and end apart: 13, of which 4 were waited for; matrix products, arithmetic and copies ran while one was open for 2% of the time, Pallas kernels for 1%

profile of v4, /device:TPU:0, one launch (start us, length us, event | category | flops | bytes accessed | tf_op | source)
XLA Modules:
  0.0 104.7 jit_solution(4908117827723223094)
XLA Ops:
  0.6 3.2 %shard_map.50 = (f32[14,64,128]{2,1,0:T(8,128)}, f32[14,64,128]{2,1,0:T(8,128)}, f32[2,32,16,128]{3,2,1,0:T(8,128)}, f32[11,16,128]{2,1,0:T(8,128)}, f32[11,16,128]{2,1,0:T(8,128)}) custom-call(f32[32,64,128]{2,1,0:T(8,128)} %phase, s32[32,64,128]{2,1,0:T(8,128)} %mask, f32[32,64,128]{2,1,0:T(8,128)} %dev), custom_call_target="tpu_custom_call" | custom-call | tf_op jit(solution)/shard_map/pallas_call | solution.py:563
  3.8 2.9 %collective-permute-start.2 = (f32[2,32,16,128]{3,2,1,0:T(8,128)}, f32[2,32,16,128]{3,2,1,0:T(8,128)S(1)}, u32[]{:S(2)}, u32[]{:S(2)}) collective-permute-start(f32[2,32,16,128]{3,2,1,0:T(8,128)} %get-tuple-element.35), channel_id=1, source_target_pairs={{0,2},{2,0},{1,3},{3,1},{4,6},{6,4},{5,7},{7,5},{8,10},{10,8},{9,1... | collective-permute-start | bytes 1572872 | tf_op jit(solution)/shard_map/ppermute | solution.py:537
  9.0 4.4 %collective-permute-start.3 = (f32[11,16,128]{2,1,0:T(8,128)}, f32[11,16,128]{2,1,0:T(8,128)S(1)}, u32[]{:S(2)}, u32[]{:S(2)}) collective-permute-start(f32[11,16,128]{2,1,0:T(8,128)} %get-tuple-element.36), channel_id=1, source_target_pairs={{0,6},{2,4},{4,2},{6,0},{8,14},{10,12},{12,10},{14,8},{1,7},{3,5},... | collective-permute-start | bytes 270344 | tf_op jit(solution)/shard_map/ppermute | solution.py:540
  18.7 2.1 %collective-permute-done.3.r_6_ = f32[11,16,128]{2,1,0:T(8,128)S(1)} collective-permute-done((f32[11,16,128]{2,1,0:T(8,128)}, f32[11,16,128]{2,1,0:T(8,128)S(1)}, u32[]{:S(2)}, u32[]{:S(2)}) %collective-permute-start.3) | collective-permute-done | bytes 90144 | tf_op jit(solution)/shard_map/ppermute | solution.py:540
  21.8 1.9 %collective-permute-done.5.r_2_ = f32[12,80,128]{2,1,0:T(8,128)S(1)} collective-permute-done((f32[12,80,128]{2,1,0:T(8,128)S(1)}, f32[12,80,128]{2,1,0:T(8,128)S(1)}, u32[]{:S(2)}, u32[]{:S(2)}) %collective-permute-start.5) | collective-permute-done | bytes 491552 | tf_op jit(solution)/shard_map/ppermute | solution.py:579
  24.4 18.8 %shard_map.53 = (f32[48,80,256]{2,1,0:T(8,128)S(1)}, f32[48,80,256]{2,1,0:T(8,128)S(1)}, f32[48,80,256]{2,1,0:T(8,128)S(1)}, f32[48,80,256]{2,1,0:T(8,128)S(1)},...) custom-call(f32[48,80,128]{2,1,0:T(8,128)S(1)} %get-tuple-element.44, ...), custom_call_target="tpu_custom_call" | custom-call | tf_op jit(solution)/shard_map/pallas_call | solution.py:582
  43.3 1.9 %copy-done.3 = f32[48,80,256]{2,1,0:T(8,128)} copy-done((f32[48,80,256]{2,1,0:T(8,128)}, f32[48,80,256]{2,1,0:T(8,128)S(1)}, u32[]{:S(2)}) %copy-start.3) | copy-done | bytes 3932184
  45.2 1.9 %copy-done.5 = f32[48,80,256]{2,1,0:T(8,128)} copy-done((f32[48,80,256]{2,1,0:T(8,128)}, f32[48,80,256]{2,1,0:T(8,128)S(1)}, u32[]{:S(2)}) %copy-start.5) | copy-done | bytes 3932184
  47.1 1.9 %copy-done.7 = f32[48,80,256]{2,1,0:T(8,128)} copy-done((f32[48,80,256]{2,1,0:T(8,128)}, f32[48,80,256]{2,1,0:T(8,128)S(1)}, u32[]{:S(2)}) %copy-start.7) | copy-done | bytes 3932184
  49.0 1.9 %copy-done.9 = f32[48,80,256]{2,1,0:T(8,128)} copy-done((f32[48,80,256]{2,1,0:T(8,128)}, f32[48,80,256]{2,1,0:T(8,128)S(1)}, u32[]{:S(2)}) %copy-start.9) | copy-done | bytes 3932184
  50.8 1.9 %copy-done.11 = f32[48,80,256]{2,1,0:T(8,128)} copy-done((f32[48,80,256]{2,1,0:T(8,128)}, f32[48,80,256]{2,1,0:T(8,128)S(1)}, u32[]{:S(2)}) %copy-start.11) | copy-done | bytes 3932184
  52.7 1.9 %copy-done.13 = f32[48,80,256]{2,1,0:T(8,128)} copy-done((f32[48,80,256]{2,1,0:T(8,128)}, f32[48,80,256]{2,1,0:T(8,128)S(1)}, u32[]{:S(2)}) %copy-start.13) | copy-done | bytes 3932184
  56.6 1.8 %collective-permute-start.9 = (f32[8,16,128]{2,1,0:T(8,128)S(1)}, f32[8,16,128]{2,1,0:T(8,128)}, u32[]{:S(2)}, u32[]{:S(2)}) collective-permute-start(f32[8,16,128]{2,1,0:T(8,128)S(1)} %add.9), channel_id=1, source_target_pairs={{0,2},{2,0},{1,3},{3,1},{4,6},{6,4},{5,7},{7,5},{8,10},{10,8},{9,1... | collective-permute-start | bytes 196616 | tf_op jit(solution)/shard_map/ppermute | solution.py:545
  58.4 4.4 %collective-permute-start.6 = (f32[7,40,128]{2,1,0:T(8,128)}, f32[7,40,128]{2,1,0:T(8,128)S(1)}, u32[]{:S(2)}, u32[]{:S(2)}) collective-permute-start(f32[7,40,128]{2,1,0:T(8,128)} %copy-done.16), channel_id=1, source_target_pairs={{0,4},{4,0},{8,12},{12,8},{1,5},{5,1},{9,13},{13,9},{2,6},{6,2},{1... | collective-permute-start | bytes 430088 | tf_op jit(solution)/shard_map/ppermute | solution.py:589
  64.3 3.0 %collective-permute-start.10 = (f32[2,8,16,128]{3,2,1,0:T(8,128)S(1)}, f32[2,8,16,128]{3,2,1,0:T(8,128)S(1)}, u32[]{:S(2)}, u32[]{:S(2)}) collective-permute-start(f32[2,8,16,128]{3,2,1,0:T(8,128)S(1)} %pad_maximum_fusion.r_15_), channel_id=1, source_target_pairs={{0,4},{4,0},{8,12},{12,8},{1,5},{5,1},{9,13},{13,9},{2,6},{6,2},{1... | collective-permute-start | bytes 393224 | tf_op jit(solution)/shard_map/ppermute | solution.py:548
  68.7 2.7 %collective-permute-start.12 = (f32[2,2,16,128]{3,2,1,0:T(8,128)S(1)}, f32[2,2,16,128]{3,2,1,0:T(8,128)S(1)}, u32[]{:S(2)}, u32[]{:S(2)}) collective-permute-start(f32[2,2,16,128]{3,2,1,0:T(8,128)S(1)} %fusion), channel_id=1, source_target_pairs={{0,8},{8,0},{4,12},{12,4},{1,9},{9,1},{5,13},{13,5},{2,10},{10,2},... | collective-permute-start | bytes 98312 | tf_op jit(solution)/shard_map/ppermute | solution.py:552
  71.5 3.3 %collective-permute-done.12.r_18_ = f32[2,2,16,128]{3,2,1,0:T(8,128)S(1)} collective-permute-done((f32[2,2,16,128]{3,2,1,0:T(8,128)S(1)}, f32[2,2,16,128]{3,2,1,0:T(8,128)S(1)}, u32[]{:S(2)}, u32[]{:S(2)}) %collective-permute-start.12) | collective-permute-done | bytes 32800 | tf_op jit(solution)/shard_map/ppermute | solution.py:552
  74.7 2.1 %copy-done.4 = f32[48,80,256]{2,1,0:T(8,128)S(1)} copy-done((f32[48,80,256]{2,1,0:T(8,128)S(1)}, f32[48,80,256]{2,1,0:T(8,128)}, u32[]{:S(2)}) %copy-start.4) | copy-done | bytes 3932184
  76.8 2.1 %copy-done.6 = f32[48,80,256]{2,1,0:T(8,128)S(1)} copy-done((f32[48,80,256]{2,1,0:T(8,128)S(1)}, f32[48,80,256]{2,1,0:T(8,128)}, u32[]{:S(2)}) %copy-start.6) | copy-done | bytes 3932184
  79.0 2.1 %copy-done.8 = f32[48,80,256]{2,1,0:T(8,128)S(1)} copy-done((f32[48,80,256]{2,1,0:T(8,128)S(1)}, f32[48,80,256]{2,1,0:T(8,128)}, u32[]{:S(2)}) %copy-start.8) | copy-done | bytes 3932184
  81.1 2.1 %copy-done.10 = f32[48,80,256]{2,1,0:T(8,128)S(1)} copy-done((f32[48,80,256]{2,1,0:T(8,128)S(1)}, f32[48,80,256]{2,1,0:T(8,128)}, u32[]{:S(2)}) %copy-start.10) | copy-done | bytes 3932184
  83.2 2.1 %copy-done.12 = f32[48,80,256]{2,1,0:T(8,128)S(1)} copy-done((f32[48,80,256]{2,1,0:T(8,128)S(1)}, f32[48,80,256]{2,1,0:T(8,128)}, u32[]{:S(2)}) %copy-start.12) | copy-done | bytes 3932184
  85.3 2.1 %copy-done.14 = f32[48,80,256]{2,1,0:T(8,128)S(1)} copy-done((f32[48,80,256]{2,1,0:T(8,128)S(1)}, f32[48,80,256]{2,1,0:T(8,128)}, u32[]{:S(2)}) %copy-start.14) | copy-done | bytes 3932184
  87.4 17.2 %shard_map.54 = (f32[32,64,128]{2,1,0:T(8,128)}, f32[32,64,128]{2,1,0:T(8,128)}) custom-call(f32[48,80,256]{2,1,0:T(8,128)S(1)} %copy-done.4, f32[48,80,256]{2,1,0:T(8,128)S(1)} %copy-done.6, f32[48,80,256]{2,1,0:T(8,128)S(1)} %copy-done.8, f32[48,80,256]{2,1,0:T(8,128)S(1)} %copy-done.10, f32[48,80,256]{2,1,0:T(8,128)S(1)} %copy-done.12, ...), custom_call_target="tpu_custom_call" | custom-call | tf_op jit(solution)/shard_map/pallas_call | solution.py:592
  (46 shorter events, 14.1 us)
Async XLA Ops:
  3.8 17.0 %collective-permute-start.2 = (f32[2,32,16,128]{3,2,1,0:T(8,128)}, f32[2,32,16,128]{3,2,1,0:T(8,128)S(1)}, u32[]{:S(2)}, u32[]{:S(2)}) collective-permute-start(f32[2,32,16,128]{3,2,1,0:T(8,128)} %get-tuple-element.35), channel_id=1, source_target_pairs={{0,2},{2,0},{1,3},{3,1},{4,6},{6,4},{5,7},{7,5},{8,10},{10,8},{9,1... | collective-permute-start | bytes 1572872 | tf_op jit(solution)/shard_map/ppermute | solution.py:537
  6.8 14.0 %collective-permute-start = (f32[14,64,128]{2,1,0:T(8,128)}, f32[14,64,128]{2,1,0:T(8,128)S(1)}, u32[]{:S(2)}, u32[]{:S(2)}) collective-permute-start(f32[14,64,128]{2,1,0:T(8,128)} %get-tuple-element.33), channel_id=1, source_target_pairs={{0,4},{4,0},{8,12},{12,8},{1,5},{5,1},{9,13},{13,9},{2,6},{6,2},{1... | collective-permute-start | bytes 1376264 | tf_op jit(solution)/shard_map/ppermute | solution.py:535
  8.3 12.5 %collective-permute-start.1 = (f32[14,64,128]{2,1,0:T(8,128)}, f32[14,64,128]{2,1,0:T(8,128)S(1)}, u32[]{:S(2)}, u32[]{:S(2)}) collective-permute-start(f32[14,64,128]{2,1,0:T(8,128)} %get-tuple-element.34), channel_id=1, source_target_pairs={{4,8},{8,4},{5,9},{9,5},{6,10},{10,6},{7,11},{11,7},{20,24},{24,20... | collective-permute-start | bytes 1376264 | tf_op jit(solution)/shard_map/ppermute | solution.py:535
  9.0 11.8 %collective-permute-start.3 = (f32[11,16,128]{2,1,0:T(8,128)}, f32[11,16,128]{2,1,0:T(8,128)S(1)}, u32[]{:S(2)}, u32[]{:S(2)}) collective-permute-start(f32[11,16,128]{2,1,0:T(8,128)} %get-tuple-element.36), channel_id=1, source_target_pairs={{0,6},{2,4},{4,2},{6,0},{8,14},{10,12},{12,10},{14,8},{1,7},{3,5},... | collective-permute-start | bytes 270344 | tf_op jit(solution)/shard_map/ppermute | solution.py:540
  13.4 7.4 %collective-permute-start.4 = (f32[11,16,128]{2,1,0:T(8,128)}, f32[11,16,128]{2,1,0:T(8,128)S(1)}, u32[]{:S(2)}, u32[]{:S(2)}) collective-permute-start(f32[11,16,128]{2,1,0:T(8,128)} %get-tuple-element.37), channel_id=1, source_target_pairs={{4,10},{6,8},{8,6},{10,4},{5,11},{7,9},{9,7},{11,5},{20,26},{22,24... | collective-permute-start | bytes 270344 | tf_op jit(solution)/shard_map/ppermute | solution.py:540
  21.7 1.9 %collective-permute-start.5 = (f32[12,80,128]{2,1,0:T(8,128)S(1)}, f32[12,80,128]{2,1,0:T(8,128)S(1)}, u32[]{:S(2)}, u32[]{:S(2)}) collective-permute-start(f32[12,80,128]{2,1,0:T(8,128)S(1)} %get-tuple-element.46), channel_id=1, source_target_pairs={{0,1},{1,0},{2,3},{3,2},{4,5},{5,4},{6,7},{7,6},{8,9},{9,8},{10,11... | collective-permute-start | bytes 1474568 | tf_op jit(solution)/shard_map/ppermute | solution.py:579
  43.3 1.9 %copy-start.3 = (f32[48,80,256]{2,1,0:T(8,128)}, f32[48,80,256]{2,1,0:T(8,128)S(1)}, u32[]{:S(2)}) copy-start(f32[48,80,256]{2,1,0:T(8,128)S(1)} %get-tuple-element.48.r_0_) | copy-start | bytes 11796484
  45.2 1.9 %copy-start.5 = (f32[48,80,256]{2,1,0:T(8,128)}, f32[48,80,256]{2,1,0:T(8,128)S(1)}, u32[]{:S(2)}) copy-start(f32[48,80,256]{2,1,0:T(8,128)S(1)} %get-tuple-element.49.r_1_) | copy-start | bytes 11796484
  47.1 1.9 %copy-start.7 = (f32[48,80,256]{2,1,0:T(8,128)}, f32[48,80,256]{2,1,0:T(8,128)S(1)}, u32[]{:S(2)}) copy-start(f32[48,80,256]{2,1,0:T(8,128)S(1)} %get-tuple-element.50.r_2_) | copy-start | bytes 11796484
  50.8 1.9 %copy-start.11 = (f32[48,80,256]{2,1,0:T(8,128)}, f32[48,80,256]{2,1,0:T(8,128)S(1)}, u32[]{:S(2)}) copy-start(f32[48,80,256]{2,1,0:T(8,128)S(1)} %get-tuple-element.52.r_4_) | copy-start | bytes 11796484
  52.7 1.9 %copy-start.13 = (f32[48,80,256]{2,1,0:T(8,128)}, f32[48,80,256]{2,1,0:T(8,128)S(1)}, u32[]{:S(2)}) copy-start(f32[48,80,256]{2,1,0:T(8,128)S(1)} %get-tuple-element.53.r_5_) | copy-start | bytes 11796484
  55.3 1.3 %collective-permute-start.8 = (f32[8,16,128]{2,1,0:T(8,128)S(1)}, f32[8,16,128]{2,1,0:T(8,128)S(1)}, u32[]{:S(2)}, u32[]{:S(2)}) collective-permute-start(f32[8,16,128]{2,1,0:T(8,128)S(1)} %get-tuple-element.63), channel_id=1, source_target_pairs={{0,1},{1,0},{2,3},{3,2},{4,5},{5,4},{6,7},{7,6},{8,9},{9,8},{10,11... | collective-permute-start | bytes 196616 | tf_op jit(solution)/shard_map/ppermute | solution.py:544
  56.6 6.9 %collective-permute-start.9 = (f32[8,16,128]{2,1,0:T(8,128)S(1)}, f32[8,16,128]{2,1,0:T(8,128)}, u32[]{:S(2)}, u32[]{:S(2)}) collective-permute-start(f32[8,16,128]{2,1,0:T(8,128)S(1)} %add.9), channel_id=1, source_target_pairs={{0,2},{2,0},{1,3},{3,1},{4,6},{6,4},{5,7},{7,5},{8,10},{10,8},{9,1... | collective-permute-start | bytes 196616 | tf_op jit(solution)/shard_map/ppermute | solution.py:545
  58.4 13.1 %collective-permute-start.6 = (f32[7,40,128]{2,1,0:T(8,128)}, f32[7,40,128]{2,1,0:T(8,128)S(1)}, u32[]{:S(2)}, u32[]{:S(2)}) collective-permute-start(f32[7,40,128]{2,1,0:T(8,128)} %copy-done.16), channel_id=1, source_target_pairs={{0,4},{4,0},{8,12},{12,8},{1,5},{5,1},{9,13},{13,9},{2,6},{6,2},{1... | collective-permute-start | bytes 430088 | tf_op jit(solution)/shard_map/ppermute | solution.py:589
  62.8 8.7 %collective-permute-start.7 = (f32[7,40,128]{2,1,0:T(8,128)}, f32[7,40,128]{2,1,0:T(8,128)S(1)}, u32[]{:S(2)}, u32[]{:S(2)}) collective-permute-start(f32[7,40,128]{2,1,0:T(8,128)} %copy-done.15), channel_id=1, source_target_pairs={{4,8},{8,4},{5,9},{9,5},{6,10},{10,6},{7,11},{11,7},{20,24},{24,20... | collective-permute-start | bytes 430088 | tf_op jit(solution)/shard_map/ppermute | solution.py:589
  64.3 10.4 %collective-permute-start.10 = (f32[2,8,16,128]{3,2,1,0:T(8,128)S(1)}, f32[2,8,16,128]{3,2,1,0:T(8,128)S(1)}, u32[]{:S(2)}, u32[]{:S(2)}) collective-permute-start(f32[2,8,16,128]{3,2,1,0:T(8,128)S(1)} %pad_maximum_fusion.r_15_), channel_id=1, source_target_pairs={{0,4},{4,0},{8,12},{12,8},{1,5},{5,1},{9,13},{13,9},{2,6},{6,2},{1... | collective-permute-start | bytes 393224 | tf_op jit(solution)/shard_map/ppermute | solution.py:548
  67.3 7.4 %collective-permute-start.11 = (f32[2,8,16,128]{3,2,1,0:T(8,128)S(1)}, f32[2,8,16,128]{3,2,1,0:T(8,128)S(1)}, u32[]{:S(2)}, u32[]{:S(2)}) collective-permute-start(f32[2,8,16,128]{3,2,1,0:T(8,128)S(1)} %pad_maximum_fusion.r_15_), channel_id=1, source_target_pairs={{4,8},{8,4},{5,9},{9,5},{6,10},{10,6},{7,11},{11,7},{20,24},{24,20... | collective-permute-start | bytes 393224 | tf_op jit(solution)/shard_map/ppermute | solution.py:548
  68.7 6.0 %collective-permute-start.12 = (f32[2,2,16,128]{3,2,1,0:T(8,128)S(1)}, f32[2,2,16,128]{3,2,1,0:T(8,128)S(1)}, u32[]{:S(2)}, u32[]{:S(2)}) collective-permute-start(f32[2,2,16,128]{3,2,1,0:T(8,128)S(1)} %fusion), channel_id=1, source_target_pairs={{0,8},{8,0},{4,12},{12,4},{1,9},{9,1},{5,13},{13,5},{2,10},{10,2},... | collective-permute-start | bytes 98312 | tf_op jit(solution)/shard_map/ppermute | solution.py:552
  74.7 2.1 %copy-start.4 = (f32[48,80,256]{2,1,0:T(8,128)S(1)}, f32[48,80,256]{2,1,0:T(8,128)}, u32[]{:S(2)}) copy-start(f32[48,80,256]{2,1,0:T(8,128)} %copy-done.3) | copy-start | bytes 11796484
  76.8 2.1 %copy-start.6 = (f32[48,80,256]{2,1,0:T(8,128)S(1)}, f32[48,80,256]{2,1,0:T(8,128)}, u32[]{:S(2)}) copy-start(f32[48,80,256]{2,1,0:T(8,128)} %copy-done.5) | copy-start | bytes 11796484
  79.0 2.1 %copy-start.8 = (f32[48,80,256]{2,1,0:T(8,128)S(1)}, f32[48,80,256]{2,1,0:T(8,128)}, u32[]{:S(2)}) copy-start(f32[48,80,256]{2,1,0:T(8,128)} %copy-done.7) | copy-start | bytes 11796484
  81.1 2.1 %copy-start.10 = (f32[48,80,256]{2,1,0:T(8,128)S(1)}, f32[48,80,256]{2,1,0:T(8,128)}, u32[]{:S(2)}) copy-start(f32[48,80,256]{2,1,0:T(8,128)} %copy-done.9) | copy-start | bytes 11796484
  83.2 2.1 %copy-start.12 = (f32[48,80,256]{2,1,0:T(8,128)S(1)}, f32[48,80,256]{2,1,0:T(8,128)}, u32[]{:S(2)}) copy-start(f32[48,80,256]{2,1,0:T(8,128)} %copy-done.11) | copy-start | bytes 11796484
  85.3 2.1 %copy-start.14 = (f32[48,80,256]{2,1,0:T(8,128)S(1)}, f32[48,80,256]{2,1,0:T(8,128)}, u32[]{:S(2)}) copy-start(f32[48,80,256]{2,1,0:T(8,128)} %copy-done.13) | copy-start | bytes 11796484
  (7 other events, 8.3 us)

commit v5 on v4

--- a/solution.py
+++ b/solution.py
@@ -330,10 +330,22 @@
     return thrice(jnp.where((i < limit) & (j == shift + lax.div(i, 2)), weight, 0.0))
 
 
+KEPT = 13
+SKIP = XH - 3
+
+
+def inner(ref, out):
+    skip = (ref.shape[0] - out.shape[0]) // 2
+    return ref.at[skip:ref.shape[0] - skip]
+
+
 def down_kernel(nx, cpad, gpad, strip, c2, *refs):
-    kx, ky, kz, rd, g, u0, kx1, ky1, kz1, rd1, c1, f1, u1, f2 = refs[:14]
-    faces = refs[14:14 + nx]
-    c, first, v1, work, work1 = refs[14 + nx:]
+    kept, f2 = refs[:KEPT], refs[KEPT]
+    faces = refs[KEPT + 1:KEPT + 1 + nx]
+    held_here = refs[KEPT + 1 + nx:2 * KEPT + 1 + nx]
+    kx, ky, kz, rd, g, u0, kx1, ky1, kz1, rd1, c1, f1, u1 = held_here
+    c, first, v1, work, work1, sems = refs[2 * KEPT + 1 + nx:]
+    copies = [pltpu.make_async_copy(inner(a, k), k, sems.at[i]) for i, (a, k) in enumerate(zip(held_here, kept))]
     planes, rows, oz = cpad.shape
     pz = lax.axis_index("pair")
     bx = lax.axis_index("boxes")
@@ -356,12 +368,15 @@
     loop(0, packed, unpack)
     edge = XH - GX
     coefficients(c, kx, ky, kz, rd, edge, planes - edge, 1.0)
+    for copy in copies[0:5]:
+        copy.start()
 
     def start_sweep(x):
         first[x] = g[x] * rd[x]
 
     loop(edge, planes - edge, start_sweep)
     sweep(first, u0, g, kx, ky, kz, rd, edge + 1, planes - edge - 1)
+    copies[5].start()
     rest = first
 
     def use(x, vx, av):
@@ -383,6 +398,8 @@
     loop(low1, high1, start_sweep1)
     u1[...] = jnp.zeros_like(u1)
     sweep(v1, u1, f1, kx1, ky1, kz1, rd1, low1 + 1, high1 - 1)
+    for copy in copies[6:]:
+        copy.start()
     h1 = XH // 2
     o1 = planes1 - XH
 
@@ -399,11 +416,13 @@
         up = upward(bx, e)
         faces[e][0:h1] = u1[pl.ds(jnp.where(up, o1, h1), h1)]
         faces[e][h1:2 * h1 - 1] = f1[pl.ds(jnp.where(up, o1 + 1, h1), h1 - 1)]
+    for copy in copies:
+        copy.wait()
 
 
 def up_kernel(nx, ny, nfar, *refs):
-    kx, ky, kz, rd, g, u0, kx1, ky1, kz1, rd1, c1, f1, u1 = refs[:13]
-    at = 13
+    kept = refs[:KEPT]
+    at = KEPT
     faces = refs[at:at + nx]
     at += nx
     pieces = 1 + nx + nfar
@@ -411,7 +430,13 @@
     at += pieces
     field, residual = refs[at:at + 2]
     at += 2
-    ua, ub, v1, w1, g1, c2, f2, kx2, ky2, kz2, rd2, v2, w2, tall, wide = refs[at:]
+    held_here = refs[at:at + KEPT]
+    at += KEPT
+    kx, ky, kz, rd, g, u0, kx1, ky1, kz1, rd1, c1, f1, u1 = held_here
+    ua, ub, v1, w1, c2, f2, kx2, ky2, kz2, rd2, v2, w2, tall, wide, sems = refs[at:]
+    copies = [pltpu.make_async_copy(k, inner(a, k), sems.at[i]) for i, (a, k) in enumerate(zip(held_here, kept))]
+    for copy in copies[6:] + copies[:6]:
+        copy.start()
     planes, rows, lanes = u0.shape
     planes1, rows1, oz = u1.shape
     planes2, rows2, _ = c2.shape
@@ -452,13 +477,12 @@
 
     h1 = XH // 2
     o1 = planes1 - XH
-    for x in range(planes1):
-        g1[x] = f1[x]
-        v1[x] = u1[x]
+    for copy in copies[6:]:
+        copy.wait()
     for e in range(nx):
         up = upward(bx, e)
-        v1[pl.ds(jnp.where(up, planes1 - h1, 0), h1)] = faces[e][0:h1]
-        g1[pl.ds(jnp.where(up, planes1 - h1, 1), h1 - 1)] = faces[e][h1:2 * h1 - 1]
+        u1[pl.ds(jnp.where(up, planes1 - h1, 0), h1)] = faces[e][0:h1]
+        f1[pl.ds(jnp.where(up, planes1 - h1, 1), h1 - 1)] = faces[e][h1:2 * h1 - 1]
     i, j = iota2((oz, oz), 0), iota2((oz, oz), 1)
     spread_z = thrice(jnp.where(i == lax.div(lax.rem(pz * (oz // 2) + j, oz), 2), 1.0, 0.0))
     base = L2X - h1 // 2
@@ -477,14 +501,16 @@
         both = tall[x, 0:rows1, :]
         for k in range(2):
             y = 2 * x + k
-            v1[y] = jnp.where(c1[y] > 0.0, v1[y] + both, 0.0)
-
-    sweep(v1, w1, g1, kx1, ky1, kz1, rd1, 1, planes1 - 1)
-    sweep(w1, v1, g1, kx1, ky1, kz1, rd1, 2, planes1 - 2)
+            v1[y] = jnp.where(c1[y] > 0.0, u1[y] + both, 0.0)
+
+    sweep(v1, w1, f1, kx1, ky1, kz1, rd1, 1, planes1 - 1)
+    sweep(w1, v1, f1, kx1, ky1, kz1, rd1, 2, planes1 - 2)
 
     i, j = iota2((oz, lanes), 0), iota2((oz, lanes), 1)
     spread_z0 = thrice(jnp.where(i == lax.div(j, 2), 1.0, 0.0))
     step = 4
+    for copy in copies[:6]:
+        copy.wait()
 
     def spread0(n):
         low = 2 + step * n
@@ -510,13 +536,22 @@
     operate(ua, kx, ky, kz, XH, planes - XH, use)
 
 
-def call(kernel, outs, scratch=(), mib=60):
-    return pl.pallas_call(
-        kernel,
-        out_shape=tuple(outs),
-        scratch_shapes=tuple(pltpu.VMEM(s, F32) for s in scratch),
-        compiler_params=params(mib),
-    )
+def call(kernel, outs, scratch=(), mib=16, raw_in=0, raw_out=0, copies=0):
+    where = [pl.BlockSpec(memory_space=pl.ANY)], [pl.BlockSpec(memory_space=pltpu.VMEM)]
+    outs = tuple(outs)
+    extra = (pltpu.SemaphoreType.DMA((copies,)),) if copies else ()
+
+    def run(*operands):
+        return pl.pallas_call(
+            kernel,
+            in_specs=where[0] * raw_in + where[1] * (len(operands) - raw_in),
+            out_specs=tuple(where[0] * raw_out + where[1] * (len(outs) - raw_out)),
+            out_shape=outs,
+            scratch_shapes=tuple(pltpu.VMEM(s, F32) for s in scratch) + extra,
+            compiler_params=params(mib),
+        )(*operands)
+
+    return run
 
 
 def per_device(phase, target_mask, deviation):
@@ -579,22 +614,28 @@
     strip = lax.ppermute(strip, "pair", pair_swap)
     fine = (planes, rows, 2 * oz)
     middle = (planes1, rows1, oz)
+    small = (planes - 2 * SKIP, rows, 2 * oz)
     down = call(
         lambda *r: down_kernel(nx, *r),
-        [in_vmem(fine)] * 6 + [in_vmem(middle)] * 7 + [spec((o2x, o2y, oz))] + [spec((XH - 1, rows1, oz))] * nx,
-        [fine, fine, middle, (8, rows, oz), (o2x, oy // 2, oz)],
-        mib=24,
+        [spec(small)] * 6 + [spec(middle)] * 7 + [spec((o2x, o2y, oz))] + [spec((XH - 1, rows1, oz))] * nx,
+        [fine] * 6 + [middle] * 7 + [fine, fine, middle, (8, rows, oz), (o2x, oy // 2, oz)],
+        mib=48,
+        raw_out=KEPT,
+        copies=KEPT,
     )(held(cpad), held(gpad), strip, c2)
-    kept, f2, sides = down[:13], down[13], down[14:]
+    kept, f2, sides = down[:KEPT], down[KEPT], down[KEPT + 1:]
     sides = [lax.ppermute(s, "boxes", p) for s, p in zip(sides, swap_x)]
     got = gathered(f2)
     lowest = (planes2, rows2, oz)
     return tuple(call(
         lambda *r: up_kernel(nx, ny, nfar, *r),
         [box, box],
-        [fine, fine, middle, middle, middle] + [lowest] * 8 + [(planes1 // 2, 2 * (o2y + 8), oz), (8, rows, oz)],
-        mib=24,
-    )(*[held(x) for x in kept], *sides, *got))
+        [fine] * 6 + [middle] * 7 + [fine, fine, middle, middle] + [lowest] * 8
+        + [(planes1 // 2, 2 * (o2y + 8), oz), (8, rows, oz)],
+        mib=52,
+        raw_in=KEPT,
+        copies=KEPT,
+    )(*kept, *sides, *got))
 
 
 def solution(mesh):

time: 105 us -> 84.2 us (0.80)
  local copies, waits for them, and re-layouts: 29.1 us -> 5.23 us
  waiting for transfers between devices: 8.4 us -> 12.8 us
  other arithmetic: 1.59 us -> 0.03 us
    unnamed x36 -> x16, local copies, waits for them, and re-layouts: 29.1 us -> 5.23 us
    ppermute x2, waiting for transfers between devices: 2.14 us -> 5.55 us  [traded(): lax.ppermute(faces[nx + ny + e * ny + f], ('boxes', 'sub'), both(swap_x[e...]
    another operation x2, other arithmetic: 1.58 us -> 0.02 us  [gathered(): sheet = jnp.stack([line] + [lax.ppermute(line, 'sub', p) for p in swap_y])]
  transfers between devices with their start and end apart: 13 -> 13, of which waited for: 4 -> 4; matrix products, arithmetic and copies ran while one was open for 2% -> 0% of each run, Pallas kernels for 1% -> 1%
where the time goes in v5:
time: 84.2 us; the launch traced here: 83.8 us
  Pallas kernels  41.1 us (49%)
  starting transfers between devices  23.9 us (28%)
  waiting for transfers between devices  12.8 us (15%)
  local copies, waits for them, and re-layouts  5.23 us (6%)
    pallas_call x5, Pallas kernels, run(): pl.pallas_call(kernel, in_specs=where[0] * raw_in + where[1] * (len(opera...  41.1 us
    ppermute x2, waiting for transfers between devices, traded(): lax.ppermute(faces[nx + ny + e * ny + f], ('boxes', 'sub'), both(swap_x[e...  5.55 us
    unnamed x16, local copies, waits for them, and re-layouts  5.23 us
    ppermute x2, starting transfers between devices, traded(): lax.ppermute(faces[nx + ny + e * ny + f], ('boxes', 'sub'), both(swap_x[e...  5.06 us
    ppermute x2, starting transfers between devices, per_device(): sides = [lax.ppermute(s, 'boxes', p) for s, p in zip(sides, swap_x)]  5.05 us
    ppermute x1, waiting for transfers between devices, gathered(): lax.ppermute(lax.dynamic_slice_in_dim(sheet, at, count, axis=1), 'boxes', p)  4.26 us
    ppermute x2, starting transfers between devices, gathered(): out.append(lax.ppermute(sheet, 'boxes', p))  3.7 us
    ppermute x1, starting transfers between devices, traded(): out.append(lax.ppermute(faces[nx + f], 'sub', swap_y[f]))  3 us
  transfers between devices with their start and end apart: 13, of which 4 were waited for; matrix products, arithmetic and copies ran while one was open for 0% of the time, Pallas kernels for 1%

profile of v5, /device:TPU:0, one launch (start us, length us, event | category | flops | bytes accessed | tf_op | source)
XLA Modules:
  0.0 83.8 jit_solution(13341901450319957234)
XLA Ops:
  0.6 1.2 %copy-done = f32[32,64,128]{2,1,0:T(8,128)S(1)} copy-done((f32[32,64,128]{2,1,0:T(8,128)S(1)}, f32[32,64,128]{2,1,0:T(8,128)}, u32[]{:S(2)}) %copy-start) | copy-done | bytes 1048600
  1.9 1.2 %copy-done.2 = s32[32,64,128]{2,1,0:T(8,128)S(1)} copy-done((s32[32,64,128]{2,1,0:T(8,128)S(1)}, s32[32,64,128]{2,1,0:T(8,128)}, u32[]{:S(2)}) %copy-start.2) | copy-done | bytes 1048600
  3.1 1.2 %copy-done.4 = f32[32,64,128]{2,1,0:T(8,128)S(1)} copy-done((f32[32,64,128]{2,1,0:T(8,128)S(1)}, f32[32,64,128]{2,1,0:T(8,128)}, u32[]{:S(2)}) %copy-start.4) | copy-done | bytes 1048600
  4.5 3.0 %collective-permute-start.2 = (f32[2,32,16,128]{3,2,1,0:T(8,128)S(1)}, f32[2,32,16,128]{3,2,1,0:T(8,128)S(1)}, u32[]{:S(2)}, u32[]{:S(2)}) collective-permute-start(f32[2,32,16,128]{3,2,1,0:T(8,128)S(1)} %get-tuple-element.35), channel_id=1, source_target_pairs={{0,2},{2,0},{1,3},{3,1},{4,6},{6,4},{5,7},{7,5},{8,10},{10,8},{9,1... | collective-permute-start | bytes 1572872 | tf_op jit(solution)/shard_map/ppermute | solution.py:572
  7.5 1.6 %collective-permute-start = (f32[14,64,128]{2,1,0:T(8,128)S(1)}, f32[14,64,128]{2,1,0:T(8,128)S(1)}, u32[]{:S(2)}, u32[]{:S(2)}) collective-permute-start(f32[14,64,128]{2,1,0:T(8,128)S(1)} %get-tuple-element.33), channel_id=1, source_target_pairs={{0,4},{4,0},{8,12},{12,8},{1,5},{5,1},{9,13},{13,9},{2,6},{6,2},{1... | collective-permute-start | bytes 1376264 | tf_op jit(solution)/shard_map/ppermute | solution.py:570
  9.1 0.7 collective-permute-start.1
  9.8 4.4 %collective-permute-start.3 = (f32[11,16,128]{2,1,0:T(8,128)S(1)}, f32[11,16,128]{2,1,0:T(8,128)S(1)}, u32[]{:S(2)}, u32[]{:S(2)}) collective-permute-start(f32[11,16,128]{2,1,0:T(8,128)S(1)} %get-tuple-element.36), channel_id=1, source_target_pairs={{0,6},{2,4},{4,2},{6,0},{8,14},{10,12},{12,10},{14,8},{1,7},{3,5},... | collective-permute-start | bytes 270344 | tf_op jit(solution)/shard_map/ppermute | solution.py:575
  14.2 0.7 collective-permute-start.4
  14.9 0.9 %shard_map.51 = (f32[32,64,128]{2,1,0:T(8,128)S(1)}, f32[32,64,128]{2,1,0:T(8,128)S(1)}, f32[2,4,64,128]{3,2,1,0:T(8,128)S(1)}, f32[8,16,128]{2,1,0:T(8,128)S(1)}) custom-call(f32[32,64,128]{2,1,0:T(8,128)S(1)} %copy-done.1, s32[32,64,128]{2,1,0:T(8,128)S(1)} %copy-done.3, f32[32,64,128]{2,1,0:T(8,128)S(1)} %copy-done.5), custom_call_target="tpu_custom_call" | custom-call | tf_op jit(solution)/shard_map/pallas_call | solution.py:545
  15.8 5.6 %collective-permute-done.3.r_6_ = f32[11,16,128]{2,1,0:T(8,128)S(1)} collective-permute-done((f32[11,16,128]{2,1,0:T(8,128)S(1)}, f32[11,16,128]{2,1,0:T(8,128)S(1)}, u32[]{:S(2)}, u32[]{:S(2)}) %collective-permute-start.3) | collective-permute-done | bytes 90144 | tf_op jit(solution)/shard_map/ppermute | solution.py:575
  21.4 0.9 %shard_map.52 = (f32[48,80,128]{2,1,0:T(8,128)S(1)}, f32[48,80,128]{2,1,0:T(8,128)S(1)}, f32[12,80,128]{2,1,0:T(8,128)S(1)}) custom-call(f32[32,64,128]{2,1,0:T(8,128)S(1)} %get-tuple-element.41.r_0_, f32[32,64,128]{2,1,0:T(8,128)S(1)} %get-tuple-element.42.r_1_, f32[2,4,64,128]{3,2,1,0:T(8,128)S(1)} %get-tuple-element.43.r_2_, ...), custom_call_target="tpu_custom_call" | custom-call | tf_op jit(solution)/shard_map/pallas_call | solution.py:545
  22.4 1.9 %collective-permute-done.5.r_2_ = f32[12,80,128]{2,1,0:T(8,128)S(1)} collective-permute-done((f32[12,80,128]{2,1,0:T(8,128)S(1)}, f32[12,80,128]{2,1,0:T(8,128)S(1)}, u32[]{:S(2)}, u32[]{:S(2)}) %collective-permute-start.5) | collective-permute-done | bytes 491552 | tf_op jit(solution)/shard_map/ppermute | solution.py:614
  24.2 0.8 copy-done.7
  25.0 20.5 %shard_map.53 = (f32[38,80,256]{2,1,0:T(8,128)}, f32[38,80,256]{2,1,0:T(8,128)}, f32[38,80,256]{2,1,0:T(8,128)}, f32[38,80,256]{2,1,0:T(8,128)}, f32[38,80,256]{...) custom-call(f32[48,80,128]{2,1,0:T(8,128)S(1)} %get-tuple-element.44, ...), custom_call_target="tpu_custom_call" | custom-call | tf_op jit(solution)/shard_map/pallas_call | solution.py:545
  45.5 0.8 copy-done.6
  46.4 1.1 %collective-permute-done.8 = f32[8,16,128]{2,1,0:T(8,128)S(1)} collective-permute-done((f32[8,16,128]{2,1,0:T(8,128)S(1)}, f32[8,16,128]{2,1,0:T(8,128)S(1)}, u32[]{:S(2)}, u32[]{:S(2)}) %collective-permute-start.8) | collective-permute-done | bytes 65568 | tf_op jit(solution)/shard_map/ppermute | solution.py:579
  47.5 1.8 %collective-permute-start.9 = (f32[8,16,128]{2,1,0:T(8,128)S(1)}, f32[8,16,128]{2,1,0:T(8,128)S(1)}, u32[]{:S(2)}, u32[]{:S(2)}) collective-permute-start(f32[8,16,128]{2,1,0:T(8,128)S(1)} %add.9), channel_id=1, source_target_pairs={{0,2},{2,0},{1,3},{3,1},{4,6},{6,4},{5,7},{7,5},{8,10},{10,8},{9,1... | collective-permute-start | bytes 196616 | tf_op jit(solution)/shard_map/ppermute | solution.py:580
  49.3 4.4 %collective-permute-start.6 = (f32[7,40,128]{2,1,0:T(8,128)S(1)}, f32[7,40,128]{2,1,0:T(8,128)S(1)}, u32[]{:S(2)}, u32[]{:S(2)}) collective-permute-start(f32[7,40,128]{2,1,0:T(8,128)S(1)} %get-tuple-element.61), channel_id=1, source_target_pairs={{0,4},{4,0},{8,12},{12,8},{1,5},{5,1},{9,13},{13,9},{2,6},{6,2},{1... | collective-permute-start | bytes 430088 | tf_op jit(solution)/shard_map/ppermute | solution.py:627
  53.7 0.7 collective-permute-start.7
  54.4 3.0 %collective-permute-start.10 = (f32[2,8,16,128]{3,2,1,0:T(8,128)S(1)}, f32[2,8,16,128]{3,2,1,0:T(8,128)S(1)}, u32[]{:S(2)}, u32[]{:S(2)}) collective-permute-start(f32[2,8,16,128]{3,2,1,0:T(8,128)S(1)} %pad_maximum_fusion.r_15_), channel_id=1, source_target_pairs={{0,4},{4,0},{8,12},{12,8},{1,5},{5,1},{9,13},{13,9},{2,6},{6,2},{1... | collective-permute-start | bytes 393224 | tf_op jit(solution)/shard_map/ppermute | solution.py:583
  57.4 0.7 collective-permute-start.11
  58.1 2.8 %collective-permute-start.12 = (f32[2,2,16,128]{3,2,1,0:T(8,128)S(1)}, f32[2,2,16,128]{3,2,1,0:T(8,128)S(1)}, u32[]{:S(2)}, u32[]{:S(2)}) collective-permute-start(f32[2,2,16,128]{3,2,1,0:T(8,128)S(1)} %fusion), channel_id=1, source_target_pairs={{0,8},{8,0},{4,12},{12,4},{1,9},{9,1},{5,13},{13,5},{2,10},{10,2},... | collective-permute-start | bytes 98312 | tf_op jit(solution)/shard_map/ppermute | solution.py:587
  60.9 4.3 %collective-permute-done.12.r_18_ = f32[2,2,16,128]{3,2,1,0:T(8,128)S(1)} collective-permute-done((f32[2,2,16,128]{3,2,1,0:T(8,128)S(1)}, f32[2,2,16,128]{3,2,1,0:T(8,128)S(1)}, u32[]{:S(2)}, u32[]{:S(2)}) %collective-permute-start.12) | collective-permute-done | bytes 32800 | tf_op jit(solution)/shard_map/ppermute | solution.py:587
  65.2 18.6 %shard_map.54 = (f32[32,64,128]{2,1,0:T(8,128)}, f32[32,64,128]{2,1,0:T(8,128)}) custom-call(f32[38,80,256]{2,1,0:T(8,128)} %get-tuple-element.48.r_0_, f32[38,80,256]{2,1,0:T(8,128)} %get-tuple-element.49.r_1_, f32[38,80,256]{2,1,0:T(8,128)} %get-tuple-element.50.r_2_, f32[38,80,256]{2,1,0:T(8,128)} %get-tuple-element.51.r_3_, ...), custom_call_target="tpu_custom_call" | custom-call | tf_op jit(solution)/shard_map/pallas_call | solution.py:545
  (26 shorter events, 0.5 us)
Async XLA Ops:
  0.6 1.2 %copy-start = (f32[32,64,128]{2,1,0:T(8,128)S(1)}, f32[32,64,128]{2,1,0:T(8,128)}, u32[]{:S(2)}) copy-start(f32[32,64,128]{2,1,0:T(8,128)} %phase) | copy-start | bytes 3145732
  1.9 1.2 %copy-start.2 = (s32[32,64,128]{2,1,0:T(8,128)S(1)}, s32[32,64,128]{2,1,0:T(8,128)}, u32[]{:S(2)}) copy-start(s32[32,64,128]{2,1,0:T(8,128)} %mask) | copy-start | bytes 3145732
  3.1 1.2 %copy-start.4 = (f32[32,64,128]{2,1,0:T(8,128)S(1)}, f32[32,64,128]{2,1,0:T(8,128)}, u32[]{:S(2)}) copy-start(f32[32,64,128]{2,1,0:T(8,128)} %dev) | copy-start | bytes 3145732
  4.3 10.6 %copy-start.1 = (f32[32,64,128]{2,1,0:T(8,128)S(1)}, f32[32,64,128]{2,1,0:T(8,128)}, u32[]{:S(2)}) copy-start(f32[32,64,128]{2,1,0:T(8,128)} %phase) | copy-start | bytes 3145732
  4.3 10.6 %copy-start.3 = (s32[32,64,128]{2,1,0:T(8,128)S(1)}, s32[32,64,128]{2,1,0:T(8,128)}, u32[]{:S(2)}) copy-start(s32[32,64,128]{2,1,0:T(8,128)} %mask) | copy-start | bytes 3145732
  4.3 10.6 %copy-start.5 = (f32[32,64,128]{2,1,0:T(8,128)S(1)}, f32[32,64,128]{2,1,0:T(8,128)}, u32[]{:S(2)}) copy-start(f32[32,64,128]{2,1,0:T(8,128)} %dev) | copy-start | bytes 3145732
  4.5 16.9 %collective-permute-start.2 = (f32[2,32,16,128]{3,2,1,0:T(8,128)S(1)}, f32[2,32,16,128]{3,2,1,0:T(8,128)S(1)}, u32[]{:S(2)}, u32[]{:S(2)}) collective-permute-start(f32[2,32,16,128]{3,2,1,0:T(8,128)S(1)} %get-tuple-element.35), channel_id=1, source_target_pairs={{0,2},{2,0},{1,3},{3,1},{4,6},{6,4},{5,7},{7,5},{8,10},{10,8},{9,1... | collective-permute-start | bytes 1572872 | tf_op jit(solution)/shard_map/ppermute | solution.py:572
  7.5 13.8 %collective-permute-start = (f32[14,64,128]{2,1,0:T(8,128)S(1)}, f32[14,64,128]{2,1,0:T(8,128)S(1)}, u32[]{:S(2)}, u32[]{:S(2)}) collective-permute-start(f32[14,64,128]{2,1,0:T(8,128)S(1)} %get-tuple-element.33), channel_id=1, source_target_pairs={{0,4},{4,0},{8,12},{12,8},{1,5},{5,1},{9,13},{13,9},{2,6},{6,2},{1... | collective-permute-start | bytes 1376264 | tf_op jit(solution)/shard_map/ppermute | solution.py:570
  9.1 12.3 %collective-permute-start.1 = (f32[14,64,128]{2,1,0:T(8,128)S(1)}, f32[14,64,128]{2,1,0:T(8,128)S(1)}, u32[]{:S(2)}, u32[]{:S(2)}) collective-permute-start(f32[14,64,128]{2,1,0:T(8,128)S(1)} %get-tuple-element.34), channel_id=1, source_target_pairs={{4,8},{8,4},{5,9},{9,5},{6,10},{10,6},{7,11},{11,7},{20,24},{24,20... | collective-permute-start | bytes 1376264 | tf_op jit(solution)/shard_map/ppermute | solution.py:570
  9.8 11.6 %collective-permute-start.3 = (f32[11,16,128]{2,1,0:T(8,128)S(1)}, f32[11,16,128]{2,1,0:T(8,128)S(1)}, u32[]{:S(2)}, u32[]{:S(2)}) collective-permute-start(f32[11,16,128]{2,1,0:T(8,128)S(1)} %get-tuple-element.36), channel_id=1, source_target_pairs={{0,6},{2,4},{4,2},{6,0},{8,14},{10,12},{12,10},{14,8},{1,7},{3,5},... | collective-permute-start | bytes 270344 | tf_op jit(solution)/shard_map/ppermute | solution.py:575
  14.2 7.2 %collective-permute-start.4 = (f32[11,16,128]{2,1,0:T(8,128)S(1)}, f32[11,16,128]{2,1,0:T(8,128)S(1)}, u32[]{:S(2)}, u32[]{:S(2)}) collective-permute-start(f32[11,16,128]{2,1,0:T(8,128)S(1)} %get-tuple-element.37), channel_id=1, source_target_pairs={{4,10},{6,8},{8,6},{10,4},{5,11},{7,9},{9,7},{11,5},{20,26},{22,24... | collective-permute-start | bytes 270344 | tf_op jit(solution)/shard_map/ppermute | solution.py:575
  22.3 1.9 %collective-permute-start.5 = (f32[12,80,128]{2,1,0:T(8,128)S(1)}, f32[12,80,128]{2,1,0:T(8,128)S(1)}, u32[]{:S(2)}, u32[]{:S(2)}) collective-permute-start(f32[12,80,128]{2,1,0:T(8,128)S(1)} %get-tuple-element.46), channel_id=1, source_target_pairs={{0,1},{1,0},{2,3},{3,2},{4,5},{5,4},{6,7},{7,6},{8,9},{9,8},{10,11... | collective-permute-start | bytes 1474568 | tf_op jit(solution)/shard_map/ppermute | solution.py:614
  24.2 0.8 copy-start.7
  45.5 0.8 copy-start.6
  46.2 1.3 %collective-permute-start.8 = (f32[8,16,128]{2,1,0:T(8,128)S(1)}, f32[8,16,128]{2,1,0:T(8,128)S(1)}, u32[]{:S(2)}, u32[]{:S(2)}) collective-permute-start(f32[8,16,128]{2,1,0:T(8,128)S(1)} %get-tuple-element.63), channel_id=1, source_target_pairs={{0,1},{1,0},{2,3},{3,2},{4,5},{5,4},{6,7},{7,6},{8,9},{9,8},{10,11... | collective-permute-start | bytes 196616 | tf_op jit(solution)/shard_map/ppermute | solution.py:579
  47.5 6.9 %collective-permute-start.9 = (f32[8,16,128]{2,1,0:T(8,128)S(1)}, f32[8,16,128]{2,1,0:T(8,128)S(1)}, u32[]{:S(2)}, u32[]{:S(2)}) collective-permute-start(f32[8,16,128]{2,1,0:T(8,128)S(1)} %add.9), channel_id=1, source_target_pairs={{0,2},{2,0},{1,3},{3,1},{4,6},{6,4},{5,7},{7,5},{8,10},{10,8},{9,1... | collective-permute-start | bytes 196616 | tf_op jit(solution)/shard_map/ppermute | solution.py:580
  49.3 11.6 %collective-permute-start.6 = (f32[7,40,128]{2,1,0:T(8,128)S(1)}, f32[7,40,128]{2,1,0:T(8,128)S(1)}, u32[]{:S(2)}, u32[]{:S(2)}) collective-permute-start(f32[7,40,128]{2,1,0:T(8,128)S(1)} %get-tuple-element.61), channel_id=1, source_target_pairs={{0,4},{4,0},{8,12},{12,8},{1,5},{5,1},{9,13},{13,9},{2,6},{6,2},{1... | collective-permute-start | bytes 430088 | tf_op jit(solution)/shard_map/ppermute | solution.py:627
  53.7 7.2 %collective-permute-start.7 = (f32[7,40,128]{2,1,0:T(8,128)S(1)}, f32[7,40,128]{2,1,0:T(8,128)S(1)}, u32[]{:S(2)}, u32[]{:S(2)}) collective-permute-start(f32[7,40,128]{2,1,0:T(8,128)S(1)} %get-tuple-element.62), channel_id=1, source_target_pairs={{4,8},{8,4},{5,9},{9,5},{6,10},{10,6},{7,11},{11,7},{20,24},{24,20... | collective-permute-start | bytes 430088 | tf_op jit(solution)/shard_map/ppermute | solution.py:627
  54.4 10.8 %collective-permute-start.10 = (f32[2,8,16,128]{3,2,1,0:T(8,128)S(1)}, f32[2,8,16,128]{3,2,1,0:T(8,128)S(1)}, u32[]{:S(2)}, u32[]{:S(2)}) collective-permute-start(f32[2,8,16,128]{3,2,1,0:T(8,128)S(1)} %pad_maximum_fusion.r_15_), channel_id=1, source_target_pairs={{0,4},{4,0},{8,12},{12,8},{1,5},{5,1},{9,13},{13,9},{2,6},{6,2},{1... | collective-permute-start | bytes 393224 | tf_op jit(solution)/shard_map/ppermute | solution.py:583
  57.4 7.8 %collective-permute-start.11 = (f32[2,8,16,128]{3,2,1,0:T(8,128)S(1)}, f32[2,8,16,128]{3,2,1,0:T(8,128)S(1)}, u32[]{:S(2)}, u32[]{:S(2)}) collective-permute-start(f32[2,8,16,128]{3,2,1,0:T(8,128)S(1)} %pad_maximum_fusion.r_15_), channel_id=1, source_target_pairs={{4,8},{8,4},{5,9},{9,5},{6,10},{10,6},{7,11},{11,7},{20,24},{24,20... | collective-permute-start | bytes 393224 | tf_op jit(solution)/shard_map/ppermute | solution.py:583
  58.1 7.1 %collective-permute-start.12 = (f32[2,2,16,128]{3,2,1,0:T(8,128)S(1)}, f32[2,2,16,128]{3,2,1,0:T(8,128)S(1)}, u32[]{:S(2)}, u32[]{:S(2)}) collective-permute-start(f32[2,2,16,128]{3,2,1,0:T(8,128)S(1)} %fusion), channel_id=1, source_target_pairs={{0,8},{8,0},{4,12},{12,4},{1,9},{9,1},{5,13},{13,5},{2,10},{10,2},... | collective-permute-start | bytes 98312 | tf_op jit(solution)/shard_map/ppermute | solution.py:587

commit v6 on v5

v6 whole, which is shorter than its diff:
```python
import jax
import jax.numpy as jnp
from jax import lax
from jax.experimental import pallas as pl
from jax.experimental.pallas import tpu as pltpu
from jax.sharding import PartitionSpec as P

SWEEPS = 2
BOTTOM_SWEEPS = 8

floor_conduct = 0.1
relax_weight = 0.8

XH = 8
YH = 16
GX = 6
DC, DG = 6, 5
ZW = 16
L2X = 10
F32 = jnp.float32
BF16 = jnp.bfloat16
MIB = 1 << 20


def exchanges(count, step=1):
    swaps = []
    for e in range(2):
        pairs = []
        for i in range(count):
            if (i // step + e) % 2 == 0 and i + step < count:
                pairs += [(i, i + step), (i + step, i)]
        if pairs:
            swaps.append(pairs)
    return swaps


def upward(index, e, step=1):
    return (index // step + e) % 2 == 0


def spec(shape):
    return jax.ShapeDtypeStruct(shape, F32)


def in_vmem(shape):
    return pltpu.VMEM(shape, F32)


def in_hbm(shape):
    return pltpu.HBM(shape, F32)


def held(x):
    return pltpu.with_memory_space_constraint(x, pltpu.VMEM)


def params(mib):
    return pltpu.CompilerParams(vmem_limit_bytes=mib * MIB)


def roll_up(v, axis):
    return pltpu.roll(v, v.shape[axis] - 1, axis)


def roll_down(v, axis):
    return pltpu.roll(v, 1, axis)


def next_z(v):
    half = v.shape[1] // 2
    if half < 128:
        return roll_up(v, 1)
    return jnp.concatenate([v[:, half:], roll_up(v[:, :half], 1)], axis=1)


def previous_z(v):
    half = v.shape[1] // 2
    if half < 128:
        return roll_down(v, 1)
    return jnp.concatenate([roll_down(v[:, half:], 1), v[:, :half]], axis=1)


def pick(v, lanes):
    return jnp.take_along_axis(v, lanes, axis=1)


def parted(v):
    lane = iota2(v.shape, 1)
    even = lax.rem(2 * lane, v.shape[1])
    return jnp.concatenate([pick(v, even), pick(v, even + 1)], axis=1)


def joining(shape):
    lane = iota2(shape, 1)
    return lax.rem(lane, 2) == 0, lax.div(lane, 2)


def joined(v, even, at):
    half = v.shape[1] // 2
    return jnp.where(even, pick(v[:, :half], at), pick(v[:, half:], at))


def loop(low, high, body, init=None, unroll=1):
    def step(i, carry):
        if init is None:
            body(i)
            return carry
        return body(i, carry)

    carry = 0 if init is None else init
    whole = (high - low) // unroll
    if whole > 1:

        def several(k, carry):
            for j in range(unroll):
                carry = step(low + k * unroll + j, carry)
            return carry

        carry = lax.fori_loop(0, whole, several, carry)
        low += whole * unroll
    for i in range(low, high):
        carry = step(i, carry)
    return carry


def unrolling(ref):
    return UNROLL.get(ref.shape[1] * ref.shape[2] // 1024, 4)


UNROLL = {20: 4, 18: 4, 6: 8, 5: 8, 4: 8}


def coefficients(c, kx, ky, kz, rd, low, high, scale):
    half = 0.5 * scale

    def faces(x):
        cx = c[x]
        fx = half * (cx + c[x + 1])
        fy = half * (cx + roll_up(cx, 0))
        fz = half * (cx + next_z(cx))
        kx[x] = fx
        ky[x] = fy
        kz[x] = fz
        return cx, fx, fy, fz

    _, first, _, _ = faces(low - 1)

    def body(x, before):
        cx, fx, fy, fz = faces(x)
        diagonal = fx + before + fy + roll_down(fy, 0) + fz + previous_z(fz)
        inside = cx > 0.0
        rd[x] = jnp.where(inside, relax_weight / jnp.where(inside, diagonal, 1.0), 0.0)
        return fx

    loop(low, high, body, first, unrolling(rd))


def operate(v, kx, ky, kz, low, high, use):
    def body(x, before):
        vx = v[x]
        fx = kx[x] * (vx - v[x + 1])
        fy = ky[x] * (vx - roll_up(vx, 0))
        fz = kz[x] * (vx - next_z(vx))
        use(x, vx, (fx - before) + (fy - roll_down(fy, 0)) + (fz - previous_z(fz)))
        return fx

    loop(low, high, body, kx[low - 1] * (v[low - 1] - v[low]), unrolling(v))


def sweep(v, out, g, kx, ky, kz, rd, low, high):
    def use(x, vx, av):
        out[x] = vx + rd[x] * (g[x] - av)

    operate(v, kx, ky, kz, low, high, use)


def iota2(shape, dim):
    return lax.broadcasted_iota(jnp.int32, shape, dim)


def conductivity(p):
    return floor_conduct + (1.0 - floor_conduct) * (p * p * p)


def send_kernel(nx, ny, phase, mask, dev, *refs):
    count = nx + ny + nx * ny
    outs = refs[:count]
    px, mx, dx, py, my, dy, sems = refs[count:]
    ox, oy, _ = phase.shape
    ups = [upward(lax.axis_index("boxes"), e) for e in range(nx)]
    rows = [pl.multiple_of(jnp.where(upward(lax.axis_index("sub"), f), oy - YH, 0), 8) for f in range(ny)]
    copies = []
    for f in range(ny):
        for source, out in ((phase, py), (mask, my), (dev, dy)):
            copies.append((source.at[:, pl.ds(rows[f], YH), :], out.at[f]))
    for e in range(nx):
        for source, out, width in ((phase, px, XH), (mask, mx, GX), (dev, dx, GX)):
            copies.append((source.at[pl.ds(jnp.where(ups[e], ox - width, 0), width)], out.at[e]))
    copies = [pltpu.make_async_copy(a, b, sems.at[i]) for i, (a, b) in enumerate(copies)]
    for copy in copies:
        copy.start()
    for copy in copies[:3 * ny]:
        copy.wait()
    for f in range(ny):
        face = outs[nx + f]

        def body(x, face=face, f=f):
            face[0, x] = conductivity(py[f, x])
            face[1, x] = my[f, x].astype(F32) * dy[f, x]

        loop(0, ox, body, unroll=8)
        for e in range(nx):
            corner = outs[nx + ny + e * ny + f]
            corner[0:DC] = face[0, pl.ds(jnp.where(ups[e], ox - DC, 0), DC)]
            corner[DC:DC + DG] = face[1, pl.ds(jnp.where(ups[e], ox - DG, 0), DG)]
    for copy in copies[3 * ny:]:
        copy.wait()
    for e in range(nx):
        for x in range(XH):
            outs[e][x] = conductivity(px[e, x])
        for x in range(GX):
            outs[e][XH + x] = mx[e, x].astype(F32) * dx[e, x]


def pack(planes, turns, lane):
    total = None
    for b, (plane, turn) in enumerate(zip(planes, turns)):
        moved = pltpu.roll(plane, turn, 1)
        total = moved if total is None else jnp.where(lane >= ZW * b, moved, total)
    return total


def strip_turns(oz, start):
    return [lax.rem(ZW * b + oz - start, oz) for b in range(oz // ZW)]


def split(x):
    high = x.astype(BF16)
    rest = x - high.astype(F32)
    middle = rest.astype(BF16)
    low = (rest - middle.astype(F32)).astype(BF16)
    return jnp.concatenate([high, middle, low], axis=-1)


def times(x, matrix):
    return jnp.dot(split(x), matrix, preferred_element_type=F32)


def thrice(matrix):
    return jnp.concatenate([matrix.astype(BF16)] * 3, axis=0)


def compact(planes, out):
    rows, lanes = planes[0].shape
    lane = iota2((rows, lanes), 1)
    for q in range(len(planes) // 4):
        total = planes[4 * q]
        for i in range(1, 4):
            moved = pltpu.roll(planes[4 * q + i], lanes // 4 * i, 1)
            total = jnp.where(lane < lanes // 4 * i, total, moved)
        out[q * rows:(q + 1) * rows, :] = total


def own_kernel(phase, mask, dev, c_out, g_out, strip, c2, c, g, sums, work):
    ox, oy, oz = phase.shape
    pz = lax.axis_index("pair")

    def body(x):
        c[x], g[x] = conductivity(phase[x]), mask[x].astype(F32) * dev[x]
        c_out[x] = parted(c[x])
        g_out[x] = parted(g[x])

    loop(0, ox, body, unroll=4)
    i, j = iota2((oz, oz), 0), iota2((oz, oz), 1)
    matrix = thrice(jnp.where(j == lax.div(i, 4), 1.0 / 64.0, 0.0))
    for x in range(ox // 4):
        sums[...] = (c[4 * x] + c[4 * x + 1]) + (c[4 * x + 2] + c[4 * x + 3])
        part = [sums[pl.ds(k, oy // 4, stride=4), :] for k in range(4)]
        work[x] = (part[0] + part[1]) + (part[2] + part[3])
    done = times(work[...].reshape(-1, oz), matrix)
    compact([done[x * oy // 4:(x + 1) * oy // 4] for x in range(ox // 4)], c2)
    group = oz // ZW
    turns = strip_turns(oz, jnp.where(pz == 0, oz - ZW, 0))
    lane = iota2((oy, oz), 1)
    for which, source in enumerate((c, g)):
        for a in range(ox // group):
            strip[which, a] = pack([source[group * a + b] for b in range(group)], turns, lane)


def halo_rows(ny, f, oy, up):
    if ny == 1:
        return oy
    return jnp.where(up, oy, oy + YH)


def place_halos(nx, ny, box, got, put, between=lambda: None):
    ox, oy, oz = box
    bx = lax.axis_index("boxes")
    sy = lax.axis_index("sub")
    place = 0
    row = iota2((YH, oz), 0)

    def trim(values, up):
        if ny > 1:
            return values
        return jnp.where(lax.div(row, 2) == jnp.where(up, YH // 2 - 1, 0), 0.0, values)

    def below(up, planes):
        return jnp.where(up, XH + ox, XH - planes)

    for e in range(nx):
        up = upward(bx, e)
        face = got[place]
        place += 1
        for x in range(XH):
            put(0, below(up, XH) + x, slice(0, oy), face[x])
        for x in range(GX):
            put(1, below(up, GX) + x, slice(0, oy), face[XH + x])
    between()
    for f in range(ny):
        up = upward(sy, f)
        face = got[place]
        place += 1
        rows = pl.ds(pl.multiple_of(halo_rows(ny, f, oy, up), 8), YH)

        def copy(x, face=face, rows=rows, up=up):
            put(0, XH + x, rows, trim(face[0, x], up))
            put(1, XH + x, rows, trim(face[1, x], up))

        loop(0, ox, copy, unroll=8)
    for e in range(nx):
        ux = upward(bx, e)
        for f in range(ny):
            up = upward(sy, f)
            face = got[place]
            place += 1
            rows = pl.ds(pl.multiple_of(halo_rows(ny, f, oy, up), 8), YH)
            for x in range(DC):
                put(0, below(ux, DC) + x, rows, trim(face[x], up))
            for x in range(DG):
                put(1, below(ux, DG) + x, rows, trim(face[DC + x], up))


def strip_kernel(nx, ny, own, *refs):
    count = nx + ny + nx * ny
    got, (strip, c, g) = refs[:count], refs[count:]
    planes, nrows, oz = c.shape
    oy = own.shape[2]
    ox = planes - 2 * XH
    pz = lax.axis_index("pair")
    for out in (c, g):
        for low, high in ((0, XH), (XH + ox, planes)):
            out[low:high, oy:, :] = jnp.zeros((high - low, nrows - oy, oz), F32)
    for low, high in ((0, XH - GX), (XH + ox + GX, planes)):
        g[low:high, 0:oy, :] = jnp.zeros((high - low, oy, oz), F32)

    def put(which, plane, rows, values):
        (c, g)[which][plane, rows, :] = values

    place_halos(nx, ny, (ox, oy, oz), got, put)
    group = oz // ZW
    turns = strip_turns(oz, jnp.where(pz == 0, oz - ZW, 0))
    packed = planes // group
    side = XH // group
    for which, source in enumerate((c, g)):
        for a in range(packed):
            at = which * packed + a
            if side <= a < packed - side:
                strip[at, 0:oy, :] = own[which, a - side]
                rows = slice(oy, nrows)
            else:
                rows = slice(0, nrows)
            lane = iota2((nrows - (rows.start or 0), oz), 1)
            strip[at, rows, :] = pack([source[group * a + b, rows, :] for b in range(group)], turns, lane)


def join_kernel(nx, ny, *refs):
    count = nx + ny + nx * ny
    got, outs, (cx, gx, cy, gy, sems) = refs[:count], refs[count:count + 4], refs[count + 4:]
    copies = [pltpu.make_async_copy(a, b, sems.at[i]) for i, (a, b) in enumerate(zip((cx, gx, cy, gy), outs))]
    planes, nrows, lanes = cy.shape
    ox, oy = planes - 2 * XH, cx.shape[1]
    for low, high in ((0, XH), (XH + ox, planes)):
        for out in (cy, gy):
            out[low:high] = jnp.zeros((high - low, nrows, lanes), F32)
    for low, high in ((0, XH - GX), (XH + GX, 2 * XH)):
        gx[low:high] = jnp.zeros((high - low, oy, lanes), F32)

    def put(which, plane, rows, values):
        if isinstance(rows, slice):
            (cx, gx)[which][jnp.where(plane < XH, plane, plane - ox)] = parted(values)
        else:
            (cy, gy)[which][plane, pl.ds(pl.multiple_of(rows.start - oy, 8), rows.size), :] = parted(values)

    def begin():
        copies[0].start()
        copies[1].start()

    place_halos(nx, ny, (ox, oy, lanes // 2), got, put, begin)
    copies[2].start()
    copies[3].start()
    for copy in copies:
        copy.wait()


def halve(total, work):
    work[...] = total
    return work[pl.ds(0, total.shape[0] // 2, stride=2), :] + work[pl.ds(1, total.shape[0] // 2, stride=2), :]


def pool_wide(source, low, high, out, work):
    step, _, width = work.shape

    def body(k):
        for j in range(step):
            total = source[2 * (low + step * k + j)] + source[2 * (low + step * k + j) + 1]
            out[step * k + j] = 0.125 * halve(total[:, :width] + total[:, width:], work.at[j])

    loop(0, (high - low) // step, body)


def pool(source, low, high, out, matrix, work):
    sums = [halve(source(2 * j) + source(2 * j + 1), work.at[j - low]) for j in range(low, high)]
    out[...] = times(jnp.concatenate(sums, axis=0), matrix).reshape(out.shape)


def pool_matrix(size_in, size_out, limit, shift, weight):
    i, j = iota2((size_in, size_out), 0), iota2((size_in, size_out), 1)
    return thrice(jnp.where((i < limit) & (j == shift + lax.div(i, 2)), weight, 0.0))


KEPT, FINE = 10, 3
SKIP = XH - 3
YN = 8


def near_rows(ny, oy):
    if ny > 1:
        return oy, oy + 2 * YH - YN
    return (pl.multiple_of(jnp.where(upward(lax.axis_index("sub"), 0), oy, oy + YH - YN), 8),)


def inner(ny, ref, out):
    planes = pl.ds(SKIP, out.shape[0])
    oy = out.shape[1] - ny * YN
    parts = [(ref.at[planes, pl.ds(0, oy), :], out.at[:, pl.ds(0, oy), :])]
    for f, start in enumerate(near_rows(ny, oy)):
        parts.append((ref.at[planes, pl.ds(start, YN), :], out.at[:, pl.ds(oy + f * YN, YN), :]))
    return parts


def down_kernel(nx, ny, c_own, g_own, cx, gx, cy, gy, strip, c2, *refs):
    kept, f2 = refs[:KEPT], refs[KEPT]
    faces = refs[KEPT + 1:KEPT + 1 + nx]
    held_here = refs[KEPT + 1 + nx:2 * KEPT + 1 + nx]
    c, g, u0, kx1, ky1, kz1, rd1, c1, f1, u1 = held_here
    kx, ky, kz, rd, first, v1, work, work1, low2, sems, arrivals = refs[2 * KEPT + 1 + nx:]
    pairs = []
    for a, k in zip(held_here[:FINE], kept):
        pairs += inner(ny, a, k)
    pairs += list(zip(held_here[FINE:], kept[FINE:]))
    copies = [pltpu.make_async_copy(a, k, sems.at[i]) for i, (a, k) in enumerate(pairs)]
    planes, rows, lanes = c.shape
    oz = lanes // 2
    oy = cx.shape[1]
    pz = lax.axis_index("pair")
    bx = lax.axis_index("boxes")
    group = oz // ZW
    wide = ZW // 2
    packed = planes // group
    lane = iota2((rows, oz), 1)
    start = jnp.where(pz == 0, oz // 2, oz - wide)
    own = lane < oz // 2
    near = (lane >= start) & (lane < start + wide)
    order = lax.rem(lane, oz // 2)
    order = ZW * lax.div(order, wide) + 2 * lax.rem(order, wide) + lax.div(lane, oz // 2)

    last = packed - 1

    def arriving(a, beside, which):
        out, own_planes, x_planes, y_rows = ((c, c_own, cx, cy), (g, g_own, gx, gy))[which]
        here = pl.ds(a * group, group)
        source = own_planes.at[pl.ds(0, group)]
        if beside:
            source = x_planes.at[pl.ds(a // last * group, group)]
        elif beside is False:
            source = own_planes.at[pl.ds((a - 1) * group, group)]
        return (
            pltpu.make_async_copy(source, out.at[here, pl.ds(0, oy), :], arrivals.at[4 * a + 2 * which]),
            pltpu.make_async_copy(
                y_rows.at[here], out.at[here, pl.ds(oy, rows - oy), :], arrivals.at[4 * a + 2 * which + 1]
            ),
        )

    for a in range(packed):
        for which in range(2):
            for copy in arriving(a, a in (0, last), which):
                copy.start()

    def unpack(a):
        for which, (strips, out) in enumerate(((strip[a], c), (strip[packed + a], g))):
            for copy in arriving(a, None, which):
                copy.wait()
            strips = pick(strips, order)
            for b in range(group):
                x = group * a + b
                for h in range(2):
                    cols = slice(h * oz, h * oz + oz)
                    turn = lax.rem(start + (3 - h) * (oz // 2) + oz // 2 - wide * b, oz)
                    far = jnp.where(near, pltpu.roll(strips, turn, 1), 0.0)
                    out[x, :, cols] = jnp.where(own, out[x, :, cols], far)

    loop(0, packed, unpack)
    parts = 1 + ny
    for copy in copies[:2 * parts]:
        copy.start()
    edge = XH - GX
    coefficients(c, kx, ky, kz, rd, edge, planes - edge, 1.0)

    def start_sweep(x):
        first[x] = g[x] * rd[x]

    loop(edge, planes - edge, start_sweep)
    sweep(first, u0, g, kx, ky, kz, rd, edge + 1, planes - edge - 1)
    for copy in copies[2 * parts:3 * parts]:
        copy.start()
    rest = first

    def use(x, vx, av):
        rest[x] = g[x] - av

    operate(u0, kx, ky, kz, edge + 2, planes - edge - 2, use)
    planes1 = planes // 2
    pool_wide(c, 0, planes1, c1, work)
    f1[...] = jnp.zeros_like(f1)
    low1 = (edge + 2) // 2
    high1 = planes1 - low1
    pool_wide(rest, low1, high1, f1.at[low1:high1], work)
    coefficients(c1, kx1, ky1, kz1, rd1, 1, planes1 - 1, 0.25)

    def start_sweep1(x):
        v1[x] = f1[x] * rd1[x]

    loop(low1, high1, start_sweep1)
    u1[...] = jnp.zeros_like(u1)
    sweep(v1, u1, f1, kx1, ky1, kz1, rd1, low1 + 1, high1 - 1)
    for copy in copies[3 * parts:]:
        copy.start()
    h1 = XH // 2
    o1 = planes1 - XH

    def use1(x, vx, av):
        v1[x] = f1[x] - av

    operate(u1, kx1, ky1, kz1, h1, planes1 - h1, use1)
    half = oz // 2
    matrix1 = pool_matrix(oz, oz, half, 0, 0.125)
    own1 = 2 * low2.shape[1]
    pool(lambda x: v1[x, 0:own1, :], h1 // 2, (planes1 - h1) // 2, low2, matrix1, work1)
    tile = c2.shape[0]
    compact([low2[x] for x in range(low2.shape[0])], f2.at[0:tile])
    f2[tile:] = c2[...]
    for e in range(nx):
        up = upward(bx, e)
        faces[e][0:h1] = u1[pl.ds(jnp.where(up, o1, h1), h1)]
        faces[e][h1:2 * h1 - 1] = f1[pl.ds(jnp.where(up, o1 + 1, h1), h1 - 1)]
    for copy in copies:
        copy.wait()


def bottom_kernel(nx, ny, nfar, c_in, g_in, u_in, *refs):
    pieces = 1 + nx + nfar
    got = refs[:pieces]
    add, c, g, u0, kx, ky, kz, rd = refs[pieces:pieces + 8]
    c2, f2, kx2, ky2, kz2, rd2, v2, w2, tall, sems = refs[pieces + 8:]
    copies = [
        pltpu.make_async_copy(a, b, sems.at[i]) for i, (a, b) in enumerate(((c_in, c), (g_in, g), (u_in, u0)))
    ]
    for copy in copies:
        copy.start()
    planes, rows, lanes = u0.shape
    planes2, rows2, oz = c2.shape
    oy = rows - ny * YN
    o2x, o2y = (planes2 - 2 * L2X), oy // 4
    bx = lax.axis_index("boxes")
    sy = lax.axis_index("sub")
    pz = lax.axis_index("pair")

    lane = iota2((o2y, oz), 1)
    row = iota2((o2y, oz), 0)
    quarter = oz // 4
    nsub = lax.axis_size("sub")
    places = [(L2X, got[0], range(o2x), None)]
    for e in range(nx):
        places.append((jnp.where(upward(bx, e), L2X + o2x, L2X - o2x), got[1 + e], range(o2x), None))
    for e in range(nfar):
        far = upward(bx, e, 2)
        places.append((jnp.where(far, L2X + 2 * o2x, 0), got[1 + nx + e], range(L2X - o2x), far))
    for f in range(ny + 1):
        y0, side, keep = 0, sy, lane < 2 * quarter
        if f > 0:
            up = upward(sy, f - 1)
            y0 = pl.multiple_of(jnp.where(up, o2y, rows2 - o2y), 8)
            side = jnp.where(up, sy + 1, sy - 1)
            keep = keep & (side >= 0) & (side < nsub)
            if ny == 1:
                keep = keep & (row != jnp.where(up, o2y - 1, 0))
        side = 2 * jnp.clip(side, 0, nsub - 1)
        for x0, message, count, far in places:
            for j in count:
                for which, out in enumerate((f2, c2)):
                    if far is None:
                        tiles = [message[side + p, which, j // 4] for p in range(2)]
                        turns = [(quarter * (p - j)) % oz for p in range(2)]
                    else:
                        tiles = [message[side + p, which] for p in range(2)]
                        at = jnp.where(far, j, o2x - (L2X - o2x) + j)
                        turns = [lax.rem(quarter * (p + o2x - at), oz) for p in range(2)]
                    low, high = (pltpu.roll(tile, turn, 1) for tile, turn in zip(tiles, turns))
                    out[x0 + j, pl.ds(y0, o2y), :] = jnp.where(keep, jnp.where(lane < quarter, low, high), 0.0)
    coefficients(c2, kx2, ky2, kz2, rd2, 1, planes2 - 1, 0.0625)

    def start_sweep2(x):
        v2[x] = f2[x] * rd2[x]

    loop(1, planes2 - 1, start_sweep2)
    old, new = v2, w2
    for k in range(2, BOTTOM_SWEEPS + 1):
        sweep(old, new, f2, kx2, ky2, kz2, rd2, k, planes2 - k)
        old, new = new, old

    i, j = iota2((oz, oz), 0), iota2((oz, oz), 1)
    spread_z = thrice(jnp.where(i == lax.div(lax.rem(pz * (oz // 2) + j, oz), 2), 1.0, 0.0))
    count, rows1, _ = add.shape
    base = (planes2 - count) // 2
    moved = times(old[base:base + count].reshape(count * rows2, oz), spread_z)
    row = iota2((8, oz), 0)
    for x in range(count):
        t = moved[x * rows2:x * rows2 + rows2]
        if ny == 1:
            halo = jnp.where(upward(sy, 0), t[o2y:o2y + 8], pltpu.roll(t[rows2 - 8:], 4, 0))
        else:
            halo = jnp.where(row < 4, t[o2y:o2y + 8], t[rows2 - 8:])
        t = jnp.concatenate([t[0:o2y], halo], axis=0)
        tall[x, pl.ds(0, o2y + 8, stride=2), :] = t
        tall[x, pl.ds(1, o2y + 8, stride=2), :] = t
        add[x] = tall[x, 0:rows1, :]

    copies[0].wait()
    row = iota2((YN, lanes), 0)

    def close(x):
        c[x, oy:, :] = jnp.where(row == jnp.where(upward(sy, 0), YN - 1, 0), 0.0, c[x, oy:, :])

    if ny == 1:
        loop(0, planes, close, unroll=2)
    coefficients(c, kx, ky, kz, rd, 1, planes - 1, 1.0)
    for copy in copies[1:]:
        copy.wait()


def up_kernel(nx, ny, add, c, g, u0, kx, ky, kz, rd, *refs):
    faces, (kx1, ky1, kz1, rd1, c1, f1, u1) = refs[:nx], refs[nx:nx + 7]
    field, residual = refs[nx + 7:nx + 9]
    ua, ub, v1, w1, x1, wide = refs[nx + 9:]
    planes, rows, lanes = u0.shape
    planes1, rows1, oz = u1.shape
    oy = field.shape[1]
    bx = lax.axis_index("boxes")

    h1 = XH // 2
    for x in range(planes1):
        v1[x] = jnp.where(c1[x] > 0.0, u1[x] + add[x // 2], 0.0)
        w1[x] = f1[x]
    for e in range(nx):
        up = upward(bx, e)
        for x in range(h1):
            at = jnp.where(up, planes1 - h1, 0) + x
            v1[at] = jnp.where(c1[at] > 0.0, faces[e][x] + add[lax.div(at, 2)], 0.0)
        for x in range(h1 - 1):
            w1[jnp.where(up, planes1 - h1, 1) + x] = faces[e][h1 + x]
    sweep(v1, x1, w1, kx1, ky1, kz1, rd1, 1, planes1 - 1)
    sweep(x1, v1, w1, kx1, ky1, kz1, rd1, 2, planes1 - 2)

    step = wide.shape[0]
    low = (SKIP + 1) // 2

    def spread0(x, m, fine):
        wide[m, pl.ds(0, rows1, stride=2), :] = v1[x]
        wide[m, pl.ds(1, rows1, stride=2), :] = v1[x]
        moved = [wide[m, 0:oy]] + [wide[m, pl.ds(start, YN)] for start in near_rows(ny, oy)]
        moved = jnp.concatenate(moved, axis=0)
        moved = jnp.concatenate([moved, moved], axis=1)
        for y in fine:
            ua[y] = jnp.where(c[y] > 0.0, u0[y] + moved, 0.0)

    def several(n):
        for m in range(step):
            x = low + step * n + m
            spread0(x, m, (2 * x - SKIP, 2 * x + 1 - SKIP))

    loop(0, (planes1 - 2 * low) // step, several)
    spread0(low - 1, 0, (0,))
    spread0(planes1 - low, 1, (planes - 1,))
    sweep(ua, ub, g, kx, ky, kz, rd, 1, planes - 1)
    sweep(ub, ua, g, kx, ky, kz, rd, 2, planes - 2)
    order = joining((oy, oz))

    def use(x, vx, av):
        field[x - 3] = joined(vx[0:oy], *order)
        residual[x - 3] = joined(g[x, 0:oy, :] - av[0:oy], *order)

    operate(ua, kx, ky, kz, 3, planes - 3, use)


def call(kernel, outs, scratch=(), mib=16, raw_in=0, raw_out=0, copies=0, more=0):
    where = [pl.BlockSpec(memory_space=pltpu.HBM)], [pl.BlockSpec(memory_space=pltpu.VMEM)]
    outs = tuple(pltpu.HBM(o.shape, o.dtype) if i < raw_out else o for i, o in enumerate(outs))
    extra = tuple(pltpu.SemaphoreType.DMA((n,)) for n in (copies, more) if n)

    def run(*operands):
        operands = [pltpu.with_memory_space_constraint(x, pltpu.HBM) if i < raw_in else x for i, x in enumerate(operands)]
        return pl.pallas_call(
            kernel,
            in_specs=where[0] * raw_in + where[1] * (len(operands) - raw_in),
            out_specs=tuple(where[0] * raw_out + where[1] * (len(outs) - raw_out)),
            out_shape=outs,
            scratch_shapes=tuple(s if hasattr(s, "memory_space") else pltpu.VMEM(s, F32) for s in scratch) + extra,
            compiler_params=params(mib),
        )(*operands)

    return run


def per_device(phase, target_mask, deviation):
    ox, oy, oz = phase.shape
    nbox, nsub = lax.axis_size("boxes"), lax.axis_size("sub")
    swap_x, swap_y, far_x = exchanges(nbox), exchanges(nsub), exchanges(nbox, 2)
    nx, ny, nfar = len(swap_x), len(swap_y), len(far_x)
    pair_swap = [(0, 1), (1, 0)]

    def both(px, py):
        return [(a * nsub + c, b * nsub + d) for a, b in px for c, d in py]

    def traded(faces):
        out = []
        for e in range(nx):
            out.append(lax.ppermute(faces[e], "boxes", swap_x[e]))
        for f in range(ny):
            out.append(lax.ppermute(faces[nx + f], "sub", swap_y[f]))
        for e in range(nx):
            for f in range(ny):
                out.append(lax.ppermute(faces[nx + ny + e * ny + f], ("boxes", "sub"), both(swap_x[e], swap_y[f])))
        return out

    planes, rows = ox + 2 * XH, oy + YH * ny
    planes1, rows1 = planes // 2, rows // 2
    o2x, o2y = ox // 4, oy // 4
    planes2 = o2x + 2 * L2X
    rows2 = o2y * (ny + 1)

    box = spec((ox, oy, oz))
    faces = [spec((XH + GX, oy, oz))] * nx + [spec((2, ox, YH, oz))] * ny + [spec((DC + DG, YH, oz))] * (nx * ny)
    width, edge = (nx, GX, oy, oz), (ny, ox, YH, oz)
    faces = call(
        lambda *r: send_kernel(nx, ny, *r),
        faces,
        [(nx, XH, oy, oz), pltpu.VMEM(width, jnp.int32), width, edge, pltpu.VMEM(edge, jnp.int32), edge],
        raw_in=3,
        copies=3 * (nx + ny),
    )(phase, target_mask, deviation)
    got = traded(faces)
    phase, target_mask, deviation, _ = lax.optimization_barrier((phase, target_mask, deviation, faces))
    group = oz // ZW
    padded = (planes, rows, oz)
    fine = (planes, rows, 2 * oz)
    parted_box = in_hbm((ox, oy, 2 * oz))
    c, g, own, c2 = call(
        own_kernel,
        [parted_box, parted_box, spec((2, ox // group, oy, oz)), spec((o2x // 4 * o2y, oz))],
        [(ox, oy, oz), (ox, oy, oz), (oy, oz), (o2x, o2y, oz)],
    )(phase, target_mask, deviation)
    (strip,) = call(
        lambda *r: strip_kernel(nx, ny, *r), [spec((2 * planes // group, rows, oz))], [padded, padded]
    )(own, *got)
    strip = lax.ppermute(strip, "pair", pair_swap)
    halos = [(2 * XH, oy, 2 * oz)] * 2 + [(planes, rows - oy, 2 * oz)] * 2
    halos = call(lambda *r: join_kernel(nx, ny, *r), [spec(h) for h in halos], halos, raw_out=4, copies=4)(*got)
    middle = (planes1, rows1, oz)
    small = (planes - 2 * SKIP, oy + ny * YN, 2 * oz)
    down = call(
        lambda *r: down_kernel(nx, ny, *r),
        [spec(small)] * FINE + [spec(middle)] * (KEPT - FINE) + [spec((o2x // 2 * o2y, oz))]
        + [spec((XH - 1, rows1, oz))] * nx,
        [fine] * FINE + [middle] * (KEPT - FINE) + [fine] * 5 + [middle, (4, rows, oz), (o2x, oy // 2, oz), (o2x, o2y, oz)],
        mib=48,
        raw_in=6,
        raw_out=KEPT,
        copies=KEPT + FINE * ny,
        more=4 * planes // group,
    )(c, g, *halos, strip, c2)
    kept, f2, sides = down[:KEPT], down[KEPT], down[KEPT + 1:]
    sheet = lax.all_gather(f2, ("sub", "pair")).reshape(-1, 2, o2x // 4, o2y, oz)
    got = [sheet] + [lax.ppermute(sheet, "boxes", p) for p in swap_x]
    for e, p in enumerate(far_x):
        at = jnp.where(upward(lax.axis_index("boxes"), e, 2), o2x // 4 - 1, 0)
        got.append(lax.ppermute(lax.dynamic_index_in_dim(sheet, at, 2, keepdims=False), "boxes", p))
    got, sides = lax.optimization_barrier((got, sides))
    sides = [lax.ppermute(side, "boxes", p) for side, p in zip(sides, swap_x)]
    lowest = (planes2, rows2, oz)
    add, *fine_up = call(
        lambda *r: bottom_kernel(nx, ny, nfar, *r),
        [in_vmem((planes1 // 2, rows1, oz))] + [in_vmem(small)] * 7,
        [lowest] * 8 + [(planes1 // 2, 2 * (o2y + 8), oz)],
        mib=12,
        raw_in=FINE,
        copies=FINE,
    )(*kept[:FINE], *got)
    return tuple(call(
        lambda *r: up_kernel(nx, ny, *r),
        [box, box],
        [small, small, middle, middle, middle, (3, rows, oz)],
        mib=14,
    )(held(add), *[held(x) for x in fine_up], *sides, *kept[FINE:]))


def solution(mesh):
    where = P(("groups", "boxes"), "sub", "pair")
    return jax.shard_map(
        per_device,
        mesh=mesh,
        in_specs=(where, where, where),
        out_specs=(where, where),
        check_vma=False,
    )
```

time: 84.2 us -> 80.2 us (0.952)
  the two profiles are of different devices: /device:TPU:0 before, /device:TPU:8 now
where the time goes in v6:
time: 80.2 us; the launch traced here: 80 us
  Pallas kernels  43.9 us (55%)
  starting transfers between devices  19.3 us (24%)
  waiting for transfers between devices  10.4 us (13%)
  blocking collectives  5.43 us (7%)
  between operations  0.95 us (1%)
    pallas_call x7, Pallas kernels, run(): pl.pallas_call(kernel, in_specs=where[0] * raw_in + where[1] * (len(opera...  43.9 us
    ppermute x2, waiting for transfers between devices, traded(): lax.ppermute(faces[nx + ny + e * ny + f], ('boxes', 'sub'), both(swap_x[e...  5.45 us
    all_gather x1, blocking collectives, per_device(): lax.all_gather(f2, ('sub', 'pair')).reshape(-1, 2, o2x // 4, o2y, oz)  5.43 us
    ppermute x2, starting transfers between devices, per_device(): sides = [lax.ppermute(side, 'boxes', p) for side, p in zip(sides, swap_x)]  5.13 us
    ppermute x2, starting transfers between devices, traded(): out.append(lax.ppermute(faces[e], 'boxes', swap_x[e]))  5.05 us
    ppermute x1, waiting for transfers between devices, per_device(): lax.ppermute(lax.dynamic_index_in_dim(sheet, at, 2, keepdims=False), 'box...  4.94 us
    ppermute x2, starting transfers between devices, per_device(): got = [sheet] + [lax.ppermute(sheet, 'boxes', p) for p in swap_x]  3.7 us
    ppermute x2, starting transfers between devices, traded(): lax.ppermute(faces[nx + ny + e * ny + f], ('boxes', 'sub'), both(swap_x[e...  2.08 us
  transfers between devices with their start and end apart: 11, of which 3 were waited for; matrix products, arithmetic and copies ran while one was open for 0% of the time, Pallas kernels for 17%

profile of v6, /device:TPU:8, one launch (start us, length us, event | category | flops | bytes accessed | tf_op | source)
XLA Modules:
  0.0 80.0 jit_solution(10657721175850313786)
XLA Ops:
  0.7 1.9 %shard_map.50 = (f32[14,64,128]{2,1,0:T(8,128)S(1)}, f32[14,64,128]{2,1,0:T(8,128)S(1)}, f32[2,32,16,128]{3,2,1,0:T(8,128)S(1)}, f32[11,16,128]{2,1,0:T(8,128)S(1)}, f32[11,16,128]{2,1,0:T(8,128)S(1)}) custom-call(f32[32,64,128]{2,1,0:T(8,128)} %phase, s32[32,64,128]{2,1,0:T(8,128)} %mask, f32[32,64,128]{2,1,0:T(8,128)} %dev), custom_call_target="tpu_custom_call" | custom-call | tf_op jit(solution)/shard_map/pallas_call | solution.py:723
  2.5 1.6 %collective-permute-start.2 = (f32[2,32,16,128]{3,2,1,0:T(8,128)S(1)}, f32[2,32,16,128]{3,2,1,0:T(8,128)S(1)}, u32[]{:S(2)}, u32[]{:S(2)}) collective-permute-start(f32[2,32,16,128]{3,2,1,0:T(8,128)S(1)} %get-tuple-element.47), channel_id=1, source_target_pairs={{0,2},{2,0},{1,3},{3,1},{4,6},{6,4},{5,7},{7,5},{8,10},{10,8},{9,1... | collective-permute-start | bytes 1572872 | tf_op jit(solution)/shard_map/ppermute | solution.py:750
  4.1 0.4 collective-permute-start
  4.5 4.6 %collective-permute-start.1 = (f32[14,64,128]{2,1,0:T(8,128)S(1)}, f32[14,64,128]{2,1,0:T(8,128)S(1)}, u32[]{:S(2)}, u32[]{:S(2)}) collective-permute-start(f32[14,64,128]{2,1,0:T(8,128)S(1)} %get-tuple-element.46), channel_id=1, source_target_pairs={{4,8},{8,4},{5,9},{9,5},{6,10},{10,6},{7,11},{11,7},{20,24},{24,20... | collective-permute-start | bytes 1376264 | tf_op jit(solution)/shard_map/ppermute | solution.py:748
  9.1 0.1 collective-permute-start.3
  9.2 2.0 %collective-permute-start.4 = (f32[11,16,128]{2,1,0:T(8,128)S(1)}, f32[11,16,128]{2,1,0:T(8,128)S(1)}, u32[]{:S(2)}, u32[]{:S(2)}) collective-permute-start(f32[11,16,128]{2,1,0:T(8,128)S(1)} %get-tuple-element.49), channel_id=1, source_target_pairs={{4,10},{6,8},{8,6},{10,4},{5,11},{7,9},{9,7},{11,5},{20,26},{22,24... | collective-permute-start | bytes 270344 | tf_op jit(solution)/shard_map/ppermute | solution.py:753
  11.3 4.3 %shard_map.51 = (f32[32,64,256]{2,1,0:T(8,128)}, f32[32,64,256]{2,1,0:T(8,128)}, f32[2,4,64,128]{3,2,1,0:T(8,128)S(1)}, f32[32,128]{1,0:T(8,128)S(1)}) custom-call(f32[32,64,128]{2,1,0:T(8,128)S(1)} %copy-done, s32[32,64,128]{2,1,0:T(8,128)S(1)} %copy-done.1, f32[32,64,128]{2,1,0:T(8,128)S(1)} %copy-done.2), custom_call_target="tpu_custom_call" | custom-call | tf_op jit(solution)/shard_map/pallas_call | solution.py:723
  15.5 2.7 %collective-permute-done.3.r_3_.r_4_ = f32[11,16,128]{2,1,0:T(8,128)S(1)} collective-permute-done((f32[11,16,128]{2,1,0:T(8,128)S(1)}, f32[11,16,128]{2,1,0:T(8,128)S(1)}, u32[]{:S(2)}, u32[]{:S(2)}) %collective-permute-start.3) | collective-permute-done | bytes 90144 | tf_op jit(solution)/shard_map/ppermute | solution.py:753
  18.2 2.7 %collective-permute-done.4.r_4_.r_5_ = f32[11,16,128]{2,1,0:T(8,128)S(1)} collective-permute-done((f32[11,16,128]{2,1,0:T(8,128)S(1)}, f32[11,16,128]{2,1,0:T(8,128)S(1)}, u32[]{:S(2)}, u32[]{:S(2)}) %collective-permute-start.4) | collective-permute-done | bytes 90144 | tf_op jit(solution)/shard_map/ppermute | solution.py:753
  21.0 0.0 collective-permute-done.r_0_.r_1_
  21.0 0.7 shard_map.53
  21.7 0.1 collective-permute-start.5
  21.8 2.9 %shard_map.52 = (f32[16,64,256]{2,1,0:T(8,128)}, f32[16,64,256]{2,1,0:T(8,128)}, f32[48,16,256]{2,1,0:T(8,128)}, f32[48,16,256]{2,1,0:T(8,128)}) custom-call(f32[14,64,128]{2,1,0:T(8,128)S(1)} %collective-permute-done.r_0_.r_1_, f32[14,64,128]{2,1,0:T(8,128)S(1)} %collective-permute-done.1.r_1_.r_2_, ...), custom_call_target="tpu_custom_call" | custom-call | tf_op jit(solution)/shard_map/pallas_call | solution.py:723
  24.7 0.0 collective-permute-done.5.r_6_
  24.8 16.6 %shard_map.54 = (f32[38,72,256]{2,1,0:T(8,128)}, f32[38,72,256]{2,1,0:T(8,128)}, f32[38,72,256]{2,1,0:T(8,128)}, f32[24,40,128]{2,1,0:T(8,128)}, f32[24,40,128]{...) custom-call(f32[32,64,256]{2,1,0:T(8,128)} %get-tuple-element.53.r_0, ...), custom_call_target="tpu_custom_call" | custom-call | tf_op jit(solution)/shard_map/pallas_call | solution.py:723
  41.4 5.4 %all-gather = f32[256,128]{1,0:T(8,128)S(1)} all-gather(f32[64,128]{1,0:T(8,128)S(1)} %get-tuple-element.64), channel_id=2, replica_groups=mesh['groups'=2,'boxes'=4,'sub'=2,'pair'=2] {'sub','pair'}, dimensions={0}, use_global_device_ids=true | all-gather | bytes 163840 | tf_op jit(solution)/shard_map/all_gather | solution.py:803
  46.8 3.6 %collective-permute-start.7 = (f32[4,2,2,16,128]{4,3,2,1,0:T(8,128)S(1)}, f32[4,2,2,16,128]{4,3,2,1,0:T(8,128)S(1)}, u32[]{:S(2)}, u32[]{:S(2)}) collective-permute-start(f32[4,2,2,16,128]{4,3,2,1,0:T(8,128)S(1)} %bitcast.3), channel_id=1, source_target_pairs={{4,8},{8,4},{5,9},{9,5},{6,10},{10,6},{7,11},{11,7},{20,24},{24,20... | collective-permute-start | bytes 393224 | tf_op jit(solution)/shard_map/ppermute | solution.py:804
  50.5 0.1 collective-permute-start.6
  50.6 1.7 %collective-permute-start.8 = (f32[4,2,16,128]{3,2,1,0:T(8,128)S(1)}, f32[4,2,16,128]{3,2,1,0:T(8,128)S(1)}, u32[]{:S(2)}, u32[]{:S(2)}) collective-permute-start(f32[4,2,16,128]{3,2,1,0:T(8,128)S(1)} %dynamic-slice_bitcast_fusion), channel_id=1, source_target_pairs={{0,8},{8,0},{4,12},{12,4},{1,9},{9,1},{5,13},{13,5},{2,10},{10,2},... | collective-permute-start | bytes 196616 | tf_op jit(solution)/shard_map/ppermute | solution.py:807
  52.3 4.9 %collective-permute-done.8.r_6_ = f32[4,2,16,128]{3,2,1,0:T(8,128)S(1)} collective-permute-done((f32[4,2,16,128]{3,2,1,0:T(8,128)S(1)}, f32[4,2,16,128]{3,2,1,0:T(8,128)S(1)}, u32[]{:S(2)}, u32[]{:S(2)}) %collective-permute-start.8) | collective-permute-done | bytes 65568 | tf_op jit(solution)/shard_map/ppermute | solution.py:807
  57.2 1.5 %collective-permute-start.9 = (f32[7,40,128]{2,1,0:T(8,128)S(1)}, f32[7,40,128]{2,1,0:T(8,128)S(1)}, u32[]{:S(2)}, u32[]{:S(2)}) collective-permute-start(f32[7,40,128]{2,1,0:T(8,128)S(1)} %get-tuple-element.79), channel_id=1, source_target_pairs={{0,4},{4,0},{8,12},{12,8},{1,5},{5,1},{9,13},{13,9},{2,6},{6,2},{1... | collective-permute-start | bytes 430088 | tf_op jit(solution)/shard_map/ppermute | solution.py:809
  58.8 3.6 %collective-permute-start.10 = (f32[7,40,128]{2,1,0:T(8,128)S(1)}, f32[7,40,128]{2,1,0:T(8,128)S(1)}, u32[]{:S(2)}, u32[]{:S(2)}) collective-permute-start(f32[7,40,128]{2,1,0:T(8,128)S(1)} %get-tuple-element.80), channel_id=1, source_target_pairs={{4,8},{8,4},{5,9},{9,5},{6,10},{10,6},{7,11},{11,7},{20,24},{24,20... | collective-permute-start | bytes 430088 | tf_op jit(solution)/shard_map/ppermute | solution.py:809
  62.4 6.6 %shard_map.55 = (f32[12,40,128]{2,1,0:T(8,128)S(1)}, f32[38,72,256]{2,1,0:T(8,128)S(1)}, f32[38,72,256]{2,1,0:T(8,128)S(1)}, f32[38,72,256]{2,1,0:T(8,128)S(1)},...) custom-call(f32[38,72,256]{2,1,0:T(8,128)} %get-tuple-element.61.r_0, ...), custom_call_target="tpu_custom_call" | custom-call | tf_op jit(solution)/shard_map/pallas_call | solution.py:723
  69.1 10.9 %shard_map.56 = (f32[32,64,128]{2,1,0:T(8,128)}, f32[32,64,128]{2,1,0:T(8,128)}) custom-call(f32[12,40,128]{2,1,0:T(8,128)S(1)} %get-tuple-element.71.r_0_, f32[38,72,256]{2,1,0:T(8,128)S(1)} %get-tuple-element.72.r_1_, f32[38,72,256]{2,1,0:T(8,128)S(1)} %get-tuple-element.73.r_2_, f32[38,72,256]{2,1,0:T(8,128)S(1)} %get-tuple-element.74.r_3_, ...), custom_call_target="tpu_custom_call" | custom-call | tf_op jit(solution)/shard_map/pallas_call | solution.py:723
  (27 shorter events, 0.1 us)
Async XLA Ops:
  0.6 10.6 %copy-start.2 = (f32[32,64,128]{2,1,0:T(8,128)S(1)}, f32[32,64,128]{2,1,0:T(8,128)}, u32[]{:S(2)}) copy-start(f32[32,64,128]{2,1,0:T(8,128)} %dev) | copy-start | bytes 3145732
  0.6 10.6 %copy-start.1 = (s32[32,64,128]{2,1,0:T(8,128)S(1)}, s32[32,64,128]{2,1,0:T(8,128)}, u32[]{:S(2)}) copy-start(s32[32,64,128]{2,1,0:T(8,128)} %mask) | copy-start | bytes 3145732
  0.6 10.6 %copy-start = (f32[32,64,128]{2,1,0:T(8,128)S(1)}, f32[32,64,128]{2,1,0:T(8,128)}, u32[]{:S(2)}) copy-start(f32[32,64,128]{2,1,0:T(8,128)} %phase) | copy-start | bytes 3145732
  2.5 18.5 %collective-permute-start.2 = (f32[2,32,16,128]{3,2,1,0:T(8,128)S(1)}, f32[2,32,16,128]{3,2,1,0:T(8,128)S(1)}, u32[]{:S(2)}, u32[]{:S(2)}) collective-permute-start(f32[2,32,16,128]{3,2,1,0:T(8,128)S(1)} %get-tuple-element.47), channel_id=1, source_target_pairs={{0,2},{2,0},{1,3},{3,1},{4,6},{6,4},{5,7},{7,5},{8,10},{10,8},{9,1... | collective-permute-start | bytes 1572872 | tf_op jit(solution)/shard_map/ppermute | solution.py:750
  4.1 16.9 %collective-permute-start = (f32[14,64,128]{2,1,0:T(8,128)S(1)}, f32[14,64,128]{2,1,0:T(8,128)S(1)}, u32[]{:S(2)}, u32[]{:S(2)}) collective-permute-start(f32[14,64,128]{2,1,0:T(8,128)S(1)} %get-tuple-element.45), channel_id=1, source_target_pairs={{0,4},{4,0},{8,12},{12,8},{1,5},{5,1},{9,13},{13,9},{2,6},{6,2},{1... | collective-permute-start | bytes 1376264 | tf_op jit(solution)/shard_map/ppermute | solution.py:748
  4.5 16.5 %collective-permute-start.1 = (f32[14,64,128]{2,1,0:T(8,128)S(1)}, f32[14,64,128]{2,1,0:T(8,128)S(1)}, u32[]{:S(2)}, u32[]{:S(2)}) collective-permute-start(f32[14,64,128]{2,1,0:T(8,128)S(1)} %get-tuple-element.46), channel_id=1, source_target_pairs={{4,8},{8,4},{5,9},{9,5},{6,10},{10,6},{7,11},{11,7},{20,24},{24,20... | collective-permute-start | bytes 1376264 | tf_op jit(solution)/shard_map/ppermute | solution.py:748
  9.1 9.1 %collective-permute-start.3 = (f32[11,16,128]{2,1,0:T(8,128)S(1)}, f32[11,16,128]{2,1,0:T(8,128)S(1)}, u32[]{:S(2)}, u32[]{:S(2)}) collective-permute-start(f32[11,16,128]{2,1,0:T(8,128)S(1)} %get-tuple-element.48), channel_id=1, source_target_pairs={{0,6},{2,4},{4,2},{6,0},{8,14},{10,12},{12,10},{14,8},{1,7},{3,5},... | collective-permute-start | bytes 270344 | tf_op jit(solution)/shard_map/ppermute | solution.py:753
  9.2 11.8 %collective-permute-start.4 = (f32[11,16,128]{2,1,0:T(8,128)S(1)}, f32[11,16,128]{2,1,0:T(8,128)S(1)}, u32[]{:S(2)}, u32[]{:S(2)}) collective-permute-start(f32[11,16,128]{2,1,0:T(8,128)S(1)} %get-tuple-element.49), channel_id=1, source_target_pairs={{4,10},{6,8},{8,6},{10,4},{5,11},{7,9},{9,7},{11,5},{20,26},{22,24... | collective-permute-start | bytes 270344 | tf_op jit(solution)/shard_map/ppermute | solution.py:753
  21.7 3.0 %collective-permute-start.5 = (f32[12,80,128]{2,1,0:T(8,128)S(1)}, f32[12,80,128]{2,1,0:T(8,128)S(1)}, u32[]{:S(2)}, u32[]{:S(2)}) collective-permute-start(f32[12,80,128]{2,1,0:T(8,128)S(1)} %shard_map.53), channel_id=1, source_target_pairs={{0,1},{1,0},{2,3},{3,2},{4,5},{5,4},{6,7},{7,6},{8,9},{9,8},{10,11... | collective-permute-start | bytes 1474568 | tf_op jit(solution)/shard_map/ppermute | solution.py:786
  46.8 10.4 %collective-permute-start.7 = (f32[4,2,2,16,128]{4,3,2,1,0:T(8,128)S(1)}, f32[4,2,2,16,128]{4,3,2,1,0:T(8,128)S(1)}, u32[]{:S(2)}, u32[]{:S(2)}) collective-permute-start(f32[4,2,2,16,128]{4,3,2,1,0:T(8,128)S(1)} %bitcast.3), channel_id=1, source_target_pairs={{4,8},{8,4},{5,9},{9,5},{6,10},{10,6},{7,11},{11,7},{20,24},{24,20... | collective-permute-start | bytes 393224 | tf_op jit(solution)/shard_map/ppermute | solution.py:804
  50.5 6.8 %collective-permute-start.6 = (f32[4,2,2,16,128]{4,3,2,1,0:T(8,128)S(1)}, f32[4,2,2,16,128]{4,3,2,1,0:T(8,128)S(1)}, u32[]{:S(2)}, u32[]{:S(2)}) collective-permute-start(f32[4,2,2,16,128]{4,3,2,1,0:T(8,128)S(1)} %bitcast.4), channel_id=1, source_target_pairs={{0,4},{4,0},{8,12},{12,8},{1,5},{5,1},{9,13},{13,9},{2,6},{6,2},{1... | collective-permute-start | bytes 393224 | tf_op jit(solution)/shard_map/ppermute | solution.py:804
  50.6 6.7 %collective-permute-start.8 = (f32[4,2,16,128]{3,2,1,0:T(8,128)S(1)}, f32[4,2,16,128]{3,2,1,0:T(8,128)S(1)}, u32[]{:S(2)}, u32[]{:S(2)}) collective-permute-start(f32[4,2,16,128]{3,2,1,0:T(8,128)S(1)} %dynamic-slice_bitcast_fusion), channel_id=1, source_target_pairs={{0,8},{8,0},{4,12},{12,4},{1,9},{9,1},{5,13},{13,5},{2,10},{10,2},... | collective-permute-start | bytes 196616 | tf_op jit(solution)/shard_map/ppermute | solution.py:807
  57.2 11.8 %collective-permute-start.9 = (f32[7,40,128]{2,1,0:T(8,128)S(1)}, f32[7,40,128]{2,1,0:T(8,128)S(1)}, u32[]{:S(2)}, u32[]{:S(2)}) collective-permute-start(f32[7,40,128]{2,1,0:T(8,128)S(1)} %get-tuple-element.79), channel_id=1, source_target_pairs={{0,4},{4,0},{8,12},{12,8},{1,5},{5,1},{9,13},{13,9},{2,6},{6,2},{1... | collective-permute-start | bytes 430088 | tf_op jit(solution)/shard_map/ppermute | solution.py:809
  58.8 10.3 %collective-permute-start.10 = (f32[7,40,128]{2,1,0:T(8,128)S(1)}, f32[7,40,128]{2,1,0:T(8,128)S(1)}, u32[]{:S(2)}, u32[]{:S(2)}) collective-permute-start(f32[7,40,128]{2,1,0:T(8,128)S(1)} %get-tuple-element.80), channel_id=1, source_target_pairs={{4,8},{8,4},{5,9},{9,5},{6,10},{10,6},{7,11},{11,7},{20,24},{24,20... | collective-permute-start | bytes 430088 | tf_op jit(solution)/shard_map/ppermute | solution.py:809
  62.4 6.7 %copy-start.3 = (f32[24,40,128]{2,1,0:T(8,128)S(1)}, f32[24,40,128]{2,1,0:T(8,128)}, u32[]{:S(2)}) copy-start(f32[24,40,128]{2,1,0:T(8,128)} %get-tuple-element.81.r_10_) | copy-start | bytes 1474564
  62.4 6.7 %copy-start.4 = (f32[24,40,128]{2,1,0:T(8,128)S(1)}, f32[24,40,128]{2,1,0:T(8,128)}, u32[]{:S(2)}) copy-start(f32[24,40,128]{2,1,0:T(8,128)} %get-tuple-element.82.r_11_) | copy-start | bytes 1474564
  62.4 6.7 %copy-start.5 = (f32[24,40,128]{2,1,0:T(8,128)S(1)}, f32[24,40,128]{2,1,0:T(8,128)}, u32[]{:S(2)}) copy-start(f32[24,40,128]{2,1,0:T(8,128)} %get-tuple-element.83.r_12_) | copy-start | bytes 1474564
  62.4 6.7 %copy-start.6 = (f32[24,40,128]{2,1,0:T(8,128)S(1)}, f32[24,40,128]{2,1,0:T(8,128)}, u32[]{:S(2)}) copy-start(f32[24,40,128]{2,1,0:T(8,128)} %get-tuple-element.84.r_13_) | copy-start | bytes 1474564
  62.4 6.7 %copy-start.7 = (f32[24,40,128]{2,1,0:T(8,128)S(1)}, f32[24,40,128]{2,1,0:T(8,128)}, u32[]{:S(2)}) copy-start(f32[24,40,128]{2,1,0:T(8,128)} %get-tuple-element.85.r_14_) | copy-start | bytes 1474564
  62.4 6.7 %copy-start.8 = (f32[24,40,128]{2,1,0:T(8,128)S(1)}, f32[24,40,128]{2,1,0:T(8,128)}, u32[]{:S(2)}) copy-start(f32[24,40,128]{2,1,0:T(8,128)} %get-tuple-element.86.r_15_) | copy-start | bytes 1474564
  62.4 6.7 %copy-start.9 = (f32[24,40,128]{2,1,0:T(8,128)S(1)}, f32[24,40,128]{2,1,0:T(8,128)}, u32[]{:S(2)}) copy-start(f32[24,40,128]{2,1,0:T(8,128)} %get-tuple-element.87.r_16_) | copy-start | bytes 1474564

commit v7 on v6

--- a/solution.py
+++ b/solution.py
@@ -130,7 +130,7 @@
 UNROLL = {20: 4, 18: 4, 6: 8, 5: 8, 4: 8}
 
 
-def coefficients(c, kx, ky, kz, rd, low, high, scale):
+def coefficients(c, kx, ky, kz, rd, low, high, scale, also=lambda x, factor: None):
     half = 0.5 * scale
 
     def faces(x):
@@ -149,7 +149,9 @@
         cx, fx, fy, fz = faces(x)
         diagonal = fx + before + fy + roll_down(fy, 0) + fz + previous_z(fz)
         inside = cx > 0.0
-        rd[x] = jnp.where(inside, relax_weight / jnp.where(inside, diagonal, 1.0), 0.0)
+        factor = jnp.where(inside, relax_weight / jnp.where(inside, diagonal, 1.0), 0.0)
+        rd[x] = factor
+        also(x, factor)
         return fx
 
     loop(low, high, body, first, unrolling(rd))
@@ -293,7 +295,7 @@
     return jnp.where(up, oy, oy + YH)
 
 
-def place_halos(nx, ny, box, got, put, between=lambda: None):
+def place_halos(nx, ny, box, got, put):
     ox, oy, oz = box
     bx = lax.axis_index("boxes")
     sy = lax.axis_index("sub")
@@ -316,7 +318,6 @@
             put(0, below(up, XH) + x, slice(0, oy), face[x])
         for x in range(GX):
             put(1, below(up, GX) + x, slice(0, oy), face[XH + x])
-    between()
     for f in range(ny):
         up = upward(sy, f)
         face = got[place]
@@ -376,8 +377,7 @@
 
 def join_kernel(nx, ny, *refs):
     count = nx + ny + nx * ny
-    got, outs, (cx, gx, cy, gy, sems) = refs[:count], refs[count:count + 4], refs[count + 4:]
-    copies = [pltpu.make_async_copy(a, b, sems.at[i]) for i, (a, b) in enumerate(zip((cx, gx, cy, gy), outs))]
+    got, (cx, gx, cy, gy) = refs[:count], refs[count:]
     planes, nrows, lanes = cy.shape
     ox, oy = planes - 2 * XH, cx.shape[1]
     for low, high in ((0, XH), (XH + ox, planes)):
@@ -392,15 +392,7 @@
         else:
             (cy, gy)[which][plane, pl.ds(pl.multiple_of(rows.start - oy, 8), rows.size), :] = parted(values)
 
-    def begin():
-        copies[0].start()
-        copies[1].start()
-
-    place_halos(nx, ny, (ox, oy, lanes // 2), got, put, begin)
-    copies[2].start()
-    copies[3].start()
-    for copy in copies:
-        copy.wait()
+    place_halos(nx, ny, (ox, oy, lanes // 2), got, put)
 
 
 def halve(total, work):
@@ -515,12 +507,11 @@
     for copy in copies[:2 * parts]:
         copy.start()
     edge = XH - GX
-    coefficients(c, kx, ky, kz, rd, edge, planes - edge, 1.0)
-
-    def start_sweep(x):
-        first[x] = g[x] * rd[x]
-
-    loop(edge, planes - edge, start_sweep)
+
+    def start_sweep(x, factor):
+        first[x] = g[x] * factor
+
+    coefficients(c, kx, ky, kz, rd, edge, planes - edge, 1.0, start_sweep)
     sweep(first, u0, g, kx, ky, kz, rd, edge + 1, planes - edge - 1)
     for copy in copies[2 * parts:3 * parts]:
         copy.start()
@@ -536,7 +527,10 @@
     low1 = (edge + 2) // 2
     high1 = planes1 - low1
     pool_wide(rest, low1, high1, f1.at[low1:high1], work)
+    copies[3 * parts + 5].start()
     coefficients(c1, kx1, ky1, kz1, rd1, 1, planes1 - 1, 0.25)
+    for copy in copies[3 * parts:3 * parts + 5]:
+        copy.start()
 
     def start_sweep1(x):
         v1[x] = f1[x] * rd1[x]
@@ -544,8 +538,7 @@
     loop(low1, high1, start_sweep1)
     u1[...] = jnp.zeros_like(u1)
     sweep(v1, u1, f1, kx1, ky1, kz1, rd1, low1 + 1, high1 - 1)
-    for copy in copies[3 * parts:]:
-        copy.start()
+    copies[3 * parts + 6].start()
     h1 = XH // 2
     o1 = planes1 - XH
 
@@ -568,20 +561,35 @@
         copy.wait()
 
 
-def bottom_kernel(nx, ny, nfar, c_in, g_in, u_in, *refs):
-    pieces = 1 + nx + nfar
-    got = refs[:pieces]
-    add, c, g, u0, kx, ky, kz, rd = refs[pieces:pieces + 8]
-    c2, f2, kx2, ky2, kz2, rd2, v2, w2, tall, sems = refs[pieces + 8:]
+def face_kernel(ny, c_in, g_in, u_in, c, g, u0, kx, ky, kz, rd, sems):
     copies = [
         pltpu.make_async_copy(a, b, sems.at[i]) for i, (a, b) in enumerate(((c_in, c), (g_in, g), (u_in, u0)))
     ]
     for copy in copies:
         copy.start()
     planes, rows, lanes = u0.shape
+    oy = rows - ny * YN
+    up = upward(lax.axis_index("sub"), 0)
+    copies[0].wait()
+    row = iota2((YN, lanes), 0)
+
+    def close(x):
+        c[x, oy:, :] = jnp.where(row == jnp.where(up, YN - 1, 0), 0.0, c[x, oy:, :])
+
+    if ny == 1:
+        loop(0, planes, close, unroll=2)
+    coefficients(c, kx, ky, kz, rd, 1, planes - 1, 1.0)
+    for copy in copies[1:]:
+        copy.wait()
+
+
+def bottom_kernel(nx, ny, nfar, *refs):
+    pieces = 1 + nx + nfar
+    got = refs[:pieces]
+    add, c2, f2, kx2, ky2, kz2, rd2, v2, w2, tall = refs[pieces:]
     planes2, rows2, oz = c2.shape
-    oy = rows - ny * YN
-    o2x, o2y = (planes2 - 2 * L2X), oy // 4
+    o2x = planes2 - 2 * L2X
+    o2y = rows2 // (ny + 1)
     bx = lax.axis_index("boxes")
     sy = lax.axis_index("sub")
     pz = lax.axis_index("pair")
@@ -646,23 +654,11 @@
         tall[x, pl.ds(1, o2y + 8, stride=2), :] = t
         add[x] = tall[x, 0:rows1, :]
 
-    copies[0].wait()
-    row = iota2((YN, lanes), 0)
-
-    def close(x):
-        c[x, oy:, :] = jnp.where(row == jnp.where(upward(sy, 0), YN - 1, 0), 0.0, c[x, oy:, :])
-
-    if ny == 1:
-        loop(0, planes, close, unroll=2)
-    coefficients(c, kx, ky, kz, rd, 1, planes - 1, 1.0)
-    for copy in copies[1:]:
-        copy.wait()
-
 
 def up_kernel(nx, ny, add, c, g, u0, kx, ky, kz, rd, *refs):
     faces, (kx1, ky1, kz1, rd1, c1, f1, u1) = refs[:nx], refs[nx:nx + 7]
-    field, residual = refs[nx + 7:nx + 9]
-    ua, ub, v1, w1, x1, wide = refs[nx + 9:]
+    outs = refs[nx + 7:nx + 9]
+    field, residual, ua, ub, v1, w1, x1, wide, sems = refs[nx + 9:]
     planes, rows, lanes = u0.shape
     planes1, rows1, oz = u1.shape
     oy = field.shape[1]
@@ -705,12 +701,22 @@
     sweep(ua, ub, g, kx, ky, kz, rd, 1, planes - 1)
     sweep(ub, ua, g, kx, ky, kz, rd, 2, planes - 2)
     order = joining((oy, oz))
-
-    def use(x, vx, av):
-        field[x - 3] = joined(vx[0:oy], *order)
-        residual[x - 3] = joined(g[x, 0:oy, :] - av[0:oy], *order)
-
-    operate(ua, kx, ky, kz, 3, planes - 3, use)
+    ox, chunk = field.shape[0], XH
+    copies = []
+    for k in range(ox // chunk):
+        base = 3 + k * chunk
+
+        def use(x, vx, av):
+            field[x - 3] = joined(vx[0:oy], *order)
+            residual[x - 3] = joined(g[x, 0:oy, :] - av[0:oy], *order)
+
+        operate(ua, kx, ky, kz, base, base + chunk, use)
+        here = pl.ds(k * chunk, chunk)
+        for n, (a, b) in enumerate(zip((field, residual), outs)):
+            copies.append(pltpu.make_async_copy(a.at[here], b.at[here], sems.at[2 * k + n]))
+            copies[-1].start()
+    for copy in copies:
+        copy.wait()
 
 
 def call(kernel, outs, scratch=(), mib=16, raw_in=0, raw_out=0, copies=0, more=0):
@@ -785,7 +791,7 @@
     )(own, *got)
     strip = lax.ppermute(strip, "pair", pair_swap)
     halos = [(2 * XH, oy, 2 * oz)] * 2 + [(planes, rows - oy, 2 * oz)] * 2
-    halos = call(lambda *r: join_kernel(nx, ny, *r), [spec(h) for h in halos], halos, raw_out=4, copies=4)(*got)
+    halos = call(lambda *r: join_kernel(nx, ny, *r), [in_vmem(h) for h in halos], mib=6)(*got)
     middle = (planes1, rows1, oz)
     small = (planes - 2 * SKIP, oy + ny * YN, 2 * oz)
     down = call(
@@ -794,33 +800,35 @@
         + [spec((XH - 1, rows1, oz))] * nx,
         [fine] * FINE + [middle] * (KEPT - FINE) + [fine] * 5 + [middle, (4, rows, oz), (o2x, oy // 2, oz), (o2x, o2y, oz)],
         mib=48,
-        raw_in=6,
+        raw_in=2,
         raw_out=KEPT,
         copies=KEPT + FINE * ny,
         more=4 * planes // group,
-    )(c, g, *halos, strip, c2)
+    )(c, g, *[held(h) for h in halos], strip, c2)
     kept, f2, sides = down[:KEPT], down[KEPT], down[KEPT + 1:]
     sheet = lax.all_gather(f2, ("sub", "pair")).reshape(-1, 2, o2x // 4, o2y, oz)
+    first, sheet = lax.optimization_barrier((kept[:FINE], sheet))
+    fine_up = call(lambda *r: face_kernel(ny, *r), [in_vmem(small)] * 7, mib=6, raw_in=FINE, copies=FINE)(*first)
     got = [sheet] + [lax.ppermute(sheet, "boxes", p) for p in swap_x]
     for e, p in enumerate(far_x):
         at = jnp.where(upward(lax.axis_index("boxes"), e, 2), o2x // 4 - 1, 0)
         got.append(lax.ppermute(lax.dynamic_index_in_dim(sheet, at, 2, keepdims=False), "boxes", p))
-    got, sides = lax.optimization_barrier((got, sides))
+    got, sides, fine_up = lax.optimization_barrier((got, sides, fine_up))
     sides = [lax.ppermute(side, "boxes", p) for side, p in zip(sides, swap_x)]
     lowest = (planes2, rows2, oz)
-    add, *fine_up = call(
+    (add,) = call(
         lambda *r: bottom_kernel(nx, ny, nfar, *r),
-        [in_vmem((planes1 // 2, rows1, oz))] + [in_vmem(small)] * 7,
+        [in_vmem((planes1 // 2, rows1, oz))],
         [lowest] * 8 + [(planes1 // 2, 2 * (o2y + 8), oz)],
         mib=12,
-        raw_in=FINE,
-        copies=FINE,
-    )(*kept[:FINE], *got)
+    )(*got)
     return tuple(call(
         lambda *r: up_kernel(nx, ny, *r),
         [box, box],
-        [small, small, middle, middle, middle, (3, rows, oz)],
-        mib=14,
+        [(ox, oy, oz)] * 2 + [small, small, middle, middle, middle, (3, rows, oz)],
+        mib=16,
+        raw_out=2,
+        copies=2 * (ox // XH),
     )(held(add), *[held(x) for x in fine_up], *sides, *kept[FINE:]))
 
 

time: 80.2 us -> 75.3 us (0.939)
  the two profiles are of different devices: /device:TPU:8 before, /device:TPU:0 now
where the time goes in v7:
time: 75.3 us; the launch traced here: 75.1 us
  Pallas kernels  42.2 us (56%)
  starting transfers between devices  21.8 us (29%)
  blocking collectives  5.55 us (7%)
  waiting for transfers between devices  4.55 us (6%)
  between operations  0.93 us (1%)
    pallas_call x8, Pallas kernels, run(): pl.pallas_call(kernel, in_specs=where[0] * raw_in + where[1] * (len(opera...  42.2 us
    all_gather x1, blocking collectives, per_device(): lax.all_gather(f2, ('sub', 'pair')).reshape(-1, 2, o2x // 4, o2y, oz)  5.55 us
    ppermute x2, starting transfers between devices, per_device(): got = [sheet] + [lax.ppermute(sheet, 'boxes', p) for p in swap_x]  5.17 us
    ppermute x2, starting transfers between devices, traded(): lax.ppermute(faces[nx + ny + e * ny + f], ('boxes', 'sub'), both(swap_x[e...  5.06 us
    ppermute x2, starting transfers between devices, per_device(): sides = [lax.ppermute(side, 'boxes', p) for side, p in zip(sides, swap_x)]  3.42 us
    ppermute x1, starting transfers between devices, traded(): out.append(lax.ppermute(faces[nx + f], 'sub', swap_y[f]))  3 us
    ppermute x1, starting transfers between devices, per_device(): lax.ppermute(lax.dynamic_index_in_dim(sheet, at, 2, keepdims=False), 'box...  2.77 us
    ppermute x1, waiting for transfers between devices, per_device(): lax.ppermute(lax.dynamic_index_in_dim(sheet, at, 2, keepdims=False), 'box...  2.27 us
  transfers between devices with their start and end apart: 11, of which 2 were waited for; matrix products, arithmetic and copies ran while one was open for 0% of the time, Pallas kernels for 19%

profile of v7, /device:TPU:0, one launch (start us, length us, event | category | flops | bytes accessed | tf_op | source)
XLA Modules:
  0.0 75.1 jit_solution(4374508767113774608)
XLA Ops:
  0.7 1.9 %shard_map.50 = (f32[14,64,128]{2,1,0:T(8,128)S(1)}, f32[14,64,128]{2,1,0:T(8,128)S(1)}, f32[2,32,16,128]{3,2,1,0:T(8,128)S(1)}, f32[11,16,128]{2,1,0:T(8,128)S(1)}, f32[11,16,128]{2,1,0:T(8,128)S(1)}) custom-call(f32[32,64,128]{2,1,0:T(8,128)} %phase, s32[32,64,128]{2,1,0:T(8,128)} %mask, f32[32,64,128]{2,1,0:T(8,128)} %dev), custom_call_target="tpu_custom_call" | custom-call | tf_op jit(solution)/shard_map/pallas_call | solution.py:729
  2.5 3.0 %collective-permute-start.2 = (f32[2,32,16,128]{3,2,1,0:T(8,128)S(1)}, f32[2,32,16,128]{3,2,1,0:T(8,128)S(1)}, u32[]{:S(2)}, u32[]{:S(2)}) collective-permute-start(f32[2,32,16,128]{3,2,1,0:T(8,128)S(1)} %get-tuple-element.57), channel_id=1, source_target_pairs={{0,2},{2,0},{1,3},{3,1},{4,6},{6,4},{5,7},{7,5},{8,10},{10,8},{9,1... | collective-permute-start | bytes 1572872 | tf_op jit(solution)/shard_map/ppermute | solution.py:756
  5.5 1.6 %collective-permute-start = (f32[14,64,128]{2,1,0:T(8,128)S(1)}, f32[14,64,128]{2,1,0:T(8,128)S(1)}, u32[]{:S(2)}, u32[]{:S(2)}) collective-permute-start(f32[14,64,128]{2,1,0:T(8,128)S(1)} %get-tuple-element.55), channel_id=1, source_target_pairs={{0,4},{4,0},{8,12},{12,8},{1,5},{5,1},{9,13},{13,9},{2,6},{6,2},{1... | collective-permute-start | bytes 1376264 | tf_op jit(solution)/shard_map/ppermute | solution.py:754
  7.1 0.7 collective-permute-start.1
  7.8 4.4 %collective-permute-start.3 = (f32[11,16,128]{2,1,0:T(8,128)S(1)}, f32[11,16,128]{2,1,0:T(8,128)S(1)}, u32[]{:S(2)}, u32[]{:S(2)}) collective-permute-start(f32[11,16,128]{2,1,0:T(8,128)S(1)} %get-tuple-element.58), channel_id=1, source_target_pairs={{0,6},{2,4},{4,2},{6,0},{8,14},{10,12},{12,10},{14,8},{1,7},{3,5},... | collective-permute-start | bytes 270344 | tf_op jit(solution)/shard_map/ppermute | solution.py:759
  12.2 0.7 collective-permute-start.4
  12.9 4.3 %shard_map.51 = (f32[32,64,256]{2,1,0:T(8,128)}, f32[32,64,256]{2,1,0:T(8,128)}, f32[2,4,64,128]{3,2,1,0:T(8,128)S(1)}, f32[32,128]{1,0:T(8,128)S(1)}) custom-call(f32[32,64,128]{2,1,0:T(8,128)S(1)} %copy-done, s32[32,64,128]{2,1,0:T(8,128)S(1)} %copy-done.1, f32[32,64,128]{2,1,0:T(8,128)S(1)} %copy-done.2), custom_call_target="tpu_custom_call" | custom-call | tf_op jit(solution)/shard_map/pallas_call | solution.py:729
  17.2 2.2 %collective-permute-done.3.r_3_.r_4_ = f32[11,16,128]{2,1,0:T(8,128)S(1)} collective-permute-done((f32[11,16,128]{2,1,0:T(8,128)S(1)}, f32[11,16,128]{2,1,0:T(8,128)S(1)}, u32[]{:S(2)}, u32[]{:S(2)}) %collective-permute-start.3) | collective-permute-done | bytes 90144 | tf_op jit(solution)/shard_map/ppermute | solution.py:759
  19.4 0.0 collective-permute-done.2.r_2_.r_3_
  19.4 0.7 shard_map.53
  20.1 0.1 collective-permute-start.5
  20.2 1.8 %shard_map.52 = (f32[16,64,256]{2,1,0:T(8,128)S(1)}, f32[16,64,256]{2,1,0:T(8,128)S(1)}, f32[48,16,256]{2,1,0:T(8,128)S(1)}, f32[48,16,256]{2,1,0:T(8,128)S(1)}) custom-call(f32[14,64,128]{2,1,0:T(8,128)S(1)} %collective-permute-done.r_0_.r_1_, f32[14,64,128]{2,1,0:T(8,128)S(1)} %collective-permute-done.1.r_1_.r_2_, ...), custom_call_target="tpu_custom_call" | custom-call | tf_op jit(solution)/shard_map/pallas_call | solution.py:729
  22.0 0.0 collective-permute-done.5.r_6_
  22.0 14.9 %shard_map.54 = (f32[38,72,256]{2,1,0:T(8,128)}, f32[38,72,256]{2,1,0:T(8,128)}, f32[38,72,256]{2,1,0:T(8,128)}, f32[24,40,128]{2,1,0:T(8,128)}, f32[24,40,128]{...) custom-call(f32[32,64,256]{2,1,0:T(8,128)} %get-tuple-element.63.r_0, ...), custom_call_target="tpu_custom_call" | custom-call | tf_op jit(solution)/shard_map/pallas_call | solution.py:729
  36.9 5.6 %all-gather = f32[256,128]{1,0:T(8,128)S(1)} all-gather(f32[64,128]{1,0:T(8,128)S(1)} %get-tuple-element.74), channel_id=2, replica_groups=mesh['groups'=2,'boxes'=4,'sub'=2,'pair'=2] {'sub','pair'}, dimensions={0}, use_global_device_ids=true | all-gather | bytes 163840 | tf_op jit(solution)/shard_map/all_gather | solution.py:809
  42.5 4.5 %collective-permute-start.6 = (f32[4,2,2,16,128]{4,3,2,1,0:T(8,128)S(1)}, f32[4,2,2,16,128]{4,3,2,1,0:T(8,128)S(1)}, u32[]{:S(2)}, u32[]{:S(2)}) collective-permute-start(f32[4,2,2,16,128]{4,3,2,1,0:T(8,128)S(1)} %bitcast.3), channel_id=1, source_target_pairs={{0,4},{4,0},{8,12},{12,8},{1,5},{5,1},{9,13},{13,9},{2,6},{6,2},{1... | collective-permute-start | bytes 393224 | tf_op jit(solution)/shard_map/ppermute | solution.py:812
  47.0 0.7 collective-permute-start.7
  47.7 2.8 %collective-permute-start.8 = (f32[4,2,16,128]{3,2,1,0:T(8,128)S(1)}, f32[4,2,16,128]{3,2,1,0:T(8,128)S(1)}, u32[]{:S(2)}, u32[]{:S(2)}) collective-permute-start(f32[4,2,16,128]{3,2,1,0:T(8,128)S(1)} %dynamic-slice_bitcast_fusion), channel_id=1, source_target_pairs={{0,8},{8,0},{4,12},{12,4},{1,9},{9,1},{5,13},{13,5},{2,10},{10,2},... | collective-permute-start | bytes 196616 | tf_op jit(solution)/shard_map/ppermute | solution.py:815
  50.5 4.1 %shard_map.55 = (f32[38,72,256]{2,1,0:T(8,128)S(1)}, f32[38,72,256]{2,1,0:T(8,128)S(1)}, f32[38,72,256]{2,1,0:T(8,128)S(1)}, f32[38,72,256]{2,1,0:T(8,128)S(1)},...) custom-call(f32[38,72,256]{2,1,0:T(8,128)} %get-tuple-element.78.r_0_, ...), custom_call_target="tpu_custom_call" | custom-call | tf_op jit(solution)/shard_map/pallas_call | solution.py:729
  54.6 2.3 %collective-permute-done.8.r_3_ = f32[4,2,16,128]{3,2,1,0:T(8,128)S(1)} collective-permute-done((f32[4,2,16,128]{3,2,1,0:T(8,128)S(1)}, f32[4,2,16,128]{3,2,1,0:T(8,128)S(1)}, u32[]{:S(2)}, u32[]{:S(2)}) %collective-permute-start.8) | collective-permute-done | bytes 65568 | tf_op jit(solution)/shard_map/ppermute | solution.py:815
  56.9 0.7 collective-permute-start.10
  57.5 2.8 %collective-permute-start.9 = (f32[7,40,128]{2,1,0:T(8,128)S(1)}, f32[7,40,128]{2,1,0:T(8,128)S(1)}, u32[]{:S(2)}, u32[]{:S(2)}) collective-permute-start(f32[7,40,128]{2,1,0:T(8,128)S(1)} %get-tuple-element.99), channel_id=1, source_target_pairs={{0,4},{4,0},{8,12},{12,8},{1,5},{5,1},{9,13},{13,9},{2,6},{6,2},{1... | collective-permute-start | bytes 430088 | tf_op jit(solution)/shard_map/ppermute | solution.py:817
  60.3 4.3 %shard_map.56.r_0_ = f32[12,40,128]{2,1,0:T(8,128)S(1)} custom-call(f32[4,2,2,16,128]{4,3,2,1,0:T(8,128)S(1)} %bitcast.6, f32[4,2,2,16,128]{4,3,2,1,0:T(8,128)S(1)} %collective-permute-done.6.r_1_, f32[4,2,2,16,128]{4,3,2,1,0:T(8,128)S(1)} %collective-permute-done.7.r_2_, f32[4,2,16,128]{3,2,1,0:T(8,128)S(1)} %collective-permute-done.8.r_3_), custom_call_target="tpu_custom_call" | custom-call | tf_op jit(solution)/shard_map/pallas_call | solution.py:729
  64.7 10.4 %shard_map.57 = (f32[32,64,128]{2,1,0:T(8,128)}, f32[32,64,128]{2,1,0:T(8,128)}) custom-call(f32[12,40,128]{2,1,0:T(8,128)S(1)} %shard_map.56.r_0_, f32[38,72,256]{2,1,0:T(8,128)S(1)} %get-tuple-element.92.r_1_, f32[38,72,256]{2,1,0:T(8,128)S(1)} %get-tuple-element.93.r_2_, f32[38,72,256]{2,1,0:T(8,128)S(1)} %get-tuple-element.94.r_3_, ...), custom_call_target="tpu_custom_call" | custom-call | tf_op jit(solution)/shard_map/pallas_call | solution.py:729
  (28 shorter events, 0.1 us)
Async XLA Ops:
  0.6 12.2 %copy-start = (f32[32,64,128]{2,1,0:T(8,128)S(1)}, f32[32,64,128]{2,1,0:T(8,128)}, u32[]{:S(2)}) copy-start(f32[32,64,128]{2,1,0:T(8,128)} %phase) | copy-start | bytes 3145732
  0.6 12.2 %copy-start.1 = (s32[32,64,128]{2,1,0:T(8,128)S(1)}, s32[32,64,128]{2,1,0:T(8,128)}, u32[]{:S(2)}) copy-start(s32[32,64,128]{2,1,0:T(8,128)} %mask) | copy-start | bytes 3145732
  0.6 12.2 %copy-start.2 = (f32[32,64,128]{2,1,0:T(8,128)S(1)}, f32[32,64,128]{2,1,0:T(8,128)}, u32[]{:S(2)}) copy-start(f32[32,64,128]{2,1,0:T(8,128)} %dev) | copy-start | bytes 3145732
  2.5 16.9 %collective-permute-start.2 = (f32[2,32,16,128]{3,2,1,0:T(8,128)S(1)}, f32[2,32,16,128]{3,2,1,0:T(8,128)S(1)}, u32[]{:S(2)}, u32[]{:S(2)}) collective-permute-start(f32[2,32,16,128]{3,2,1,0:T(8,128)S(1)} %get-tuple-element.57), channel_id=1, source_target_pairs={{0,2},{2,0},{1,3},{3,1},{4,6},{6,4},{5,7},{7,5},{8,10},{10,8},{9,1... | collective-permute-start | bytes 1572872 | tf_op jit(solution)/shard_map/ppermute | solution.py:756
  5.5 13.8 %collective-permute-start = (f32[14,64,128]{2,1,0:T(8,128)S(1)}, f32[14,64,128]{2,1,0:T(8,128)S(1)}, u32[]{:S(2)}, u32[]{:S(2)}) collective-permute-start(f32[14,64,128]{2,1,0:T(8,128)S(1)} %get-tuple-element.55), channel_id=1, source_target_pairs={{0,4},{4,0},{8,12},{12,8},{1,5},{5,1},{9,13},{13,9},{2,6},{6,2},{1... | collective-permute-start | bytes 1376264 | tf_op jit(solution)/shard_map/ppermute | solution.py:754
  7.1 12.3 %collective-permute-start.1 = (f32[14,64,128]{2,1,0:T(8,128)S(1)}, f32[14,64,128]{2,1,0:T(8,128)S(1)}, u32[]{:S(2)}, u32[]{:S(2)}) collective-permute-start(f32[14,64,128]{2,1,0:T(8,128)S(1)} %get-tuple-element.56), channel_id=1, source_target_pairs={{4,8},{8,4},{5,9},{9,5},{6,10},{10,6},{7,11},{11,7},{20,24},{24,20... | collective-permute-start | bytes 1376264 | tf_op jit(solution)/shard_map/ppermute | solution.py:754
  7.8 11.6 %collective-permute-start.3 = (f32[11,16,128]{2,1,0:T(8,128)S(1)}, f32[11,16,128]{2,1,0:T(8,128)S(1)}, u32[]{:S(2)}, u32[]{:S(2)}) collective-permute-start(f32[11,16,128]{2,1,0:T(8,128)S(1)} %get-tuple-element.58), channel_id=1, source_target_pairs={{0,6},{2,4},{4,2},{6,0},{8,14},{10,12},{12,10},{14,8},{1,7},{3,5},... | collective-permute-start | bytes 270344 | tf_op jit(solution)/shard_map/ppermute | solution.py:759
  12.2 7.2 %collective-permute-start.4 = (f32[11,16,128]{2,1,0:T(8,128)S(1)}, f32[11,16,128]{2,1,0:T(8,128)S(1)}, u32[]{:S(2)}, u32[]{:S(2)}) collective-permute-start(f32[11,16,128]{2,1,0:T(8,128)S(1)} %get-tuple-element.59), channel_id=1, source_target_pairs={{4,10},{6,8},{8,6},{10,4},{5,11},{7,9},{9,7},{11,5},{20,26},{22,24... | collective-permute-start | bytes 270344 | tf_op jit(solution)/shard_map/ppermute | solution.py:759
  20.1 1.9 %collective-permute-start.5 = (f32[12,80,128]{2,1,0:T(8,128)S(1)}, f32[12,80,128]{2,1,0:T(8,128)S(1)}, u32[]{:S(2)}, u32[]{:S(2)}) collective-permute-start(f32[12,80,128]{2,1,0:T(8,128)S(1)} %shard_map.53), channel_id=1, source_target_pairs={{0,1},{1,0},{2,3},{3,2},{4,5},{5,4},{6,7},{7,6},{8,9},{9,8},{10,11... | collective-permute-start | bytes 1474568 | tf_op jit(solution)/shard_map/ppermute | solution.py:792
  42.5 14.4 %collective-permute-start.6 = (f32[4,2,2,16,128]{4,3,2,1,0:T(8,128)S(1)}, f32[4,2,2,16,128]{4,3,2,1,0:T(8,128)S(1)}, u32[]{:S(2)}, u32[]{:S(2)}) collective-permute-start(f32[4,2,2,16,128]{4,3,2,1,0:T(8,128)S(1)} %bitcast.3), channel_id=1, source_target_pairs={{0,4},{4,0},{8,12},{12,8},{1,5},{5,1},{9,13},{13,9},{2,6},{6,2},{1... | collective-permute-start | bytes 393224 | tf_op jit(solution)/shard_map/ppermute | solution.py:812
  47.0 9.9 %collective-permute-start.7 = (f32[4,2,2,16,128]{4,3,2,1,0:T(8,128)S(1)}, f32[4,2,2,16,128]{4,3,2,1,0:T(8,128)S(1)}, u32[]{:S(2)}, u32[]{:S(2)}) collective-permute-start(f32[4,2,2,16,128]{4,3,2,1,0:T(8,128)S(1)} %bitcast.4), channel_id=1, source_target_pairs={{4,8},{8,4},{5,9},{9,5},{6,10},{10,6},{7,11},{11,7},{20,24},{24,20... | collective-permute-start | bytes 393224 | tf_op jit(solution)/shard_map/ppermute | solution.py:812
  47.7 16.9 %copy-start.3 = (f32[24,40,128]{2,1,0:T(8,128)S(1)}, f32[24,40,128]{2,1,0:T(8,128)}, u32[]{:S(2)}) copy-start(f32[24,40,128]{2,1,0:T(8,128)} %get-tuple-element.101.r_10_) | copy-start | bytes 1474564
  47.7 16.9 %copy-start.4 = (f32[24,40,128]{2,1,0:T(8,128)S(1)}, f32[24,40,128]{2,1,0:T(8,128)}, u32[]{:S(2)}) copy-start(f32[24,40,128]{2,1,0:T(8,128)} %get-tuple-element.102.r_11_) | copy-start | bytes 1474564
  47.7 16.9 %copy-start.5 = (f32[24,40,128]{2,1,0:T(8,128)S(1)}, f32[24,40,128]{2,1,0:T(8,128)}, u32[]{:S(2)}) copy-start(f32[24,40,128]{2,1,0:T(8,128)} %get-tuple-element.103.r_12_) | copy-start | bytes 1474564
  47.7 16.9 %copy-start.6 = (f32[24,40,128]{2,1,0:T(8,128)S(1)}, f32[24,40,128]{2,1,0:T(8,128)}, u32[]{:S(2)}) copy-start(f32[24,40,128]{2,1,0:T(8,128)} %get-tuple-element.104.r_13_) | copy-start | bytes 1474564
  47.7 16.9 %copy-start.7 = (f32[24,40,128]{2,1,0:T(8,128)S(1)}, f32[24,40,128]{2,1,0:T(8,128)}, u32[]{:S(2)}) copy-start(f32[24,40,128]{2,1,0:T(8,128)} %get-tuple-element.105.r_14_) | copy-start | bytes 1474564
  47.7 16.9 %copy-start.8 = (f32[24,40,128]{2,1,0:T(8,128)S(1)}, f32[24,40,128]{2,1,0:T(8,128)}, u32[]{:S(2)}) copy-start(f32[24,40,128]{2,1,0:T(8,128)} %get-tuple-element.106.r_15_) | copy-start | bytes 1474564
  47.7 16.9 %copy-start.9 = (f32[24,40,128]{2,1,0:T(8,128)S(1)}, f32[24,40,128]{2,1,0:T(8,128)}, u32[]{:S(2)}) copy-start(f32[24,40,128]{2,1,0:T(8,128)} %get-tuple-element.107.r_16_) | copy-start | bytes 1474564
  47.7 9.1 %collective-permute-start.8 = (f32[4,2,16,128]{3,2,1,0:T(8,128)S(1)}, f32[4,2,16,128]{3,2,1,0:T(8,128)S(1)}, u32[]{:S(2)}, u32[]{:S(2)}) collective-permute-start(f32[4,2,16,128]{3,2,1,0:T(8,128)S(1)} %dynamic-slice_bitcast_fusion), channel_id=1, source_target_pairs={{0,8},{8,0},{4,12},{12,4},{1,9},{9,1},{5,13},{13,5},{2,10},{10,2},... | collective-permute-start | bytes 196616 | tf_op jit(solution)/shard_map/ppermute | solution.py:815
  56.9 7.7 %collective-permute-start.10 = (f32[7,40,128]{2,1,0:T(8,128)S(1)}, f32[7,40,128]{2,1,0:T(8,128)S(1)}, u32[]{:S(2)}, u32[]{:S(2)}) collective-permute-start(f32[7,40,128]{2,1,0:T(8,128)S(1)} %get-tuple-element.100), channel_id=1, source_target_pairs={{4,8},{8,4},{5,9},{9,5},{6,10},{10,6},{7,11},{11,7},{20,24},{24,20... | collective-permute-start | bytes 430088 | tf_op jit(solution)/shard_map/ppermute | solution.py:817
  57.5 7.1 %collective-permute-start.9 = (f32[7,40,128]{2,1,0:T(8,128)S(1)}, f32[7,40,128]{2,1,0:T(8,128)S(1)}, u32[]{:S(2)}, u32[]{:S(2)}) collective-permute-start(f32[7,40,128]{2,1,0:T(8,128)S(1)} %get-tuple-element.99), channel_id=1, source_target_pairs={{0,4},{4,0},{8,12},{12,8},{1,5},{5,1},{9,13},{13,9},{2,6},{6,2},{1... | collective-permute-start | bytes 430088 | tf_op jit(solution)/shard_map/ppermute | solution.py:817

commit v8 on v7

--- a/solution.py
+++ b/solution.py
@@ -127,7 +127,7 @@
     return UNROLL.get(ref.shape[1] * ref.shape[2] // 1024, 4)
 
 
-UNROLL = {20: 4, 18: 4, 6: 8, 5: 8, 4: 8}
+UNROLL = {20: 6, 18: 4, 6: 8, 5: 8, 4: 10}
 
 
 def coefficients(c, kx, ky, kz, rd, low, high, scale, also=lambda x, factor: None):

time: 75.3 us -> 74.4 us (0.988)
  Pallas kernels: 42.2 us -> 41.3 us
    pallas_call x8, Pallas kernels: 42.2 us -> 41.3 us  [run(): pl.pallas_call(kernel, in_specs=where[0] * raw_in + where[1] * (len(opera...]
  transfers between devices with their start and end apart: 11 -> 11, of which waited for: 2 -> 2; matrix products, arithmetic and copies ran while one was open for 0% -> 0% of each run, Pallas kernels for 19% -> 18%
where the time goes in v8:
time: 74.4 us; the launch traced here: 74.2 us
  Pallas kernels  41.3 us (56%)
  starting transfers between devices  21.8 us (29%)
  blocking collectives  5.55 us (7%)
  waiting for transfers between devices  4.55 us (6%)
  between operations  0.93 us (1%)
    pallas_call x8, Pallas kernels, run(): pl.pallas_call(kernel, in_specs=where[0] * raw_in + where[1] * (len(opera...  41.3 us
    all_gather x1, blocking collectives, per_device(): lax.all_gather(f2, ('sub', 'pair')).reshape(-1, 2, o2x // 4, o2y, oz)  5.55 us
    ppermute x2, starting transfers between devices, per_device(): got = [sheet] + [lax.ppermute(sheet, 'boxes', p) for p in swap_x]  5.17 us
    ppermute x2, starting transfers between devices, traded(): lax.ppermute(faces[nx + ny + e * ny + f], ('boxes', 'sub'), both(swap_x[e...  5.06 us
    ppermute x2, starting transfers between devices, per_device(): sides = [lax.ppermute(side, 'boxes', p) for side, p in zip(sides, swap_x)]  3.42 us
    ppermute x1, starting transfers between devices, traded(): out.append(lax.ppermute(faces[nx + f], 'sub', swap_y[f]))  3 us
    ppermute x1, starting transfers between devices, per_device(): lax.ppermute(lax.dynamic_index_in_dim(sheet, at, 2, keepdims=False), 'box...  2.77 us
    ppermute x1, waiting for transfers between devices, per_device(): lax.ppermute(lax.dynamic_index_in_dim(sheet, at, 2, keepdims=False), 'box...  2.27 us
  transfers between devices with their start and end apart: 11, of which 2 were waited for; matrix products, arithmetic and copies ran while one was open for 0% of the time, Pallas kernels for 18%

profile of v8, /device:TPU:0, one launch (start us, length us, event | category | flops | bytes accessed | tf_op | source)
XLA Modules:
  0.0 74.2 jit_solution(13864873224891122268)
XLA Ops:
  0.7 1.9 %shard_map.50 = (f32[14,64,128]{2,1,0:T(8,128)S(1)}, f32[14,64,128]{2,1,0:T(8,128)S(1)}, f32[2,32,16,128]{3,2,1,0:T(8,128)S(1)}, f32[11,16,128]{2,1,0:T(8,128)S(1)}, f32[11,16,128]{2,1,0:T(8,128)S(1)}) custom-call(f32[32,64,128]{2,1,0:T(8,128)} %phase, s32[32,64,128]{2,1,0:T(8,128)} %mask, f32[32,64,128]{2,1,0:T(8,128)} %dev), custom_call_target="tpu_custom_call" | custom-call | tf_op jit(solution)/shard_map/pallas_call | solution.py:729
  2.5 3.0 %collective-permute-start.2 = (f32[2,32,16,128]{3,2,1,0:T(8,128)S(1)}, f32[2,32,16,128]{3,2,1,0:T(8,128)S(1)}, u32[]{:S(2)}, u32[]{:S(2)}) collective-permute-start(f32[2,32,16,128]{3,2,1,0:T(8,128)S(1)} %get-tuple-element.57), channel_id=1, source_target_pairs={{0,2},{2,0},{1,3},{3,1},{4,6},{6,4},{5,7},{7,5},{8,10},{10,8},{9,1... | collective-permute-start | bytes 1572872 | tf_op jit(solution)/shard_map/ppermute | solution.py:756
  5.5 1.6 %collective-permute-start = (f32[14,64,128]{2,1,0:T(8,128)S(1)}, f32[14,64,128]{2,1,0:T(8,128)S(1)}, u32[]{:S(2)}, u32[]{:S(2)}) collective-permute-start(f32[14,64,128]{2,1,0:T(8,128)S(1)} %get-tuple-element.55), channel_id=1, source_target_pairs={{0,4},{4,0},{8,12},{12,8},{1,5},{5,1},{9,13},{13,9},{2,6},{6,2},{1... | collective-permute-start | bytes 1376264 | tf_op jit(solution)/shard_map/ppermute | solution.py:754
  7.1 0.7 collective-permute-start.1
  7.8 4.4 %collective-permute-start.3 = (f32[11,16,128]{2,1,0:T(8,128)S(1)}, f32[11,16,128]{2,1,0:T(8,128)S(1)}, u32[]{:S(2)}, u32[]{:S(2)}) collective-permute-start(f32[11,16,128]{2,1,0:T(8,128)S(1)} %get-tuple-element.58), channel_id=1, source_target_pairs={{0,6},{2,4},{4,2},{6,0},{8,14},{10,12},{12,10},{14,8},{1,7},{3,5},... | collective-permute-start | bytes 270344 | tf_op jit(solution)/shard_map/ppermute | solution.py:759
  12.2 0.7 collective-permute-start.4
  12.9 4.3 %shard_map.51 = (f32[32,64,256]{2,1,0:T(8,128)}, f32[32,64,256]{2,1,0:T(8,128)}, f32[2,4,64,128]{3,2,1,0:T(8,128)S(1)}, f32[32,128]{1,0:T(8,128)S(1)}) custom-call(f32[32,64,128]{2,1,0:T(8,128)S(1)} %copy-done, s32[32,64,128]{2,1,0:T(8,128)S(1)} %copy-done.1, f32[32,64,128]{2,1,0:T(8,128)S(1)} %copy-done.2), custom_call_target="tpu_custom_call" | custom-call | tf_op jit(solution)/shard_map/pallas_call | solution.py:729
  17.2 2.2 %collective-permute-done.3.r_3_.r_4_ = f32[11,16,128]{2,1,0:T(8,128)S(1)} collective-permute-done((f32[11,16,128]{2,1,0:T(8,128)S(1)}, f32[11,16,128]{2,1,0:T(8,128)S(1)}, u32[]{:S(2)}, u32[]{:S(2)}) %collective-permute-start.3) | collective-permute-done | bytes 90144 | tf_op jit(solution)/shard_map/ppermute | solution.py:759
  19.4 0.0 collective-permute-done.2.r_2_.r_3_
  19.4 0.7 shard_map.53
  20.1 0.1 collective-permute-start.5
  20.2 1.8 %shard_map.52 = (f32[16,64,256]{2,1,0:T(8,128)S(1)}, f32[16,64,256]{2,1,0:T(8,128)S(1)}, f32[48,16,256]{2,1,0:T(8,128)S(1)}, f32[48,16,256]{2,1,0:T(8,128)S(1)}) custom-call(f32[14,64,128]{2,1,0:T(8,128)S(1)} %collective-permute-done.r_0_.r_1_, f32[14,64,128]{2,1,0:T(8,128)S(1)} %collective-permute-done.1.r_1_.r_2_, ...), custom_call_target="tpu_custom_call" | custom-call | tf_op jit(solution)/shard_map/pallas_call | solution.py:729
  22.0 0.0 collective-permute-done.5.r_6_
  22.0 14.7 %shard_map.54 = (f32[38,72,256]{2,1,0:T(8,128)}, f32[38,72,256]{2,1,0:T(8,128)}, f32[38,72,256]{2,1,0:T(8,128)}, f32[24,40,128]{2,1,0:T(8,128)}, f32[24,40,128]{...) custom-call(f32[32,64,256]{2,1,0:T(8,128)} %get-tuple-element.63.r_0, ...), custom_call_target="tpu_custom_call" | custom-call | tf_op jit(solution)/shard_map/pallas_call | solution.py:729
  36.7 5.6 %all-gather = f32[256,128]{1,0:T(8,128)S(1)} all-gather(f32[64,128]{1,0:T(8,128)S(1)} %get-tuple-element.74), channel_id=2, replica_groups=mesh['groups'=2,'boxes'=4,'sub'=2,'pair'=2] {'sub','pair'}, dimensions={0}, use_global_device_ids=true | all-gather | bytes 163840 | tf_op jit(solution)/shard_map/all_gather | solution.py:809
  42.3 4.5 %collective-permute-start.6 = (f32[4,2,2,16,128]{4,3,2,1,0:T(8,128)S(1)}, f32[4,2,2,16,128]{4,3,2,1,0:T(8,128)S(1)}, u32[]{:S(2)}, u32[]{:S(2)}) collective-permute-start(f32[4,2,2,16,128]{4,3,2,1,0:T(8,128)S(1)} %bitcast.3), channel_id=1, source_target_pairs={{0,4},{4,0},{8,12},{12,8},{1,5},{5,1},{9,13},{13,9},{2,6},{6,2},{1... | collective-permute-start | bytes 393224 | tf_op jit(solution)/shard_map/ppermute | solution.py:812
  46.8 0.7 collective-permute-start.7
  47.6 2.8 %collective-permute-start.8 = (f32[4,2,16,128]{3,2,1,0:T(8,128)S(1)}, f32[4,2,16,128]{3,2,1,0:T(8,128)S(1)}, u32[]{:S(2)}, u32[]{:S(2)}) collective-permute-start(f32[4,2,16,128]{3,2,1,0:T(8,128)S(1)} %dynamic-slice_bitcast_fusion), channel_id=1, source_target_pairs={{0,8},{8,0},{4,12},{12,4},{1,9},{9,1},{5,13},{13,5},{2,10},{10,2},... | collective-permute-start | bytes 196616 | tf_op jit(solution)/shard_map/ppermute | solution.py:815
  50.3 4.1 %shard_map.55 = (f32[38,72,256]{2,1,0:T(8,128)S(1)}, f32[38,72,256]{2,1,0:T(8,128)S(1)}, f32[38,72,256]{2,1,0:T(8,128)S(1)}, f32[38,72,256]{2,1,0:T(8,128)S(1)},...) custom-call(f32[38,72,256]{2,1,0:T(8,128)} %get-tuple-element.78.r_0_, ...), custom_call_target="tpu_custom_call" | custom-call | tf_op jit(solution)/shard_map/pallas_call | solution.py:729
  54.4 2.3 %collective-permute-done.8.r_3_ = f32[4,2,16,128]{3,2,1,0:T(8,128)S(1)} collective-permute-done((f32[4,2,16,128]{3,2,1,0:T(8,128)S(1)}, f32[4,2,16,128]{3,2,1,0:T(8,128)S(1)}, u32[]{:S(2)}, u32[]{:S(2)}) %collective-permute-start.8) | collective-permute-done | bytes 65568 | tf_op jit(solution)/shard_map/ppermute | solution.py:815
  56.7 0.7 collective-permute-start.10
  57.4 2.8 %collective-permute-start.9 = (f32[7,40,128]{2,1,0:T(8,128)S(1)}, f32[7,40,128]{2,1,0:T(8,128)S(1)}, u32[]{:S(2)}, u32[]{:S(2)}) collective-permute-start(f32[7,40,128]{2,1,0:T(8,128)S(1)} %get-tuple-element.99), channel_id=1, source_target_pairs={{0,4},{4,0},{8,12},{12,8},{1,5},{5,1},{9,13},{13,9},{2,6},{6,2},{1... | collective-permute-start | bytes 430088 | tf_op jit(solution)/shard_map/ppermute | solution.py:817
  60.1 3.6 %shard_map.56.r_0_ = f32[12,40,128]{2,1,0:T(8,128)S(1)} custom-call(f32[4,2,2,16,128]{4,3,2,1,0:T(8,128)S(1)} %bitcast.6, f32[4,2,2,16,128]{4,3,2,1,0:T(8,128)S(1)} %collective-permute-done.6.r_1_, f32[4,2,2,16,128]{4,3,2,1,0:T(8,128)S(1)} %collective-permute-done.7.r_2_, f32[4,2,16,128]{3,2,1,0:T(8,128)S(1)} %collective-permute-done.8.r_3_), custom_call_target="tpu_custom_call" | custom-call | tf_op jit(solution)/shard_map/pallas_call | solution.py:729
  63.8 10.4 %shard_map.57 = (f32[32,64,128]{2,1,0:T(8,128)}, f32[32,64,128]{2,1,0:T(8,128)}) custom-call(f32[12,40,128]{2,1,0:T(8,128)S(1)} %shard_map.56.r_0_, f32[38,72,256]{2,1,0:T(8,128)S(1)} %get-tuple-element.92.r_1_, f32[38,72,256]{2,1,0:T(8,128)S(1)} %get-tuple-element.93.r_2_, f32[38,72,256]{2,1,0:T(8,128)S(1)} %get-tuple-element.94.r_3_, ...), custom_call_target="tpu_custom_call" | custom-call | tf_op jit(solution)/shard_map/pallas_call | solution.py:729
  (28 shorter events, 0.1 us)
Async XLA Ops:
  0.6 12.2 %copy-start = (f32[32,64,128]{2,1,0:T(8,128)S(1)}, f32[32,64,128]{2,1,0:T(8,128)}, u32[]{:S(2)}) copy-start(f32[32,64,128]{2,1,0:T(8,128)} %phase) | copy-start | bytes 3145732
  0.6 12.2 %copy-start.1 = (s32[32,64,128]{2,1,0:T(8,128)S(1)}, s32[32,64,128]{2,1,0:T(8,128)}, u32[]{:S(2)}) copy-start(s32[32,64,128]{2,1,0:T(8,128)} %mask) | copy-start | bytes 3145732
  0.6 12.2 %copy-start.2 = (f32[32,64,128]{2,1,0:T(8,128)S(1)}, f32[32,64,128]{2,1,0:T(8,128)}, u32[]{:S(2)}) copy-start(f32[32,64,128]{2,1,0:T(8,128)} %dev) | copy-start | bytes 3145732
  2.5 16.9 %collective-permute-start.2 = (f32[2,32,16,128]{3,2,1,0:T(8,128)S(1)}, f32[2,32,16,128]{3,2,1,0:T(8,128)S(1)}, u32[]{:S(2)}, u32[]{:S(2)}) collective-permute-start(f32[2,32,16,128]{3,2,1,0:T(8,128)S(1)} %get-tuple-element.57), channel_id=1, source_target_pairs={{0,2},{2,0},{1,3},{3,1},{4,6},{6,4},{5,7},{7,5},{8,10},{10,8},{9,1... | collective-permute-start | bytes 1572872 | tf_op jit(solution)/shard_map/ppermute | solution.py:756
  5.5 13.8 %collective-permute-start = (f32[14,64,128]{2,1,0:T(8,128)S(1)}, f32[14,64,128]{2,1,0:T(8,128)S(1)}, u32[]{:S(2)}, u32[]{:S(2)}) collective-permute-start(f32[14,64,128]{2,1,0:T(8,128)S(1)} %get-tuple-element.55), channel_id=1, source_target_pairs={{0,4},{4,0},{8,12},{12,8},{1,5},{5,1},{9,13},{13,9},{2,6},{6,2},{1... | collective-permute-start | bytes 1376264 | tf_op jit(solution)/shard_map/ppermute | solution.py:754
  7.1 12.3 %collective-permute-start.1 = (f32[14,64,128]{2,1,0:T(8,128)S(1)}, f32[14,64,128]{2,1,0:T(8,128)S(1)}, u32[]{:S(2)}, u32[]{:S(2)}) collective-permute-start(f32[14,64,128]{2,1,0:T(8,128)S(1)} %get-tuple-element.56), channel_id=1, source_target_pairs={{4,8},{8,4},{5,9},{9,5},{6,10},{10,6},{7,11},{11,7},{20,24},{24,20... | collective-permute-start | bytes 1376264 | tf_op jit(solution)/shard_map/ppermute | solution.py:754
  7.8 11.6 %collective-permute-start.3 = (f32[11,16,128]{2,1,0:T(8,128)S(1)}, f32[11,16,128]{2,1,0:T(8,128)S(1)}, u32[]{:S(2)}, u32[]{:S(2)}) collective-permute-start(f32[11,16,128]{2,1,0:T(8,128)S(1)} %get-tuple-element.58), channel_id=1, source_target_pairs={{0,6},{2,4},{4,2},{6,0},{8,14},{10,12},{12,10},{14,8},{1,7},{3,5},... | collective-permute-start | bytes 270344 | tf_op jit(solution)/shard_map/ppermute | solution.py:759
  12.2 7.2 %collective-permute-start.4 = (f32[11,16,128]{2,1,0:T(8,128)S(1)}, f32[11,16,128]{2,1,0:T(8,128)S(1)}, u32[]{:S(2)}, u32[]{:S(2)}) collective-permute-start(f32[11,16,128]{2,1,0:T(8,128)S(1)} %get-tuple-element.59), channel_id=1, source_target_pairs={{4,10},{6,8},{8,6},{10,4},{5,11},{7,9},{9,7},{11,5},{20,26},{22,24... | collective-permute-start | bytes 270344 | tf_op jit(solution)/shard_map/ppermute | solution.py:759
  20.1 1.9 %collective-permute-start.5 = (f32[12,80,128]{2,1,0:T(8,128)S(1)}, f32[12,80,128]{2,1,0:T(8,128)S(1)}, u32[]{:S(2)}, u32[]{:S(2)}) collective-permute-start(f32[12,80,128]{2,1,0:T(8,128)S(1)} %shard_map.53), channel_id=1, source_target_pairs={{0,1},{1,0},{2,3},{3,2},{4,5},{5,4},{6,7},{7,6},{8,9},{9,8},{10,11... | collective-permute-start | bytes 1474568 | tf_op jit(solution)/shard_map/ppermute | solution.py:792
  42.3 14.4 %collective-permute-start.6 = (f32[4,2,2,16,128]{4,3,2,1,0:T(8,128)S(1)}, f32[4,2,2,16,128]{4,3,2,1,0:T(8,128)S(1)}, u32[]{:S(2)}, u32[]{:S(2)}) collective-permute-start(f32[4,2,2,16,128]{4,3,2,1,0:T(8,128)S(1)} %bitcast.3), channel_id=1, source_target_pairs={{0,4},{4,0},{8,12},{12,8},{1,5},{5,1},{9,13},{13,9},{2,6},{6,2},{1... | collective-permute-start | bytes 393224 | tf_op jit(solution)/shard_map/ppermute | solution.py:812
  46.8 9.9 %collective-permute-start.7 = (f32[4,2,2,16,128]{4,3,2,1,0:T(8,128)S(1)}, f32[4,2,2,16,128]{4,3,2,1,0:T(8,128)S(1)}, u32[]{:S(2)}, u32[]{:S(2)}) collective-permute-start(f32[4,2,2,16,128]{4,3,2,1,0:T(8,128)S(1)} %bitcast.4), channel_id=1, source_target_pairs={{4,8},{8,4},{5,9},{9,5},{6,10},{10,6},{7,11},{11,7},{20,24},{24,20... | collective-permute-start | bytes 393224 | tf_op jit(solution)/shard_map/ppermute | solution.py:812
  47.5 16.2 %copy-start.3 = (f32[24,40,128]{2,1,0:T(8,128)S(1)}, f32[24,40,128]{2,1,0:T(8,128)}, u32[]{:S(2)}) copy-start(f32[24,40,128]{2,1,0:T(8,128)} %get-tuple-element.101.r_10_) | copy-start | bytes 1474564
  47.5 16.2 %copy-start.4 = (f32[24,40,128]{2,1,0:T(8,128)S(1)}, f32[24,40,128]{2,1,0:T(8,128)}, u32[]{:S(2)}) copy-start(f32[24,40,128]{2,1,0:T(8,128)} %get-tuple-element.102.r_11_) | copy-start | bytes 1474564
  47.5 16.2 %copy-start.5 = (f32[24,40,128]{2,1,0:T(8,128)S(1)}, f32[24,40,128]{2,1,0:T(8,128)}, u32[]{:S(2)}) copy-start(f32[24,40,128]{2,1,0:T(8,128)} %get-tuple-element.103.r_12_) | copy-start | bytes 1474564
  47.5 16.2 %copy-start.6 = (f32[24,40,128]{2,1,0:T(8,128)S(1)}, f32[24,40,128]{2,1,0:T(8,128)}, u32[]{:S(2)}) copy-start(f32[24,40,128]{2,1,0:T(8,128)} %get-tuple-element.104.r_13_) | copy-start | bytes 1474564
  47.5 16.2 %copy-start.7 = (f32[24,40,128]{2,1,0:T(8,128)S(1)}, f32[24,40,128]{2,1,0:T(8,128)}, u32[]{:S(2)}) copy-start(f32[24,40,128]{2,1,0:T(8,128)} %get-tuple-element.105.r_14_) | copy-start | bytes 1474564
  47.5 16.2 %copy-start.8 = (f32[24,40,128]{2,1,0:T(8,128)S(1)}, f32[24,40,128]{2,1,0:T(8,128)}, u32[]{:S(2)}) copy-start(f32[24,40,128]{2,1,0:T(8,128)} %get-tuple-element.106.r_15_) | copy-start | bytes 1474564
  47.6 16.2 %copy-start.9 = (f32[24,40,128]{2,1,0:T(8,128)S(1)}, f32[24,40,128]{2,1,0:T(8,128)}, u32[]{:S(2)}) copy-start(f32[24,40,128]{2,1,0:T(8,128)} %get-tuple-element.107.r_16_) | copy-start | bytes 1474564
  47.6 9.1 %collective-permute-start.8 = (f32[4,2,16,128]{3,2,1,0:T(8,128)S(1)}, f32[4,2,16,128]{3,2,1,0:T(8,128)S(1)}, u32[]{:S(2)}, u32[]{:S(2)}) collective-permute-start(f32[4,2,16,128]{3,2,1,0:T(8,128)S(1)} %dynamic-slice_bitcast_fusion), channel_id=1, source_target_pairs={{0,8},{8,0},{4,12},{12,4},{1,9},{9,1},{5,13},{13,5},{2,10},{10,2},... | collective-permute-start | bytes 196616 | tf_op jit(solution)/shard_map/ppermute | solution.py:815
  56.7 7.0 %collective-permute-start.10 = (f32[7,40,128]{2,1,0:T(8,128)S(1)}, f32[7,40,128]{2,1,0:T(8,128)S(1)}, u32[]{:S(2)}, u32[]{:S(2)}) collective-permute-start(f32[7,40,128]{2,1,0:T(8,128)S(1)} %get-tuple-element.100), channel_id=1, source_target_pairs={{4,8},{8,4},{5,9},{9,5},{6,10},{10,6},{7,11},{11,7},{20,24},{24,20... | collective-permute-start | bytes 430088 | tf_op jit(solution)/shard_map/ppermute | solution.py:817
  57.4 6.3 %collective-permute-start.9 = (f32[7,40,128]{2,1,0:T(8,128)S(1)}, f32[7,40,128]{2,1,0:T(8,128)S(1)}, u32[]{:S(2)}, u32[]{:S(2)}) collective-permute-start(f32[7,40,128]{2,1,0:T(8,128)S(1)} %get-tuple-element.99), channel_id=1, source_target_pairs={{0,4},{4,0},{8,12},{12,8},{1,5},{5,1},{9,13},{13,9},{2,6},{6,2},{1... | collective-permute-start | bytes 430088 | tf_op jit(solution)/shard_map/ppermute | solution.py:817
